TPU v7x, 32 devices: a whole 2x2x4 slice. The times are simulated.
32 devices in a mesh: gx: 2 (over y), gy: 4 (over x, core), gz: 4 (over z).
Axes of the slice: x: 2, y: 2, z: 4, core: 2. Of those that a mesh axis runs over, the one named last changes fastest.
Arguments:
- magnetic: float32 [3, 32, 128, 512], P(None, 'gx', 'gy', 'gz'), may hold values from -11 to 11
Outputs:
- cleaned: float32 [3, 32, 128, 512], P(None, 'gx', 'gy', 'gz')
All inputs are finite; a program needn't handle non-finite values.
Results may differ from a plain program's by a relative error of at most 0.00018.
Values sent between devices are 32-bit elements; how exact they have to be, the bound alone decides.
No kernel may reach another device: no remote copies, remote signals or barrier semaphores. Data moves between devices by JAX's collectives and lax.ppermute only.
A program may use at most 128 MiB of HBM per device.

v0:
```python
import jax
import jax.numpy as jnp
from jax import lax
from jax.sharding import PartitionSpec as P

LEVELS = 5
SWEEPS = 3
COARSE_ITERS = 24


relax_weight = 6.0 / 7.0


def extended(block, sides, width):
    for axis, dim in sides:
        count = lax.axis_size(axis)
        forward = [(i, i + 1) for i in range(count - 1)]
        forward.append((count - 1, 0))
        backward = [(target, source) for source, target in forward]
        low = lax.ppermute(
            lax.slice_in_dim(block, block.shape[dim] - width, None, axis=dim), axis, forward
        )
        high = lax.ppermute(lax.slice_in_dim(block, 0, width, axis=dim), axis, backward)
        block = jnp.concatenate([low, block, high], axis=dim)
    return block


def passed_along(value, axis, steps):
    count = lax.axis_size(axis)
    pairs = [(source, (source + steps) % count) for source in range(count)]
    return lax.ppermute(value, axis, pairs)


def faces(values, layers):
    return extended(values, (("gx", 0), ("gy", 1), ("gz", 2)), layers)


def apply_padded(padded, stretch):
    center = padded[1:-1, 1:-1, 1:-1]
    beside = padded[2:, 1:-1, 1:-1] + padded[:-2, 1:-1, 1:-1]
    beside = beside + padded[1:-1, 2:, 1:-1] + padded[1:-1, :-2, 1:-1]
    beside = beside + padded[1:-1, 1:-1, 2:] + padded[1:-1, 1:-1, :-2]
    return (6.0 * center - beside) * stretch


def apply_local(values, stretch):
    beside = jnp.roll(values, -1, 0) + jnp.roll(values, 1, 0)
    beside = beside + jnp.roll(values, -1, 1) + jnp.roll(values, 1, 1)
    beside = beside + jnp.roll(values, -1, 2) + jnp.roll(values, 1, 2)
    return (6.0 * values - beside) * stretch


def restrict(values):
    extent = values.shape
    blocks = values.reshape(extent[0] // 2, 2, extent[1] // 2, 2, extent[2] // 2, 2)
    return jnp.sum(blocks, axis=(1, 3, 5)) * 0.125


def prolong(values):
    extent = values.shape
    spread = jnp.broadcast_to(
        values[:, None, :, None, :, None], (extent[0], 2, extent[1], 2, extent[2], 2)
    )
    return spread.reshape(extent[0] * 2, extent[1] * 2, extent[2] * 2)


def cycle_whole(source, level_index):
    stretch = 0.25**level_index
    factor = relax_weight * 4.0**level_index / 6.0
    solution = factor * source

    def coarse_sweep(iteration, current):
        return current + factor * (source - apply_local(current, stretch))

    return lax.fori_loop(0, COARSE_ITERS - 1, coarse_sweep, solution)


def collect(source):
    extent = source.shape
    stacked = lax.all_gather(source[None], ("gx", "gy", "gz"), axis=0, tiled=True)
    count_x, count_y, count_z = (lax.axis_size("gx"), lax.axis_size("gy"), lax.axis_size("gz"))
    gathered_grid = stacked.reshape(count_x, count_y, count_z, extent[0], extent[1], extent[2])
    gathered_grid = gathered_grid.transpose(0, 3, 1, 4, 2, 5)
    return gathered_grid.reshape(count_x * extent[0], count_y * extent[1], count_z * extent[2])


def own_block(solution, extent):
    starts = (
        lax.axis_index("gx") * extent[0],
        lax.axis_index("gy") * extent[1],
        lax.axis_index("gz") * extent[2],
    )
    return lax.dynamic_slice(solution, starts, extent)


def cycle_shard(source, level_index, gather_level, deep_faces):
    extent = source.shape
    if level_index == gather_level:
        whole_grid = collect(source)
        return own_block(cycle_whole(whole_grid, level_index), extent)
    stretch = 0.25**level_index
    factor = relax_weight * 4.0**level_index / 6.0
    layers = SWEEPS
    solution = factor * source
    for repeat in range(layers - 1):
        padded = faces(solution, 1)
        solution = solution + factor * (source - apply_padded(padded, stretch))
    residual_field = source - apply_padded(faces(solution, 1), stretch)
    correction = cycle_shard(restrict(residual_field), level_index + 1, gather_level, deep_faces)
    solution = solution + prolong(correction)
    for repeat in range(layers):
        padded = faces(solution, 1)
        solution = solution + factor * (source - apply_padded(padded, stretch))
    return solution


def body(magnetic):
    along_x, along_y, along_z = (magnetic[0], magnetic[1], magnetic[2])
    below_x = passed_along(along_x[-1:], "gx", 1)
    below_y = passed_along(along_y[:, -1:], "gy", 1)
    below_z = passed_along(along_z[:, :, -1:], "gz", 1)
    lower_x = jnp.concatenate([below_x, along_x[:-1]], axis=0)
    lower_y = jnp.concatenate([below_y, along_y[:, :-1]], axis=1)
    lower_z = jnp.concatenate([below_z, along_z[:, :, :-1]], axis=2)
    divergence = along_x - lower_x + (along_y - lower_y) + (along_z - lower_z)
    gather_level = LEVELS - 1
    potential = cycle_shard(-divergence, 0, gather_level, False)
    padded = faces(potential, 1)
    center = padded[1:-1, 1:-1, 1:-1]
    cleaned_x = along_x - (padded[2:, 1:-1, 1:-1] - center)
    cleaned_y = along_y - (padded[1:-1, 2:, 1:-1] - center)
    cleaned_z = along_z - (padded[1:-1, 1:-1, 2:] - center)
    return jnp.stack([cleaned_x, cleaned_y, cleaned_z])


def solution(mesh):
    in_specs = (P(None, "gx", "gy", "gz"),)
    out_specs = P(None, "gx", "gy", "gz")
    return jax.shard_map(body, mesh=mesh, in_specs=in_specs, out_specs=out_specs, check_vma=False)
```

profile of v0, /device:TPU:0, one launch (start us, length us, event | category | flops | bytes accessed | tf_op | source)
XLA Modules:
  0.0 581.5 jit_solution(8493738391552205307)
XLA Ops:
  7.6 5.0 collective-permute-done.2
  24.9 9.2 %collective-permute-done.7 = f32[18,34,1]{2,1,0:T(8,128)S(1)} collective-permute-done((f32[18,34,1]{2,1,0:T(8,128)S(1)}, f32[18,34,1]{2,1,0:T(8,128)S(1)}, u32[]{:S(2)}, u32[]{:S(2)}) %collective-permute-start.7) | collective-permute-done | bytes 2480 | tf_op jit(solution)/shard_map/ppermute | solution.py:23
  34.1 7.4 %collective-permute-done.8 = f32[18,34,1]{2,1,0:T(8,128)S(1)} collective-permute-done((f32[18,34,1]{2,1,0:T(8,128)S(1)}, f32[18,34,1]{2,1,0:T(8,128)S(1)}, u32[]{:S(2)}, u32[]{:S(2)}) %collective-permute-start.8) | collective-permute-done | bytes 2480 | tf_op jit(solution)/shard_map/ppermute | solution.py:20
  51.7 8.8 %collective-permute-done.13 = f32[18,34,1]{2,1,0:T(8,128)S(1)} collective-permute-done((f32[18,34,1]{2,1,0:T(8,128)S(1)}, f32[18,34,1]{2,1,0:T(8,128)S(1)}, u32[]{:S(2)}, u32[]{:S(2)}) %collective-permute-start.13) | collective-permute-done | bytes 2480 | tf_op jit(solution)/shard_map/ppermute | solution.py:23
  60.5 7.0 %collective-permute-done.14 = f32[18,34,1]{2,1,0:T(8,128)S(1)} collective-permute-done((f32[18,34,1]{2,1,0:T(8,128)S(1)}, f32[18,34,1]{2,1,0:T(8,128)S(1)}, u32[]{:S(2)}, u32[]{:S(2)}) %collective-permute-start.14) | collective-permute-done | bytes 2480 | tf_op jit(solution)/shard_map/ppermute | solution.py:20
  78.9 8.7 %collective-permute-done.19 = f32[18,34,1]{2,1,0:T(8,128)S(1)} collective-permute-done((f32[18,34,1]{2,1,0:T(8,128)S(1)}, f32[18,34,1]{2,1,0:T(8,128)S(1)}, u32[]{:S(2)}, u32[]{:S(2)}) %collective-permute-start.19) | collective-permute-done | bytes 2480 | tf_op jit(solution)/shard_map/ppermute | solution.py:23
  87.6 9.1 %collective-permute-done.20 = f32[18,34,1]{2,1,0:T(8,128)S(1)} collective-permute-done((f32[18,34,1]{2,1,0:T(8,128)S(1)}, f32[18,34,1]{2,1,0:T(8,128)S(1)}, u32[]{:S(2)}, u32[]{:S(2)}) %collective-permute-start.20) | collective-permute-done | bytes 2480 | tf_op jit(solution)/shard_map/ppermute | solution.py:20
  97.0 18.1 %reshape.49 = f32[8,2,16,2,64,2]{5,4,3,2,1,0:T(8,128)} reshape(f32[16,32,128]{2,1,0:T(8,128)S(1)} %fusion.47) | data formatting | bytes 524288 | tf_op jit(solution)/shard_map/reshape | solution.py:55
  115.1 7.0 %reduce_sum.43 = f32[8,16,64]{2,1,0:T(8,128)S(1)} reduce(f32[8,2,16,2,64,2]{5,4,3,2,1,0:T(8,128)} %reshape.49, f32[]{:T(128)} %constant.15.clone.1), dimensions={1,3,5}, to_apply=%region_0.0 | reduce | flops 57344 | bytes 294916 | tf_op jit(solution)/shard_map/reduce_sum | solution.py:56
  148.9 5.5 collective-permute-done.31
  164.2 3.5 collective-permute-done.37
  257.6 63.6 %all-gather.1 = f32[32,2,8]{2,1,0:T(2,128)S(1)} all-gather(f32[1,2,8]{2,1,0:T(2,128)S(1)} %multiply_bitcast_fusion), channel_id=2, replica_groups=mesh['gx'=2,'gy'=4,'gz'=4] {'gx','gy','gz'}, dimensions={0}, use_global_device_ids=true | all-gather | bytes 2112 | tf_op jit(solution)/shard_map/all_gather | solution.py:80
  321.3 5.7 while.10
  424.2 5.5 collective-permute-done.115
  458.7 3.5 collective-permute-done.128
  462.3 6.4 %broadcast_in_dim.37 = f32[8,2,16,2,64,2]{5,4,3,2,1,0:T(8,128)} broadcast(f32[8,16,64]{2,1,0:T(8,128)S(1)} %fusion.78), dimensions={0,2,4} | broadcast | bytes 294912 | tf_op jit(solution)/shard_map/broadcast_in_dim | solution.py:61
  468.7 12.7 %reshape.56 = f32[16,32,128]{2,1,0:T(8,128)S(1)} reshape(f32[8,2,16,2,64,2]{5,4,3,2,1,0:T(8,128)} %broadcast_in_dim.37) | data formatting | bytes 524288 | tf_op jit(solution)/shard_map/reshape | solution.py:64
  491.3 7.9 %collective-permute-done.133 = f32[18,34,1]{2,1,0:T(8,128)S(1)} collective-permute-done((f32[18,34,1]{2,1,0:T(8,128)S(1)}, f32[18,34,1]{2,1,0:T(8,128)S(1)}, u32[]{:S(2)}, u32[]{:S(2)}) %collective-permute-start.133) | collective-permute-done | bytes 2480 | tf_op jit(solution)/shard_map/ppermute | solution.py:23
  499.2 8.5 %collective-permute-done.134 = f32[18,34,1]{2,1,0:T(8,128)S(1)} collective-permute-done((f32[18,34,1]{2,1,0:T(8,128)S(1)}, f32[18,34,1]{2,1,0:T(8,128)S(1)}, u32[]{:S(2)}, u32[]{:S(2)}) %collective-permute-start.134) | collective-permute-done | bytes 2480 | tf_op jit(solution)/shard_map/ppermute | solution.py:20
  519.0 8.8 %collective-permute-done.139 = f32[18,34,1]{2,1,0:T(8,128)S(1)} collective-permute-done((f32[18,34,1]{2,1,0:T(8,128)S(1)}, f32[18,34,1]{2,1,0:T(8,128)S(1)}, u32[]{:S(2)}, u32[]{:S(2)}) %collective-permute-start.139) | collective-permute-done | bytes 2480 | tf_op jit(solution)/shard_map/ppermute | solution.py:23
  527.8 7.1 %collective-permute-done.140 = f32[18,34,1]{2,1,0:T(8,128)S(1)} collective-permute-done((f32[18,34,1]{2,1,0:T(8,128)S(1)}, f32[18,34,1]{2,1,0:T(8,128)S(1)}, u32[]{:S(2)}, u32[]{:S(2)}) %collective-permute-start.140) | collective-permute-done | bytes 2480 | tf_op jit(solution)/shard_map/ppermute | solution.py:20
  545.1 8.9 %collective-permute-done.145 = f32[18,34,1]{2,1,0:T(8,128)S(1)} collective-permute-done((f32[18,34,1]{2,1,0:T(8,128)S(1)}, f32[18,34,1]{2,1,0:T(8,128)S(1)}, u32[]{:S(2)}, u32[]{:S(2)}) %collective-permute-start.145) | collective-permute-done | bytes 2480 | tf_op jit(solution)/shard_map/ppermute | solution.py:23
  554.0 7.7 %collective-permute-done.146 = f32[18,34,1]{2,1,0:T(8,128)S(1)} collective-permute-done((f32[18,34,1]{2,1,0:T(8,128)S(1)}, f32[18,34,1]{2,1,0:T(8,128)S(1)}, u32[]{:S(2)}, u32[]{:S(2)}) %collective-permute-start.146) | collective-permute-done | bytes 2480 | tf_op jit(solution)/shard_map/ppermute | solution.py:20
  572.6 7.7 %collective-permute-done.151 = f32[18,34,1]{2,1,0:T(8,128)S(1)} collective-permute-done((f32[18,34,1]{2,1,0:T(8,128)S(1)}, f32[18,34,1]{2,1,0:T(8,128)S(1)}, u32[]{:S(2)}, u32[]{:S(2)}) %collective-permute-start.151) | collective-permute-done | bytes 2480 | tf_op jit(solution)/shard_map/ppermute | solution.py:23
  (582 shorter events, 342.8 us)
Async XLA Ops:
  1.2 11.4 %collective-permute-start.2 = (f32[16,32,1]{2,1,0:T(8,128)S(1)}, f32[16,32,1]{2,1,0:T(8,128)S(1)}, u32[]{:S(2)}, u32[]{:S(2)}) collective-permute-start(f32[16,32,1]{2,1,0:T(8,128)S(1)} %slice.1423), channel_id=1, source_target_pairs={{0,1},{1,2},{2,3},{3,0},{4,5},{5,6},{6,7},{7,4},{8,9},{9,10},{10,1... | collective-permute-start | bytes 6152 | tf_op jit(solution)/shard_map/ppermute | solution.py:31
  4.3 8.3 %collective-permute-start.1 = (f32[16,1,128]{2,1,0:T(1,128)S(1)}, f32[16,1,128]{2,1,0:T(1,128)S(1)}, u32[]{:S(2)}, u32[]{:S(2)}) collective-permute-start(f32[16,1,128]{2,1,0:T(1,128)S(1)} %slice.1421), channel_id=1, source_target_pairs={{0,4},{4,8},{8,12},{12,0},{1,5},{5,9},{9,13},{13,1},{2,6},{6,10},{... | collective-permute-start | bytes 24584 | tf_op jit(solution)/shard_map/ppermute | solution.py:31
  5.1 7.5 %collective-permute-start = (f32[1,32,128]{2,1,0:T(8,128)S(1)}, f32[1,32,128]{2,1,0:T(8,128)S(1)}, u32[]{:S(2)}, u32[]{:S(2)}) collective-permute-start(f32[1,32,128]{2,1,0:T(8,128)S(1)} %slice_bitcast_fusion.3), channel_id=1, source_target_pairs={{0,16},{16,0},{1,17},{17,1},{2,18},{18,2},{3,19},{19,3},{4,20},{20... | collective-permute-start | bytes 49160 | tf_op jit(solution)/shard_map/ppermute | solution.py:31
  22.8 11.3 %collective-permute-start.7 = (f32[18,34,1]{2,1,0:T(8,128)S(1)}, f32[18,34,1]{2,1,0:T(8,128)S(1)}, u32[]{:S(2)}, u32[]{:S(2)}) collective-permute-start(f32[18,34,1]{2,1,0:T(8,128)S(1)} %get-tuple-element.56), channel_id=1, source_target_pairs={{1,0},{2,1},{3,2},{0,3},{5,4},{6,5},{7,6},{4,7},{9,8},{10,9},{11,1... | collective-permute-start | bytes 7352 | tf_op jit(solution)/shard_map/ppermute | solution.py:23
  24.6 16.9 %collective-permute-start.8 = (f32[18,34,1]{2,1,0:T(8,128)S(1)}, f32[18,34,1]{2,1,0:T(8,128)S(1)}, u32[]{:S(2)}, u32[]{:S(2)}) collective-permute-start(f32[18,34,1]{2,1,0:T(8,128)S(1)} %get-tuple-element.57), channel_id=1, source_target_pairs={{0,1},{1,2},{2,3},{3,0},{4,5},{5,6},{6,7},{7,4},{8,9},{9,10},{10,1... | collective-permute-start | bytes 7352 | tf_op jit(solution)/shard_map/ppermute | solution.py:20
  49.7 10.8 %collective-permute-start.13 = (f32[18,34,1]{2,1,0:T(8,128)S(1)}, f32[18,34,1]{2,1,0:T(8,128)S(1)}, u32[]{:S(2)}, u32[]{:S(2)}) collective-permute-start(f32[18,34,1]{2,1,0:T(8,128)S(1)} %get-tuple-element.54), channel_id=1, source_target_pairs={{1,0},{2,1},{3,2},{0,3},{5,4},{6,5},{7,6},{4,7},{9,8},{10,9},{11,1... | collective-permute-start | bytes 7352 | tf_op jit(solution)/shard_map/ppermute | solution.py:23
  51.5 16.0 %collective-permute-start.14 = (f32[18,34,1]{2,1,0:T(8,128)S(1)}, f32[18,34,1]{2,1,0:T(8,128)S(1)}, u32[]{:S(2)}, u32[]{:S(2)}) collective-permute-start(f32[18,34,1]{2,1,0:T(8,128)S(1)} %get-tuple-element.55), channel_id=1, source_target_pairs={{0,1},{1,2},{2,3},{3,0},{4,5},{5,6},{6,7},{7,4},{8,9},{9,10},{10,1... | collective-permute-start | bytes 7352 | tf_op jit(solution)/shard_map/ppermute | solution.py:20
  76.9 10.7 %collective-permute-start.19 = (f32[18,34,1]{2,1,0:T(8,128)S(1)}, f32[18,34,1]{2,1,0:T(8,128)S(1)}, u32[]{:S(2)}, u32[]{:S(2)}) collective-permute-start(f32[18,34,1]{2,1,0:T(8,128)S(1)} %get-tuple-element.52), channel_id=1, source_target_pairs={{1,0},{2,1},{3,2},{0,3},{5,4},{6,5},{7,6},{4,7},{9,8},{10,9},{11,1... | collective-permute-start | bytes 7352 | tf_op jit(solution)/shard_map/ppermute | solution.py:23
  78.6 18.1 %collective-permute-start.20 = (f32[18,34,1]{2,1,0:T(8,128)S(1)}, f32[18,34,1]{2,1,0:T(8,128)S(1)}, u32[]{:S(2)}, u32[]{:S(2)}) collective-permute-start(f32[18,34,1]{2,1,0:T(8,128)S(1)} %get-tuple-element.53), channel_id=1, source_target_pairs={{0,1},{1,2},{2,3},{3,0},{4,5},{5,6},{6,7},{7,4},{8,9},{9,10},{10,1... | collective-permute-start | bytes 7352 | tf_op jit(solution)/shard_map/ppermute | solution.py:20
  131.4 6.7 %collective-permute-start.26 = (f32[10,18,1]{2,1,0:T(8,128)S(1)}, f32[10,18,1]{2,1,0:T(8,128)S(1)}, u32[]{:S(2)}, u32[]{:S(2)}) collective-permute-start(f32[10,18,1]{2,1,0:T(8,128)S(1)} %get-tuple-element.97), channel_id=1, source_target_pairs={{0,1},{1,2},{2,3},{3,0},{4,5},{5,6},{6,7},{7,4},{8,9},{9,10},{10,1... | collective-permute-start | bytes 2168 | tf_op jit(solution)/shard_map/ppermute | solution.py:20
  146.8 7.6 %collective-permute-start.31 = (f32[10,18,1]{2,1,0:T(8,128)S(1)}, f32[10,18,1]{2,1,0:T(8,128)S(1)}, u32[]{:S(2)}, u32[]{:S(2)}) collective-permute-start(f32[10,18,1]{2,1,0:T(8,128)S(1)} %get-tuple-element.94), channel_id=1, source_target_pairs={{1,0},{2,1},{3,2},{0,3},{5,4},{6,5},{7,6},{4,7},{9,8},{10,9},{11,1... | collective-permute-start | bytes 2168 | tf_op jit(solution)/shard_map/ppermute | solution.py:23
  147.3 7.1 %collective-permute-start.32 = (f32[10,18,1]{2,1,0:T(8,128)S(1)}, f32[10,18,1]{2,1,0:T(8,128)S(1)}, u32[]{:S(2)}, u32[]{:S(2)}) collective-permute-start(f32[10,18,1]{2,1,0:T(8,128)S(1)} %get-tuple-element.95), channel_id=1, source_target_pairs={{0,1},{1,2},{2,3},{3,0},{4,5},{5,6},{6,7},{7,4},{8,9},{9,10},{10,1... | collective-permute-start | bytes 2168 | tf_op jit(solution)/shard_map/ppermute | solution.py:20
  163.6 6.9 %collective-permute-start.38 = (f32[10,18,1]{2,1,0:T(8,128)S(1)}, f32[10,18,1]{2,1,0:T(8,128)S(1)}, u32[]{:S(2)}, u32[]{:S(2)}) collective-permute-start(f32[10,18,1]{2,1,0:T(8,128)S(1)} %get-tuple-element.93), channel_id=1, source_target_pairs={{0,1},{1,2},{2,3},{3,0},{4,5},{5,6},{6,7},{7,4},{8,9},{9,10},{10,1... | collective-permute-start | bytes 2168 | tf_op jit(solution)/shard_map/ppermute | solution.py:20
  422.1 7.6 %collective-permute-start.115 = (f32[10,18,1]{2,1,0:T(8,128)S(1)}, f32[10,18,1]{2,1,0:T(8,128)S(1)}, u32[]{:S(2)}, u32[]{:S(2)}) collective-permute-start(f32[10,18,1]{2,1,0:T(8,128)S(1)} %get-tuple-element.90), channel_id=1, source_target_pairs={{1,0},{2,1},{3,2},{0,3},{5,4},{6,5},{7,6},{4,7},{9,8},{10,9},{11,1... | collective-permute-start | bytes 2168 | tf_op jit(solution)/shard_map/ppermute | solution.py:23
  422.2 7.5 %collective-permute-start.116 = (f32[10,18,1]{2,1,0:T(8,128)S(1)}, f32[10,18,1]{2,1,0:T(8,128)S(1)}, u32[]{:S(2)}, u32[]{:S(2)}) collective-permute-start(f32[10,18,1]{2,1,0:T(8,128)S(1)} %get-tuple-element.91), channel_id=1, source_target_pairs={{0,1},{1,2},{2,3},{3,0},{4,5},{5,6},{6,7},{7,4},{8,9},{9,10},{10,1... | collective-permute-start | bytes 2168 | tf_op jit(solution)/shard_map/ppermute | solution.py:20
  437.8 7.2 %collective-permute-start.122 = (f32[10,18,1]{2,1,0:T(8,128)S(1)}, f32[10,18,1]{2,1,0:T(8,128)S(1)}, u32[]{:S(2)}, u32[]{:S(2)}) collective-permute-start(f32[10,18,1]{2,1,0:T(8,128)S(1)} %get-tuple-element.89), channel_id=1, source_target_pairs={{0,1},{1,2},{2,3},{3,0},{4,5},{5,6},{6,7},{7,4},{8,9},{9,10},{10,1... | collective-permute-start | bytes 2168 | tf_op jit(solution)/shard_map/ppermute | solution.py:20
  455.4 6.7 %collective-permute-start.128 = (f32[10,18,1]{2,1,0:T(8,128)S(1)}, f32[10,18,1]{2,1,0:T(8,128)S(1)}, u32[]{:S(2)}, u32[]{:S(2)}) collective-permute-start(f32[10,18,1]{2,1,0:T(8,128)S(1)} %get-tuple-element.87), channel_id=1, source_target_pairs={{0,1},{1,2},{2,3},{3,0},{4,5},{5,6},{6,7},{7,4},{8,9},{9,10},{10,1... | collective-permute-start | bytes 2168 | tf_op jit(solution)/shard_map/ppermute | solution.py:20
  489.2 10.0 %collective-permute-start.133 = (f32[18,34,1]{2,1,0:T(8,128)S(1)}, f32[18,34,1]{2,1,0:T(8,128)S(1)}, u32[]{:S(2)}, u32[]{:S(2)}) collective-permute-start(f32[18,34,1]{2,1,0:T(8,128)S(1)} %get-tuple-element.50), channel_id=1, source_target_pairs={{1,0},{2,1},{3,2},{0,3},{5,4},{6,5},{7,6},{4,7},{9,8},{10,9},{11,1... | collective-permute-start | bytes 7352 | tf_op jit(solution)/shard_map/ppermute | solution.py:23
  490.2 17.6 %collective-permute-start.134 = (f32[18,34,1]{2,1,0:T(8,128)S(1)}, f32[18,34,1]{2,1,0:T(8,128)S(1)}, u32[]{:S(2)}, u32[]{:S(2)}) collective-permute-start(f32[18,34,1]{2,1,0:T(8,128)S(1)} %get-tuple-element.51), channel_id=1, source_target_pairs={{0,1},{1,2},{2,3},{3,0},{4,5},{5,6},{6,7},{7,4},{8,9},{9,10},{10,1... | collective-permute-start | bytes 7352 | tf_op jit(solution)/shard_map/ppermute | solution.py:20
  516.9 10.8 %collective-permute-start.139 = (f32[18,34,1]{2,1,0:T(8,128)S(1)}, f32[18,34,1]{2,1,0:T(8,128)S(1)}, u32[]{:S(2)}, u32[]{:S(2)}) collective-permute-start(f32[18,34,1]{2,1,0:T(8,128)S(1)} %get-tuple-element.48), channel_id=1, source_target_pairs={{1,0},{2,1},{3,2},{0,3},{5,4},{6,5},{7,6},{4,7},{9,8},{10,9},{11,1... | collective-permute-start | bytes 7352 | tf_op jit(solution)/shard_map/ppermute | solution.py:23
  518.7 16.1 %collective-permute-start.140 = (f32[18,34,1]{2,1,0:T(8,128)S(1)}, f32[18,34,1]{2,1,0:T(8,128)S(1)}, u32[]{:S(2)}, u32[]{:S(2)}) collective-permute-start(f32[18,34,1]{2,1,0:T(8,128)S(1)} %get-tuple-element.49), channel_id=1, source_target_pairs={{0,1},{1,2},{2,3},{3,0},{4,5},{5,6},{6,7},{7,4},{8,9},{9,10},{10,1... | collective-permute-start | bytes 7352 | tf_op jit(solution)/shard_map/ppermute | solution.py:20
  543.0 11.0 %collective-permute-start.145 = (f32[18,34,1]{2,1,0:T(8,128)S(1)}, f32[18,34,1]{2,1,0:T(8,128)S(1)}, u32[]{:S(2)}, u32[]{:S(2)}) collective-permute-start(f32[18,34,1]{2,1,0:T(8,128)S(1)} %get-tuple-element.46), channel_id=1, source_target_pairs={{1,0},{2,1},{3,2},{0,3},{5,4},{6,5},{7,6},{4,7},{9,8},{10,9},{11,1... | collective-permute-start | bytes 7352 | tf_op jit(solution)/shard_map/ppermute | solution.py:23
  544.8 16.9 %collective-permute-start.146 = (f32[18,34,1]{2,1,0:T(8,128)S(1)}, f32[18,34,1]{2,1,0:T(8,128)S(1)}, u32[]{:S(2)}, u32[]{:S(2)}) collective-permute-start(f32[18,34,1]{2,1,0:T(8,128)S(1)} %get-tuple-element.47), channel_id=1, source_target_pairs={{0,1},{1,2},{2,3},{3,0},{4,5},{5,6},{6,7},{7,4},{8,9},{9,10},{10,1... | collective-permute-start | bytes 7352 | tf_op jit(solution)/shard_map/ppermute | solution.py:20
  570.7 9.6 %collective-permute-start.151 = (f32[18,34,1]{2,1,0:T(8,128)S(1)}, f32[18,34,1]{2,1,0:T(8,128)S(1)}, u32[]{:S(2)}, u32[]{:S(2)}) collective-permute-start(f32[18,34,1]{2,1,0:T(8,128)S(1)} %pad_maximum_fusion.1), channel_id=1, source_target_pairs={{1,0},{2,1},{3,2},{0,3},{5,4},{6,5},{7,6},{4,7},{9,8},{10,9},{11,1... | collective-permute-start | bytes 7352 | tf_op jit(solution)/shard_map/ppermute | solution.py:23
  (129 other events, 546.3 us)
where the time goes:
time: 582 us; the launch traced here: 581 us
  waiting for transfers between devices  326 us (56%)
  starting transfers between devices  122 us (21%)
  blocking collectives  63.6 us (11%)
  local copies, waits for them, and re-layouts  51.2 us (9%)
  other arithmetic  17.1 us (3%)
    ppermute x75, waiting for transfers between devices, extended(): lax.ppermute(lax.slice_in_dim(block, 0, width, axis=dim), axis, backward)  167 us
    ppermute x74, waiting for transfers between devices, extended(): lax.ppermute(lax.slice_in_dim(block, block.shape[dim] - width, None, axis...  154 us
    ppermute x74, starting transfers between devices, extended(): lax.ppermute(lax.slice_in_dim(block, block.shape[dim] - width, None, axis...  68.1 us
    all_gather x1, blocking collectives, collect(): lax.all_gather(source[None], ('gx', 'gy', 'gz'), axis=0, tiled=True)  63.6 us
    ppermute x75, starting transfers between devices, extended(): lax.ppermute(lax.slice_in_dim(block, 0, width, axis=dim), axis, backward)  49.3 us
    reshape x3, local copies, waits for them, and re-layouts, restrict(): values.reshape(extent[0] // 2, 2, extent[1] // 2, 2, extent[2] // 2, 2)  20.4 us
    reshape x3, local copies, waits for them, and re-layouts, prolong(): return spread.reshape(extent[0] * 2, extent[1] * 2, extent[2] * 2)  14.5 us
  transfers between devices with their start and end apart: 152, of which 148 were waited for; matrix products, arithmetic and copies ran while one was open for 0% of the time, Pallas kernels for 0%

commit v1 on v0

v1 whole, which is shorter than its diff:
```python
import functools

import jax
import jax.numpy as jnp
from jax import lax
from jax.experimental import pallas as pl
from jax.experimental.pallas import tpu as pltpu
from jax.sharding import PartitionSpec as P

LEVELS = 5
SWEEPS = 3
COARSE_ITERS = 24


F32 = jnp.float32
LANES = 128
VMEM_LIMIT = 16 * 1024 * 1024


def weight(level):
    return 4.0**level / 7.0


def shape(*extent):
    return jax.ShapeDtypeStruct(extent, F32)


def call(kernel, outs, scratch, flops, *args):
    bytes_accessed = 4 * sum(a.size for a in args)
    return pl.pallas_call(
        kernel,
        out_shape=outs,
        scratch_shapes=[pltpu.VMEM(s, F32) for s in scratch],
        compiler_params=pltpu.CompilerParams(vmem_limit_bytes=VMEM_LIMIT),
        cost_estimate=pl.CostEstimate(flops=flops, bytes_accessed=bytes_accessed, transcendentals=0),
    )(*args)


def iota(extent, dim):
    return lax.broadcasted_iota(jnp.int32, extent, dim)


def one_hot(condition):
    rows = iota((LANES, LANES), 0)
    columns = iota((LANES, LANES), 1)
    return jnp.where(condition(rows, columns), 1.0, 0.0).astype(F32)


def dot(left, right):
    return lax.dot_general(
        left,
        right,
        (((1,), (0,)), ((), ())),
        precision=lax.Precision.HIGHEST,
        preferred_element_type=F32,
    )


def seven_sum(source, plane, below, above):
    tiles = source.shape[0]
    rows = source.shape[2]
    center = [source[t, plane] for t in range(tiles)]
    left = [pltpu.roll(v, 1, 1) for v in center]
    right = [pltpu.roll(v, LANES - 1, 1) for v in center]
    if tiles > 1:
        lane = iota((rows, LANES), 1)
        left = [jnp.where(lane == 0, left[t - 1], left[t]) for t in range(tiles)]
        right = [
            jnp.where(lane == LANES - 1, right[(t + 1) % tiles], right[t]) for t in range(tiles)
        ]
    out = []
    for t in range(tiles):
        v = center[t]
        total = v + (source[t, below] + source[t, above])
        total = total + (pltpu.roll(v, 1, 0) + pltpu.roll(v, rows - 1, 0))
        out.append(total + (left[t] + right[t]))
    return out


def sweep(target, source, low, high, base=None, scale=None, period=None, base_shift=0):
    def step(plane, carry):
        if period is None:
            below, above = plane - 1, plane + 1
        else:
            below = lax.rem(plane + period - 1, period)
            above = lax.rem(plane + 1, period)
        for t, value in enumerate(seven_sum(source, plane, below, above)):
            if scale is not None:
                value = value * scale
            if base is not None:
                value = value + base[t, plane + base_shift]
            target[t, plane] = value
        return carry

    lax.fori_loop(low, high, step, 0, unroll=False)


PLANE0 = 6
ROW0 = 8
SPILL = 5


def fill_source(field, target):
    planes, rows = field.shape[1], field.shape[2]
    lane = iota((rows, LANES), 1)
    row = iota((rows, LANES), 0)
    row8 = iota((8, LANES), 0)
    zero8 = jnp.zeros((8, LANES), F32)
    zeros = jnp.zeros((rows, LANES), F32)

    def one_plane(i, before):
        along_x, along_y, along_z = field[0, i], field[1, i], field[2, i]
        value = before - along_x - along_y - along_z
        value = value + jnp.where(row == 0, 0.0, pltpu.roll(along_y, 1, 0))
        turned = pltpu.roll(along_z, 1, 1)
        value = value + jnp.where(lane == 0, 0.0, turned)
        p = PLANE0 + i
        target[0, p, 0:ROW0] = zero8
        target[0, p, ROW0 : ROW0 + rows] = value
        last = pltpu.roll(along_y[rows - 8 : rows], 1, 0)
        target[0, p, ROW0 + rows : ROW0 + rows + 8] = jnp.where(row8 == 0, last, 0.0)
        target[1, p, 0:ROW0] = zero8
        target[1, p, ROW0 : ROW0 + rows] = jnp.where(lane == 0, turned, 0.0)
        target[1, p, ROW0 + rows : ROW0 + rows + 8] = zero8

    one_plane(0, zeros)

    def step(i, carry):
        one_plane(i, field[0, i - 1])
        return carry

    lax.fori_loop(1, planes, step, 0)
    p = PLANE0 + planes
    target[0, p] = jnp.zeros(target.shape[2:], F32)
    target[1, p] = jnp.zeros(target.shape[2:], F32)
    target[0, p, ROW0 : ROW0 + rows] = field[0, planes - 1]


def clear_planes(target, planes):
    for t in range(target.shape[0]):
        for p in planes:
            target[t, p] = jnp.zeros(target.shape[2:], F32)


def pack_lanes(read, count, first, width, spacing, rows):
    lane = iota((rows, LANES), 1)
    per_tile = LANES // spacing
    tiles = []
    for start in range(0, count, per_tile):
        packed = jnp.zeros((rows, LANES), F32)
        for k in range(min(per_tile, count - start)):
            turned = pltpu.roll(read(start + k), (spacing * k - first) % LANES, 1)
            inside = (lane >= spacing * k) & (lane < spacing * k + width)
            packed = jnp.where(inside, turned, packed)
        tiles.append(packed)
    return tiles


def unpacked(packed, k, spacing, offset, width, first, rows):
    lane = iota((rows, LANES), 1)
    turned = pltpu.roll(packed, (first - spacing * k - offset) % LANES, 1)
    inside = (lane >= first) & (lane < first + width)
    return jnp.where(inside, turned, 0.0)


def spread_kernel(field, up, down, far, g1_out, first, second, g1_a, g1_b):
    planes = field.shape[1]
    count = first.shape[1]
    edge = [p for p in range(count) if p < PLANE0 or p > PLANE0 + planes]
    clear_planes(first, edge)
    clear_planes(second, edge)
    fill_source(field, first)
    low, high = PLANE0, PLANE0 + planes + 1
    sweep(second, first, low - 1, high + 1)
    sweep(first, second, low - 2, high + 2)
    sweep(second, first, low - 3, high + 3)

    n1 = planes // 2
    rows1 = first.shape[2] // 2
    pieces = []
    for t in range(2):
        parts = []
        for c in range(-2, n1 + 2):
            p = PLANE0 + 2 * c
            total = second[t, p, pl.ds(0, rows1, stride=2), :]
            total = total + second[t, p, pl.ds(1, rows1, stride=2), :]
            total = total + second[t, p + 1, pl.ds(0, rows1, stride=2), :]
            total = total + second[t, p + 1, pl.ds(1, rows1, stride=2), :]
            parts.append(total)
        pieces.append(jnp.concatenate(parts, axis=0))
    main = one_hot(lambda r, c: c == 32 + r // 2)
    side = one_hot(lambda r, c: c == jnp.where(r < 64, 96 + r // 2, r // 2 - 32))
    g1 = (dot(pieces[0], main) + dot(pieces[1], side)) * (0.125 / 343.0)
    share = n1 + 4
    g1 = g1.reshape(share, rows1, LANES)
    g1_out[...] = g1

    clear_planes(g1_a, range(g1_a.shape[1]))
    clear_planes(g1_b, range(g1_b.shape[1]))
    for c in range(share):
        g1_a[0, 4 + c, 4 : 4 + rows1] = g1[c]
    sweep(g1_b, g1_a, 3, 5 + share)
    sweep(g1_a, g1_b, 2, 6 + share)
    sweep(g1_b, g1_a, 1, 7 + share)
    rows2 = g1_a.shape[2] // 2
    parts = []
    for c in range(g1_a.shape[1] // 2):
        total = g1_b[0, 2 * c, pl.ds(0, rows2, stride=2), :]
        total = total + g1_b[0, 2 * c, pl.ds(1, rows2, stride=2), :]
        total = total + g1_b[0, 2 * c + 1, pl.ds(0, rows2, stride=2), :]
        total = total + g1_b[0, 2 * c + 1, pl.ds(1, rows2, stride=2), :]
        parts.append(total)
    even = jnp.concatenate(parts[0::2], axis=0)
    odd = jnp.concatenate(parts[1::2], axis=0)
    g2 = dot(even, one_hot(lambda r, c: c == r // 2))
    g2 = g2 + dot(odd, one_hot(lambda r, c: c == 64 + r // 2))
    g2 = g2 * (0.125 / 343.0)
    size = g2.shape[0]
    far[...] = g2
    up[0:size] = g2
    down[0:size] = g2
    up[size:] = pack_lanes(lambda c: g1[c], share, 89, 9, 10, rows1)[0]
    down[size:] = pack_lanes(lambda c: g1[c], share, 30, 9, 10, rows1)[0]


def gather_z_kernel(count, *refs):
    own, g1, received, (g2_out, g1_out) = refs[0], refs[1], refs[2 : 1 + count], refs[1 + count :]
    size = own.shape[0]
    period = 32 * count
    rows2 = 16
    tiles, planes = g2_out.shape[0], g2_out.shape[1]
    lane = iota((size, LANES), 1)
    for parity in range(2):
        totals = [jnp.zeros((size, LANES), F32) for _ in range(tiles)]
        for o in range(count):
            value = own[...] if o == 0 else received[o - 1][0:size]
            shift = (32 * o - 64 * parity) % LANES
            turned = pltpu.roll(value, shift, 1) if shift else value
            position = ((lane - shift) & (LANES - 1)) - 64 * parity
            inside = (position >= 0) & (position < 64)
            for t in range(tiles):
                lands = lax.rem(position + (32 * o + period), period) == lane + LANES * t
                totals[t] = totals[t] + jnp.where(inside & lands, turned, 0.0)
        for t in range(tiles):
            for k in range(planes // 2):
                g2_out[t, 2 * k + parity] = totals[t][rows2 * k : rows2 * (k + 1)]
    above = received[0][size:]
    below = received[count - 2][size:]
    rows1 = g1.shape[1]
    for c in range(g1.shape[0]):
        value = g1[c] + unpacked(below, c, 10, 0, 9, 25, rows1)
        g1_out[c] = value + unpacked(above, c, 10, 0, 9, 94, rows1)


def fold_x_kernel(count, *refs):
    shares, out = refs[:count], refs[count]
    tiles, period = out.shape[0], out.shape[1]
    for t in range(tiles):
        for x in range(period):
            total = None
            for o in range(count):
                for c in range(10):
                    if (c - 3 + 4 * o) % period == x:
                        value = shares[o][t, c]
                        total = value if total is None else total + value
            out[t, x] = total


def window_x_kernel(sources, *refs):
    inputs, (out, down, up) = refs[:-3], refs[-3:]
    planes = out.shape[0]
    for p in range(planes):
        total = None
        for index, offset, first, length in sources:
            k = p - 7 - 8 * offset + 2 - first
            inside = 0 <= p - 7 - 8 * offset + 2 < 12
            if inside and 0 <= k < length:
                value = inputs[index][k]
                total = value if total is None else total + value
        out[p] = total
        down[p] = total[2:10]
        up[p] = total[13:21]
        down[planes + p // 8, p % 8 : p % 8 + 1] = total[10:11]
        up[planes + p // 8, p % 8 : p % 8 + 1] = total[21:22]


def fine_tail_kernel(g1, above, below, out, base, first, second):
    planes, rows1 = g1.shape[0], g1.shape[1]

    def step(p, carry):
        base[0, p] = jnp.zeros(base.shape[2:], F32)
        base[0, p, 4 : 4 + rows1] = g1[p]
        base[0, p, 22:30] = base[0, p, 22:30] + above[p]
        base[0, p, 1:9] = base[0, p, 1:9] + below[p]
        return carry

    lax.fori_loop(0, planes, step, 0)
    for p in range(planes):
        ninth = p % 8
        base[0, p, 30:31] = base[0, p, 30:31] + above[planes + p // 8, ninth : ninth + 1]
        base[0, p, 9:10] = base[0, p, 9:10] + below[planes + p // 8, ninth : ninth + 1]
    seventh = 1.0 / 7.0
    sweep(first, base, 1, planes - 1, base, seventh)
    sweep(second, first, 2, planes - 2, base, seventh)
    sweep(first, second, 3, planes - 3, base, seventh)
    sweep(second, first, 4, planes - 4, base, seventh)
    sweep(first, second, 5, planes - 5, base, seventh)
    for c in range(out.shape[0]):
        out[c] = first[0, 5 + c] * weight(1)


def restrict_lanes(values, width, coarse_width, coarse_tiles):
    out = []
    for s in range(coarse_tiles):
        total = None
        for t, value in enumerate(values):
            matrix = one_hot(
                lambda r, c: ((LANES * t + r) // 2 == lax.rem(LANES * s + c, coarse_width))
                & (LANES * t + r < width)
            )
            term = dot(value, matrix)
            total = term if total is None else total + term
        out.append(total)
    return out


def prolong_lanes(values, width, fine_tiles):
    out = []
    for s in range(fine_tiles):
        total = None
        for t, value in enumerate(values):
            matrix = one_hot(lambda r, c: LANES * t + r == lax.rem(LANES * s + c, width) // 2)
            term = dot(value, matrix)
            total = term if total is None else total + term
        out.append(total)
    return out


def solve(level, width, buffers):
    g, a, b = buffers[level]
    tiles, planes, rows = g.shape[0], g.shape[1], g.shape[2]
    seventh = 1.0 / 7.0
    if level == LEVELS - 1:
        source = [[g[t, p] for t in range(tiles)] for p in range(planes)]

        def step(iteration, carry):
            out = []
            for p in range(planes):
                v = carry[p]
                total = v + carry[(p + 1) % planes] + carry[(p - 1) % planes]
                total = total + (pltpu.roll(v, 1, 0) + pltpu.roll(v, rows - 1, 0))
                total = total + (pltpu.roll(v, 1, 1) + pltpu.roll(v, LANES - 1, 1))
                out.append(source[p][0] + total * seventh)
            return tuple(out)

        start = tuple(source[p][0] for p in range(planes))
        final = lax.fori_loop(0, COARSE_ITERS - 1, step, start)
        for p in range(planes):
            g[0, p] = final[p] * weight(level)
        return
    w = weight(level)
    coarse = buffers[level + 1][0]
    sweep(a, g, 0, planes, None, seventh, planes)
    sweep(b, a, 0, planes, None, seventh, planes)
    for t in range(tiles):
        for p in range(planes):
            g[t, p] = (g[t, p] + a[t, p] + b[t, p]) * w
    sweep(a, b, 0, planes, None, seventh, planes)
    half = rows // 2
    values = []
    for t in range(tiles):
        parts = []
        for c in range(planes // 2):
            total = a[t, 2 * c, pl.ds(0, half, stride=2), :]
            total = total + a[t, 2 * c, pl.ds(1, half, stride=2), :]
            total = total + a[t, 2 * c + 1, pl.ds(0, half, stride=2), :]
            total = total + a[t, 2 * c + 1, pl.ds(1, half, stride=2), :]
            parts.append(total)
        values.append(jnp.concatenate(parts, axis=0))
    values = restrict_lanes(values, width, width // 2, coarse.shape[0])
    for t, value in enumerate(values):
        for c in range(planes // 2):
            coarse[t, c] = value[half * c : half * (c + 1)] * 0.125
    solve(level + 1, width // 2, buffers)
    values = [
        jnp.concatenate([coarse[t, c] for c in range(planes // 2)], axis=0)
        for t in range(coarse.shape[0])
    ]
    values = prolong_lanes(values, width, tiles)
    for t, value in enumerate(values):
        for c in range(planes // 2):
            part = value[half * c : half * (c + 1)]
            for p in (2 * c, 2 * c + 1):
                b[t, p, pl.ds(0, half, stride=2), :] = part
                b[t, p, pl.ds(1, half, stride=2), :] = part
        for p in range(planes):
            b[t, p] = b[t, p] + g[t, p]
    sweep(a, b, 0, planes, None, seventh, planes)
    sweep(b, a, 0, planes, None, seventh, planes)
    sweep(a, b, 0, planes, None, seventh, planes)
    for t in range(tiles):
        for p in range(planes):
            g[t, p] = g[t, p] + a[t, p]


def coarse_kernel(count, *refs):
    shares, out, scratch = refs[:count], refs[count], refs[count + 1 :]
    buffers = {level: scratch[3 * (level - 2) : 3 * (level - 1)] for level in (2, 3, 4)}
    g = buffers[2][0]
    tiles, planes = g.shape[0], g.shape[1]
    for t in range(tiles):
        for p in range(planes):
            for b in range(count):
                value = shares[b][t, p, 0:8] + shares[(b - 1) % count][t, p, 8:16]
                g[t, p, 8 * b : 8 * b + 8] = value
    solve(2, LANES * tiles, buffers)
    for c in range(out.shape[0]):
        out[c] = g[0, (c - 3) % planes, 0:16]


def finish_kernel(field, e2, f1, f0, below, above, out, u1_a, u1_b, u0_a, u0_b, pot):
    share2 = e2.shape[0]
    rows2 = e2.shape[1]
    value = e2[...].reshape(share2 * rows2, LANES)
    value = dot(value, one_hot(lambda r, c: r == c // 2))
    for c in range(share2):
        part = value[rows2 * c : rows2 * (c + 1)]
        for p in (2 * c, 2 * c + 1):
            u1_a[0, p, pl.ds(0, rows2, stride=2), :] = part
            u1_a[0, p, pl.ds(1, rows2, stride=2), :] = part
    count1 = 2 * share2
    sweep(u1_b, u1_a, 1, count1 - 1)
    sweep(u1_a, u1_b, 2, count1 - 2)
    sweep(u1_b, u1_a, 3, count1 - 3)
    share1 = f1.shape[0]
    rows1 = 24
    parts = []
    for c in range(share1):
        parts.append(f1[c, 4 : 4 + rows1] + u1_b[0, 4 + c, 4 : 4 + rows1] * (1.0 / 343.0))
    value = jnp.concatenate(parts, axis=0)
    main = dot(value, one_hot(lambda r, c: r == 32 + c // 2))
    side = dot(value, one_hot(lambda r, c: r == jnp.where(c < 64, 96 + c // 2, c // 2 - 32)))
    for t, value in enumerate((main, side)):
        for c in range(share1):
            part = value[rows1 * c : rows1 * (c + 1)]
            for p in (2 * c, 2 * c + 1):
                u0_a[t, p, pl.ds(0, rows1, stride=2), :] = part
                u0_a[t, p, pl.ds(1, rows1, stride=2), :] = part
    count0 = 2 * share1
    sweep(u0_b, u0_a, 1, count0 - 1)
    sweep(u0_a, u0_b, 2, count0 - 2)
    sweep(u0_b, u0_a, 3, count0 - 3)

    planes, rows = field.shape[1], field.shape[2]
    scale = 1.0 / 343.0
    for i in range(planes + 1):
        value = u0_b[0, 4 + i, ROW0 : ROW0 + rows] * scale + f0[fine_plane(i)]
        if i <= SPILL:
            value = value + below[2 + i]
        if i >= planes - SPILL:
            value = value + above[i - (planes - SPILL)]
        pot[i, 0:rows] = value
        edge = u0_b[0, 4 + i, ROW0 + rows : ROW0 + rows + 1] * scale
        if i < planes:
            edge = edge + f0[6, i + SPILL : i + SPILL + 1]
            if i <= SPILL:
                edge = edge + below[0, i + SPILL + planes : i + SPILL + planes + 1]
            if i >= planes - SPILL:
                edge = edge + above[6, i + SPILL - planes : i + SPILL - planes + 1]
            pot[i, rows : rows + 1] = edge
    column = f0[7] + pltpu.roll(below[1], LANES - planes, 1) + pltpu.roll(above[7], planes, 1)
    lane = iota((rows, LANES), 1)
    for i in range(planes):
        here = pot[i, 0:rows]
        out[0, i] = field[0, i] - (pot[i + 1, 0:rows] - here)
        out[1, i] = field[1, i] - (pot[i, 1 : rows + 1] - here)
        beyond = pltpu.roll(u0_b[1, 4 + i, ROW0 : ROW0 + rows], LANES - 1, 1) * scale
        beyond = beyond + pltpu.roll(column, LANES - 1 - (i + SPILL), 1)
        next_z = jnp.where(lane == LANES - 1, beyond, pltpu.roll(here, LANES - 1, 1))
        out[2, i] = field[2, i] - (next_z - here)


def fine_plane(i):
    return i + SPILL if i <= 0 else i + SPILL + 2


def fine_share_kernel(field, main, up, down, base, first, second):
    planes = field.shape[1]
    count = base.shape[1]
    edge = [p for p in range(count) if p < PLANE0 or p > PLANE0 + planes]
    clear_planes(base, edge)
    clear_planes(first, edge)
    clear_planes(second, edge)
    fill_source(field, base)
    low, high = PLANE0, PLANE0 + planes + 1
    seventh = 1.0 / 7.0
    sweep(first, base, low - 1, high + 1, base, seventh)
    sweep(second, first, low - 2, high + 2, base, seventh)
    sweep(first, second, low - 3, high + 3, base, seventh)
    sweep(second, first, low - 4, high + 4, base, seventh)
    sweep(first, second, low - 5, high + 5, base, seventh)
    share, rows = main.shape[0], main.shape[1]

    def step(p, carry):
        main[p] = first[0, p + 1] * weight(0)
        return carry

    lax.fori_loop(0, share, step, 0)

    def read_up(p):
        return first[1, p + 1]

    def read_down(p):
        lane = iota((rows, LANES), 1)
        turned = pltpu.roll(first[1, p + 1], SPILL, 1)
        return jnp.where(lane == SPILL, pltpu.roll(first[0, p + 1], SPILL, 1), turned)

    for k, packed in enumerate(pack_lanes(read_up, share, 0, 6, 8, rows)):
        up[k] = packed * weight(0)
    for k, packed in enumerate(pack_lanes(read_down, share, 0, 6, 8, rows)):
        down[k] = packed * weight(0)


def fine_z_kernel(main, own, above, below, out, column_out, down, up):
    share, rows = main.shape[0], main.shape[1]
    lane = iota((rows, LANES), 1)
    column = jnp.zeros((rows, LANES), F32)
    for p in range(share):
        tile, k = p // 16, p % 16
        value = main[p] + unpacked(below[tile], k, 8, 0, 6, 0, rows)
        value = value + unpacked(above[tile], k, 8, 0, 5, LANES - 5, rows)
        out[p] = value
        turned = pltpu.roll(own[tile], (p - 8 * k) % LANES, 1)
        turned = turned + pltpu.roll(above[tile], (p - 8 * k - 5) % LANES, 1)
        column = jnp.where(lane == p, turned, column)
        down[p] = value[1:9]
        up[p] = value[40:48]
    column_out[...] = column
    down[share] = column[1:9]
    up[share] = column[40:48]


def fine_y_kernel(main, column, above, below, out, work):
    share = main.shape[0]
    rows = out.shape[1]

    def folded(k, value):
        work[...] = value
        work[33:41] = work[33:41] + above[k]
        work[8:16] = work[8:16] + below[k]

    out[6] = jnp.zeros((rows, LANES), F32)
    for p in range(share):
        folded(p, main[p])
        place = p if p <= SPILL else p + 2
        out[place] = work[ROW0 : ROW0 + rows]
        out[6, p : p + 1] = work[ROW0 + rows : ROW0 + rows + 1]
    folded(share, column[...])
    out[7] = work[ROW0 : ROW0 + rows]


def body(field):
    nx, ny, nz = field.shape[1:]
    size_x, size_y, size_z = lax.axis_size("gx"), lax.axis_size("gy"), lax.axis_size("gz")
    n1 = nx // 2
    share1 = n1 + 4
    rows0 = ny + 16
    rows1 = ny // 2 + 8
    planes0 = nx + 13

    def from_offset(value, axis, offset):
        count = lax.axis_size(axis)
        pairs = [(source, (source - offset) % count) for source in range(count)]
        return lax.ppermute(value, axis, pairs)

    level0 = (2, planes0, rows0, LANES)
    level1 = (1, n1 + 12, ny // 2 + 16, LANES)
    packed = ((n1 // 2 + 6) // 2) * 16
    up, down, far, g1 = call(
        spread_kernel,
        [shape(packed + rows1, LANES), shape(packed + rows1, LANES), shape(packed, LANES),
         shape(share1, rows1, LANES)],
        [level0, level0, level1, level1],
        6_000_000,
        field,
    )
    received = []
    for o in range(1, size_z):
        message = down if o == 1 else (up if o == size_z - 1 else far)
        received.append(from_offset(message, "gz", o))
    share0 = nx + 11
    main, f_up, f_down = call(
        fine_share_kernel,
        [shape(share0, rows0, LANES), shape(2, rows0, LANES), shape(2, rows0, LANES)],
        [level0, level0, level0],
        20_000_000,
        field,
    )
    f_above = from_offset(f_down, "gz", 1)
    f_below = from_offset(f_up, "gz", -1)

    tiles = size_z * 32 // LANES
    g2, g1 = call(
        functools.partial(gather_z_kernel, size_z),
        [shape(tiles, n1 // 2 + 6, 16, LANES), shape(share1, rows1, LANES)],
        [],
        500_000,
        far, g1, *received,
    )
    shares = [g2] + [from_offset(g2, "gx", o) for o in range(1, size_x)]
    inputs = [g1]
    sources = [(0, 0, 0, share1)]
    spans = {1: (0, 9), -1: (3, 12), 2: (0, 1), -2: (11, 12)}
    residues = {}
    for offset, span in spans.items():
        residues.setdefault(offset % size_x, []).append((offset, span))
    for residue, members in residues.items():
        if residue == 0:
            sources.extend((0, offset, 0, share1) for offset, span in members)
            continue
        first = min(span[0] for offset, span in members)
        last = max(span[1] for offset, span in members)
        inputs.append(from_offset(g1[first:last], "gx", residue))
        sources.extend((len(inputs) - 1, offset, first, last - first) for offset, span in members)
    g2 = call(
        functools.partial(fold_x_kernel, size_x),
        shape(tiles, 4 * size_x, 16, LANES),
        [],
        100_000,
        *shares,
    )
    planes1 = n1 + 14
    extra = -(-planes1 // 8)
    g1, g1_down, g1_up = call(
        functools.partial(window_x_kernel, tuple(sources)),
        [shape(planes1, rows1, LANES), shape(planes1 + extra, 8, LANES),
         shape(planes1 + extra, 8, LANES)],
        [],
        100_000,
        *inputs,
    )
    shares = [g2] + [from_offset(g2, "gy", o) for o in range(1, size_y)]
    g1_above = from_offset(g1_down, "gy", 1)
    g1_below = from_offset(g1_up, "gy", -1)

    main, column, f_down, f_up = call(
        fine_z_kernel,
        [shape(share0, rows0, LANES), shape(rows0, LANES), shape(share0 + 1, 8, LANES),
         shape(share0 + 1, 8, LANES)],
        [],
        1_000_000,
        main, f_up, f_above, f_below,
    )
    f_above = from_offset(f_down, "gy", 1)
    f_below = from_offset(f_up, "gy", -1)
    f0 = call(
        fine_y_kernel,
        shape(share0 + 2, ny, LANES),
        [(rows0, LANES)],
        500_000,
        main, column, f_above, f_below,
    )
    f_down, f_up = f0[0:8], jnp.concatenate([f0[6:8], f0[share0 + 2 - 6 :]], axis=0)
    if size_x == 2:
        other = from_offset(jnp.concatenate([f_down, f_up[2:]], axis=0), "gx", 1)
        f_above, f_below = other[0:8], jnp.concatenate([other[6:8], other[8:]], axis=0)
    else:
        f_above = from_offset(f_down, "gx", 1)
        f_below = from_offset(f_up, "gx", -1)

    scratch = []
    for level in (2, 3, 4):
        cut = 2 ** (level - 2)
        extent = (max(1, tiles // cut), 4 * size_x // cut, 8 * size_y // cut, LANES)
        scratch.extend([extent] * 3)
    e2 = call(
        functools.partial(coarse_kernel, size_y),
        shape(n1 // 2 + 6, 16, LANES),
        scratch,
        5_000_000,
        *shares,
    )
    window = (1, planes1, ny // 2 + 16, LANES)
    f1 = call(
        fine_tail_kernel,
        shape(share1, ny // 2 + 16, LANES),
        [window, window, window],
        3_000_000,
        g1, g1_above, g1_below,
    )
    return call(
        finish_kernel,
        shape(*field.shape),
        [level1, level1, (2, nx + 8, rows0, LANES), (2, nx + 8, rows0, LANES),
         (nx + 1, ny + 8, LANES)],
        6_000_000,
        field, e2, f1, f0, f_below, f_above,
    )


def solution(mesh):
    in_specs = (P(None, "gx", "gy", "gz"),)
    out_specs = P(None, "gx", "gy", "gz")
    return jax.shard_map(body, mesh=mesh, in_specs=in_specs, out_specs=out_specs, check_vma=False)
```

time: 582 us -> 94.1 us (0.16)
  waiting for transfers between devices: 326 us -> 21.1 us
  starting transfers between devices: 122 us -> 16.7 us
  blocking collectives: 63.6 us -> 0 us
  Pallas kernels: 0 us -> 54.9 us
  local copies, waits for them, and re-layouts: 51.2 us -> 1.17 us
  other arithmetic: 17.1 us -> 0.02 us
    ppermute x152 -> x15, waiting for transfers between devices: 326 us -> 21.1 us  [from_offset(): return lax.ppermute(value, axis, pairs)]
    ppermute x152 -> x15, starting transfers between devices: 122 us -> 16.7 us  [from_offset(): return lax.ppermute(value, axis, pairs)]
    all_gather x1 -> x0, blocking collectives: 63.6 us -> none  [collect(): lax.all_gather(source[None], ('gx', 'gy', 'gz'), axis=0, tiled=True)]
    pallas_call x0 -> x10, Pallas kernels: none -> 54.9 us  [call(): pl.pallas_call(kernel, out_shape=outs, scratch_shapes=[pltpu.VMEM(s, F32)...]
    reshape x7 -> x0, local copies, waits for them, and re-layouts: 35 us -> none  [the longest x3 20.4 us: restrict(): values.reshape(extent[0] // 2, 2, extent[1] // 2, 2, extent[2] // 2, 2)]
    slice x168 -> x3, local copies, waits for them, and re-layouts: 8.01 us -> 0.04 us  [the longest x1 0.02 us: body(): other[0:8]]
    reduce_sum x5 -> x0, other arithmetic: 7.51 us -> none  [restrict(): return jnp.sum(blocks, axis=(1, 3, 5)) * 0.125]
    broadcast_in_dim x6 -> x0, local copies, waits for them, and re-layouts: 7.08 us -> none  [prolong(): jnp.broadcast_to(values[:, None, :, None, :, None], (extent[0], 2, extent...]
  transfers between devices with their start and end apart: 152 -> 15, of which waited for: 148 -> 7; matrix products, arithmetic and copies ran while one was open for 0% -> 0% of each run, Pallas kernels for 0% -> 29%
where the time goes in v1:
time: 94.1 us; the launch traced here: 94 us
  Pallas kernels  54.9 us (58%)
  waiting for transfers between devices  21.1 us (22%)
  starting transfers between devices  16.7 us (18%)
  local copies, waits for them, and re-layouts  1.17 us (1%)
    pallas_call x10, Pallas kernels, call(): pl.pallas_call(kernel, out_shape=outs, scratch_shapes=[pltpu.VMEM(s, F32)...  54.9 us
    ppermute x15, waiting for transfers between devices, from_offset(): return lax.ppermute(value, axis, pairs)  21.1 us
    ppermute x15, starting transfers between devices, from_offset(): return lax.ppermute(value, axis, pairs)  16.7 us
  transfers between devices with their start and end apart: 15, of which 7 were waited for; matrix products, arithmetic and copies ran while one was open for 0% of the time, Pallas kernels for 29%

profile of v1, /device:TPU:0, one launch (start us, length us, event | category | flops | bytes accessed | tf_op | source)
XLA Modules:
  0.0 94.0 jit_solution(16829318979952761304)
XLA Ops:
  0.0 1.1 %copy-done = f32[3,16,32,128]{3,2,1,0:T(8,128)S(1)} copy-done((f32[3,16,32,128]{3,2,1,0:T(8,128)S(1)}, f32[3,16,32,128]{3,2,1,0:T(8,128)}, u32[]{:S(2)}) %copy-start) | copy-done | bytes 786456
  1.1 15.1 %shard_map.23 = (f32[27,48,128]{2,1,0:T(8,128)S(1)}, f32[2,48,128]{2,1,0:T(8,128)S(1)}, f32[2,48,128]{2,1,0:T(8,128)S(1)}) custom-call(f32[3,16,32,128]{3,2,1,0:T(8,128)S(1)} %copy-done), custom_call_target="tpu_custom_call" | custom-call | flops 20000000 | bytes 786432 | tf_op jit(solution)/shard_map/pallas_call | solution.py:30
  16.3 3.1 %collective-permute-start.11 = (f32[2,48,128]{2,1,0:T(8,128)S(1)}, f32[2,48,128]{2,1,0:T(8,128)S(1)}, u32[]{:S(2)}, u32[]{:S(2)}) collective-permute-start(f32[2,48,128]{2,1,0:T(8,128)S(1)} %get-tuple-element.31.own), channel_id=1, source_target_pairs={{0,1},{1,2},{2,3},{3,0},{4,5},{5,6},{6,7},{7,4},{8,9},{9,10},{10,1... | collective-permute-start | bytes 147464 | tf_op jit(solution)/shard_map/ppermute | solution.py:574
  19.3 2.1 %collective-permute-start.10 = (f32[2,48,128]{2,1,0:T(8,128)S(1)}, f32[2,48,128]{2,1,0:T(8,128)S(1)}, u32[]{:S(2)}, u32[]{:S(2)}) collective-permute-start(f32[2,48,128]{2,1,0:T(8,128)S(1)} %get-tuple-element.32), channel_id=1, source_target_pairs={{0,3},{1,0},{2,1},{3,2},{4,7},{5,4},{6,5},{7,6},{8,11},{9,8},{10,9... | collective-permute-start | bytes 147464 | tf_op jit(solution)/shard_map/ppermute | solution.py:574
  21.4 2.1 %collective-permute-done.11.below = f32[2,48,128]{2,1,0:T(8,128)S(1)} collective-permute-done((f32[2,48,128]{2,1,0:T(8,128)S(1)}, f32[2,48,128]{2,1,0:T(8,128)S(1)}, u32[]{:S(2)}, u32[]{:S(2)}) %collective-permute-start.11) | collective-permute-done | bytes 49184 | tf_op jit(solution)/shard_map/ppermute | solution.py:574
  23.5 0.4 collective-permute-done.10.above
  23.9 0.7 shard_map.24
  24.7 0.5 collective-permute-start.13
  25.2 11.8 %shard_map.17 = (f32[104,128]{1,0:T(8,128)S(1)}, f32[104,128]{1,0:T(8,128)S(1)}, f32[80,128]{1,0:T(8,128)S(1)}, f32[12,24,128]{2,1,0:T(8,128)S(1)}) custom-call(f32[3,16,32,128]{3,2,1,0:T(8,128)S(1)} %copy-done.1), custom_call_target="tpu_custom_call" | custom-call | flops 6000000 | bytes 786432 | tf_op jit(solution)/shard_map/pallas_call | solution.py:30
  37.1 3.4 %collective-permute-start = (f32[104,128]{1,0:T(8,128)S(1)}, f32[104,128]{1,0:T(8,128)S(1)}, u32[]{:S(2)}, u32[]{:S(2)}) collective-permute-start(f32[104,128]{1,0:T(8,128)S(1)} %get-tuple-element.23), channel_id=1, source_target_pairs={{0,3},{1,0},{2,1},{3,2},{4,7},{5,4},{6,5},{7,6},{8,11},{9,8},{10,9... | collective-permute-start | bytes 159752 | tf_op jit(solution)/shard_map/ppermute | solution.py:574
  40.5 0.7 collective-permute-start.1
  41.2 4.5 %collective-permute-done.1.refs_3_ = f32[80,128]{1,0:T(8,128)S(1)} collective-permute-done((f32[80,128]{1,0:T(8,128)S(1)}, f32[80,128]{1,0:T(8,128)S(1)}, u32[]{:S(2)}, u32[]{:S(2)}) %collective-permute-start.1) | collective-permute-done | bytes 40992 | tf_op jit(solution)/shard_map/ppermute | solution.py:574
  45.8 1.2 %collective-permute-done.2.refs_4_ = f32[104,128]{1,0:T(8,128)S(1)} collective-permute-done((f32[104,128]{1,0:T(8,128)S(1)}, f32[104,128]{1,0:T(8,128)S(1)}, u32[]{:S(2)}, u32[]{:S(2)}) %collective-permute-start.2) | collective-permute-done | bytes 53280 | tf_op jit(solution)/shard_map/ppermute | solution.py:574
  47.1 1.8 %collective-permute-start.7 = (f32[12,24,128]{2,1,0:T(8,128)S(1)}, f32[12,24,128]{2,1,0:T(8,128)S(1)}, u32[]{:S(2)}, u32[]{:S(2)}) collective-permute-start(f32[12,24,128]{2,1,0:T(8,128)S(1)} %get-tuple-element.26.refs_0_), channel_id=1, source_target_pairs={{0,16},{16,0},{1,17},{17,1},{2,18},{18,2},{3,19},{19,3},{4,20},{20... | collective-permute-start | bytes 442376 | tf_op jit(solution)/shard_map/ppermute | solution.py:574
  49.0 0.4 shard_map.25.f0
  49.7 1.7 %collective-permute-start.3 = (f32[1,10,16,128]{3,2,1,0:T(8,128)S(1)}, f32[1,10,16,128]{3,2,1,0:T(8,128)S(1)}, u32[]{:S(2)}, u32[]{:S(2)}) collective-permute-start(f32[1,10,16,128]{3,2,1,0:T(8,128)S(1)} %get-tuple-element.25.refs_0_), channel_id=1, source_target_pairs={{0,16},{16,0},{1,17},{17,1},{2,18},{18,2},{3,19},{19,3},{4,20},{20... | collective-permute-start | bytes 245768 | tf_op jit(solution)/shard_map/ppermute | solution.py:574
  51.5 8.3 %collective-permute-done.3.refs_1_ = f32[1,10,16,128]{3,2,1,0:T(8,128)S(1)} collective-permute-done((f32[1,10,16,128]{3,2,1,0:T(8,128)S(1)}, f32[1,10,16,128]{3,2,1,0:T(8,128)S(1)}, u32[]{:S(2)}, u32[]{:S(2)}) %collective-permute-start.3) | collective-permute-done | bytes 81952 | tf_op jit(solution)/shard_map/ppermute | solution.py:574
  60.1 0.4 collective-permute-start.9
  60.5 1.6 %collective-permute-start.5 = (f32[1,8,16,128]{3,2,1,0:T(8,128)S(1)}, f32[1,8,16,128]{3,2,1,0:T(8,128)S(1)}, u32[]{:S(2)}, u32[]{:S(2)}) collective-permute-start(f32[1,8,16,128]{3,2,1,0:T(8,128)S(1)} %shard_map.19.refs_0_), channel_id=1, source_target_pairs={{0,8},{4,12},{8,0},{12,4},{1,9},{5,13},{9,1},{13,5},{2,10},{6,14},... | collective-permute-start | bytes 196616 | tf_op jit(solution)/shard_map/ppermute | solution.py:574
  62.1 0.7 collective-permute-start.6
  62.8 4.3 %collective-permute-done.5.refs_2_ = f32[1,8,16,128]{3,2,1,0:T(8,128)S(1)} collective-permute-done((f32[1,8,16,128]{3,2,1,0:T(8,128)S(1)}, f32[1,8,16,128]{3,2,1,0:T(8,128)S(1)}, u32[]{:S(2)}, u32[]{:S(2)}) %collective-permute-start.5) | collective-permute-done | bytes 65568 | tf_op jit(solution)/shard_map/ppermute | solution.py:574
  67.4 8.1 %shard_map.20.e2 = f32[10,16,128]{2,1,0:T(8,128)S(1)} custom-call(f32[1,8,16,128]{3,2,1,0:T(8,128)S(1)} %shard_map.19.refs_0_, f32[1,8,16,128]{3,2,1,0:T(8,128)S(1)} %collective-permute-done.4.refs_1_, f32[1,8,16,128]{3,2,1,0:T(8,128)S(1)} %collective-permute-done.5.refs_2_, f32[1,8,16,128]{3,2,1,0:T(8,128)S(1)} %collective-permute-done.6.refs_3_), custom_call_target="tpu_custom_call" | custom-call | flops 5000000 | bytes 262144 | tf_op jit(solution)/shard_map/pallas_call | solution.py:30
  75.5 6.6 %shard_map.22.f1 = f32[12,32,128]{2,1,0:T(8,128)S(1)} custom-call(f32[22,24,128]{2,1,0:T(8,128)S(1)} %get-tuple-element.27.g1, f32[25,8,128]{2,1,0:T(8,128)S(1)} %collective-permute-done.8.above, f32[25,8,128]{2,1,0:T(8,128)S(1)} %collective-permute-done.9.below), custom_call_target="tpu_custom_call" | custom-call | flops 3000000 | bytes 475136 | tf_op jit(solution)/shard_map/pallas_call | solution.py:30
  82.2 11.8 %shard_map.26 = f32[3,16,32,128]{3,2,1,0:T(8,128)} custom-call(f32[3,16,32,128]{3,2,1,0:T(8,128)S(1)} %copy-done.1, f32[10,16,128]{2,1,0:T(8,128)S(1)} %shard_map.20.e2, f32[12,32,128]{2,1,0:T(8,128)S(1)} %shard_map.22.f1, f32[29,32,128]{2,1,0:T(8,128)S(1)} %shard_map.25.f0, f32[8,32,128]{2,1,0:T(8,128)S(1)} %get-tuple-element.38.below, ...), custom_call_target="tpu_custom_call" | custom-call | flops 6000000 | bytes 1802240 | tf_op jit(solution)/shard_map/pallas_call | solution.py:30
  (24 shorter events, 1.2 us)
Async XLA Ops:
  0.0 1.1 %copy-start = (f32[3,16,32,128]{3,2,1,0:T(8,128)S(1)}, f32[3,16,32,128]{3,2,1,0:T(8,128)}, u32[]{:S(2)}) copy-start(f32[3,16,32,128]{3,2,1,0:T(8,128)} %field.5) | copy-start | bytes 2359300
  1.1 24.1 %copy-start.1 = (f32[3,16,32,128]{3,2,1,0:T(8,128)S(1)}, f32[3,16,32,128]{3,2,1,0:T(8,128)}, u32[]{:S(2)}) copy-start(f32[3,16,32,128]{3,2,1,0:T(8,128)} %field.5) | copy-start | bytes 2359300
  16.3 7.3 %collective-permute-start.11 = (f32[2,48,128]{2,1,0:T(8,128)S(1)}, f32[2,48,128]{2,1,0:T(8,128)S(1)}, u32[]{:S(2)}, u32[]{:S(2)}) collective-permute-start(f32[2,48,128]{2,1,0:T(8,128)S(1)} %get-tuple-element.31.own), channel_id=1, source_target_pairs={{0,1},{1,2},{2,3},{3,0},{4,5},{5,6},{6,7},{7,4},{8,9},{9,10},{10,1... | collective-permute-start | bytes 147464 | tf_op jit(solution)/shard_map/ppermute | solution.py:574
  19.3 4.6 %collective-permute-start.10 = (f32[2,48,128]{2,1,0:T(8,128)S(1)}, f32[2,48,128]{2,1,0:T(8,128)S(1)}, u32[]{:S(2)}, u32[]{:S(2)}) collective-permute-start(f32[2,48,128]{2,1,0:T(8,128)S(1)} %get-tuple-element.32), channel_id=1, source_target_pairs={{0,3},{1,0},{2,1},{3,2},{4,7},{5,4},{6,5},{7,6},{8,11},{9,8},{10,9... | collective-permute-start | bytes 147464 | tf_op jit(solution)/shard_map/ppermute | solution.py:574
  24.7 24.3 %collective-permute-start.12 = (f32[28,8,128]{2,1,0:T(8,128)S(1)}, f32[28,8,128]{2,1,0:T(8,128)S(1)}, u32[]{:S(2)}, u32[]{:S(2)}) collective-permute-start(f32[28,8,128]{2,1,0:T(8,128)S(1)} %get-tuple-element.35), channel_id=1, source_target_pairs={{0,12},{4,0},{8,4},{12,8},{1,13},{5,1},{9,5},{13,9},{2,14},{6,2},{... | collective-permute-start | bytes 344072 | tf_op jit(solution)/shard_map/ppermute | solution.py:574
  24.7 24.2 %collective-permute-start.13 = (f32[28,8,128]{2,1,0:T(8,128)S(1)}, f32[28,8,128]{2,1,0:T(8,128)S(1)}, u32[]{:S(2)}, u32[]{:S(2)}) collective-permute-start(f32[28,8,128]{2,1,0:T(8,128)S(1)} %get-tuple-element.36), channel_id=1, source_target_pairs={{0,4},{4,8},{8,12},{12,0},{1,5},{5,9},{9,13},{13,1},{2,6},{6,10},{... | collective-permute-start | bytes 344072 | tf_op jit(solution)/shard_map/ppermute | solution.py:574
  37.1 8.7 %collective-permute-start = (f32[104,128]{1,0:T(8,128)S(1)}, f32[104,128]{1,0:T(8,128)S(1)}, u32[]{:S(2)}, u32[]{:S(2)}) collective-permute-start(f32[104,128]{1,0:T(8,128)S(1)} %get-tuple-element.23), channel_id=1, source_target_pairs={{0,3},{1,0},{2,1},{3,2},{4,7},{5,4},{6,5},{7,6},{8,11},{9,8},{10,9... | collective-permute-start | bytes 159752 | tf_op jit(solution)/shard_map/ppermute | solution.py:574
  40.5 6.4 %collective-permute-start.2 = (f32[104,128]{1,0:T(8,128)S(1)}, f32[104,128]{1,0:T(8,128)S(1)}, u32[]{:S(2)}, u32[]{:S(2)}) collective-permute-start(f32[104,128]{1,0:T(8,128)S(1)} %get-tuple-element.24), channel_id=1, source_target_pairs={{0,1},{1,2},{2,3},{3,0},{4,5},{5,6},{6,7},{7,4},{8,9},{9,10},{10,1... | collective-permute-start | bytes 159752 | tf_op jit(solution)/shard_map/ppermute | solution.py:574
  40.5 5.3 %collective-permute-start.1 = (f32[80,128]{1,0:T(8,128)S(1)}, f32[80,128]{1,0:T(8,128)S(1)}, u32[]{:S(2)}, u32[]{:S(2)}) collective-permute-start(f32[80,128]{1,0:T(8,128)S(1)} %get-tuple-element.21.refs_0_), channel_id=1, source_target_pairs={{0,2},{1,3},{2,0},{3,1},{4,6},{5,7},{6,4},{7,5},{8,10},{9,11},{10,... | collective-permute-start | bytes 122888 | tf_op jit(solution)/shard_map/ppermute | solution.py:574
  47.1 12.7 %collective-permute-start.7 = (f32[12,24,128]{2,1,0:T(8,128)S(1)}, f32[12,24,128]{2,1,0:T(8,128)S(1)}, u32[]{:S(2)}, u32[]{:S(2)}) collective-permute-start(f32[12,24,128]{2,1,0:T(8,128)S(1)} %get-tuple-element.26.refs_0_), channel_id=1, source_target_pairs={{0,16},{16,0},{1,17},{17,1},{2,18},{18,2},{3,19},{19,3},{4,20},{20... | collective-permute-start | bytes 442376 | tf_op jit(solution)/shard_map/ppermute | solution.py:574
  49.4 32.7 %collective-permute-start.14 = (f32[14,32,128]{2,1,0:T(8,128)S(1)}, f32[14,32,128]{2,1,0:T(8,128)S(1)}, u32[]{:S(2)}, u32[]{:S(2)}) collective-permute-start(f32[14,32,128]{2,1,0:T(8,128)S(1)} %pad_maximum_fusion), channel_id=1, source_target_pairs={{0,16},{16,0},{1,17},{17,1},{2,18},{18,2},{3,19},{19,3},{4,20},{20... | collective-permute-start | bytes 688136 | tf_op jit(solution)/shard_map/ppermute | solution.py:574
  49.7 10.0 %collective-permute-start.3 = (f32[1,10,16,128]{3,2,1,0:T(8,128)S(1)}, f32[1,10,16,128]{3,2,1,0:T(8,128)S(1)}, u32[]{:S(2)}, u32[]{:S(2)}) collective-permute-start(f32[1,10,16,128]{3,2,1,0:T(8,128)S(1)} %get-tuple-element.25.refs_0_), channel_id=1, source_target_pairs={{0,16},{16,0},{1,17},{17,1},{2,18},{18,2},{3,19},{19,3},{4,20},{20... | collective-permute-start | bytes 245768 | tf_op jit(solution)/shard_map/ppermute | solution.py:574
  59.8 2.3 %collective-permute-start.4 = (f32[1,8,16,128]{3,2,1,0:T(8,128)S(1)}, f32[1,8,16,128]{3,2,1,0:T(8,128)S(1)}, u32[]{:S(2)}, u32[]{:S(2)}) collective-permute-start(f32[1,8,16,128]{3,2,1,0:T(8,128)S(1)} %shard_map.19.refs_0_), channel_id=1, source_target_pairs={{0,12},{4,0},{8,4},{12,8},{1,13},{5,1},{9,5},{13,9},{2,14},{6,2},{... | collective-permute-start | bytes 196616 | tf_op jit(solution)/shard_map/ppermute | solution.py:574
  59.9 15.6 %collective-permute-start.8 = (f32[25,8,128]{2,1,0:T(8,128)S(1)}, f32[25,8,128]{2,1,0:T(8,128)S(1)}, u32[]{:S(2)}, u32[]{:S(2)}) collective-permute-start(f32[25,8,128]{2,1,0:T(8,128)S(1)} %get-tuple-element.28), channel_id=1, source_target_pairs={{0,12},{4,0},{8,4},{12,8},{1,13},{5,1},{9,5},{13,9},{2,14},{6,2},{... | collective-permute-start | bytes 307208 | tf_op jit(solution)/shard_map/ppermute | solution.py:574
  60.1 15.4 %collective-permute-start.9 = (f32[25,8,128]{2,1,0:T(8,128)S(1)}, f32[25,8,128]{2,1,0:T(8,128)S(1)}, u32[]{:S(2)}, u32[]{:S(2)}) collective-permute-start(f32[25,8,128]{2,1,0:T(8,128)S(1)} %get-tuple-element.29), channel_id=1, source_target_pairs={{0,4},{4,8},{8,12},{12,0},{1,5},{5,9},{9,13},{13,1},{2,6},{6,10},{... | collective-permute-start | bytes 307208 | tf_op jit(solution)/shard_map/ppermute | solution.py:574
  60.5 6.6 %collective-permute-start.5 = (f32[1,8,16,128]{3,2,1,0:T(8,128)S(1)}, f32[1,8,16,128]{3,2,1,0:T(8,128)S(1)}, u32[]{:S(2)}, u32[]{:S(2)}) collective-permute-start(f32[1,8,16,128]{3,2,1,0:T(8,128)S(1)} %shard_map.19.refs_0_), channel_id=1, source_target_pairs={{0,8},{4,12},{8,0},{12,4},{1,9},{5,13},{9,1},{13,5},{2,10},{6,14},... | collective-permute-start | bytes 196616 | tf_op jit(solution)/shard_map/ppermute | solution.py:574
  62.1 5.3 %collective-permute-start.6 = (f32[1,8,16,128]{3,2,1,0:T(8,128)S(1)}, f32[1,8,16,128]{3,2,1,0:T(8,128)S(1)}, u32[]{:S(2)}, u32[]{:S(2)}) collective-permute-start(f32[1,8,16,128]{3,2,1,0:T(8,128)S(1)} %shard_map.19.refs_0_), channel_id=1, source_target_pairs={{0,4},{4,8},{8,12},{12,0},{1,5},{5,9},{9,13},{13,1},{2,6},{6,10},{... | collective-permute-start | bytes 196616 | tf_op jit(solution)/shard_map/ppermute | solution.py:574

commit v2 on v1

--- a/solution.py
+++ b/solution.py
@@ -77,22 +77,17 @@
     return out
 
 
-def sweep(target, source, low, high, base=None, scale=None, period=None, base_shift=0):
-    def step(plane, carry):
-        if period is None:
-            below, above = plane - 1, plane + 1
-        else:
-            below = lax.rem(plane + period - 1, period)
-            above = lax.rem(plane + 1, period)
+def sweep(target, source, low, high, base=None, scale=None, period=None):
+    for plane in range(low, high):
+        below, above = plane - 1, plane + 1
+        if period is not None:
+            below, above = below % period, above % period
         for t, value in enumerate(seven_sum(source, plane, below, above)):
             if scale is not None:
                 value = value * scale
             if base is not None:
-                value = value + base[t, plane + base_shift]
+                value = value + base[t, plane]
             target[t, plane] = value
-        return carry
-
-    lax.fori_loop(low, high, step, 0, unroll=False)
 
 
 PLANE0 = 6
@@ -123,13 +118,8 @@
         target[1, p, ROW0 : ROW0 + rows] = jnp.where(lane == 0, turned, 0.0)
         target[1, p, ROW0 + rows : ROW0 + rows + 8] = zero8
 
-    one_plane(0, zeros)
-
-    def step(i, carry):
-        one_plane(i, field[0, i - 1])
-        return carry
-
-    lax.fori_loop(1, planes, step, 0)
+    for i in range(planes):
+        one_plane(i, field[0, i - 1] if i else zeros)
     p = PLANE0 + planes
     target[0, p] = jnp.zeros(target.shape[2:], F32)
     target[1, p] = jnp.zeros(target.shape[2:], F32)
@@ -287,15 +277,11 @@
 def fine_tail_kernel(g1, above, below, out, base, first, second):
     planes, rows1 = g1.shape[0], g1.shape[1]
 
-    def step(p, carry):
+    for p in range(planes):
         base[0, p] = jnp.zeros(base.shape[2:], F32)
         base[0, p, 4 : 4 + rows1] = g1[p]
         base[0, p, 22:30] = base[0, p, 22:30] + above[p]
         base[0, p, 1:9] = base[0, p, 1:9] + below[p]
-        return carry
-
-    lax.fori_loop(0, planes, step, 0)
-    for p in range(planes):
         ninth = p % 8
         base[0, p, 30:31] = base[0, p, 30:31] + above[planes + p // 8, ninth : ninth + 1]
         base[0, p, 9:10] = base[0, p, 9:10] + below[planes + p // 8, ninth : ninth + 1]
@@ -484,7 +470,7 @@
     return i + SPILL if i <= 0 else i + SPILL + 2
 
 
-def fine_share_kernel(field, main, up, down, base, first, second):
+def fine_share_kernel(field, after, main, up, down, base, first, second):
     planes = field.shape[1]
     count = base.shape[1]
     edge = [p for p in range(count) if p < PLANE0 or p > PLANE0 + planes]
@@ -501,11 +487,8 @@
     sweep(first, second, low - 5, high + 5, base, seventh)
     share, rows = main.shape[0], main.shape[1]
 
-    def step(p, carry):
+    for p in range(share):
         main[p] = first[0, p + 1] * weight(0)
-        return carry
-
-    lax.fori_loop(0, share, step, 0)
 
     def read_up(p):
         return first[1, p + 1]
@@ -594,7 +577,7 @@
         [shape(share0, rows0, LANES), shape(2, rows0, LANES), shape(2, rows0, LANES)],
         [level0, level0, level0],
         20_000_000,
-        field,
+        field, far,
     )
     f_above = from_offset(f_down, "gz", 1)
     f_below = from_offset(f_up, "gz", -1)

time: 94.1 us -> 59.2 us (0.63)
  Pallas kernels: 54.9 us -> 18 us
  waiting for transfers between devices: 21.1 us -> 25 us
  starting transfers between devices: 16.7 us -> 14.2 us
    pallas_call x10, Pallas kernels: 54.9 us -> 18 us  [call(): pl.pallas_call(kernel, out_shape=outs, scratch_shapes=[pltpu.VMEM(s, F32)...]
    ppermute x15, waiting for transfers between devices: 21.1 us -> 25 us  [from_offset(): return lax.ppermute(value, axis, pairs)]
    ppermute x15, starting transfers between devices: 16.7 us -> 14.2 us  [from_offset(): return lax.ppermute(value, axis, pairs)]
  transfers between devices with their start and end apart: 15 -> 15, of which waited for: 7 -> 7; matrix products, arithmetic and copies ran while one was open for 0% -> 0% of each run, Pallas kernels for 29% -> 9%
where the time goes in v2:
time: 59.2 us; the launch traced here: 58.6 us
  waiting for transfers between devices  25 us (42%)
  Pallas kernels  18 us (30%)
  starting transfers between devices  14.2 us (24%)
  local copies, waits for them, and re-layouts  1.18 us (2%)
    ppermute x15, waiting for transfers between devices, from_offset(): return lax.ppermute(value, axis, pairs)  25 us
    pallas_call x10, Pallas kernels, call(): pl.pallas_call(kernel, out_shape=outs, scratch_shapes=[pltpu.VMEM(s, F32)...  18 us
    ppermute x15, starting transfers between devices, from_offset(): return lax.ppermute(value, axis, pairs)  14.2 us
  transfers between devices with their start and end apart: 15, of which 7 were waited for; matrix products, arithmetic and copies ran while one was open for 0% of the time, Pallas kernels for 9%

profile of v2, /device:TPU:0, one launch (start us, length us, event | category | flops | bytes accessed | tf_op | source)
XLA Modules:
  0.0 58.6 jit_solution(10261935599648212024)
XLA Ops:
  0.0 1.1 %copy-done = f32[3,16,32,128]{3,2,1,0:T(8,128)S(1)} copy-done((f32[3,16,32,128]{3,2,1,0:T(8,128)S(1)}, f32[3,16,32,128]{3,2,1,0:T(8,128)}, u32[]{:S(2)}) %copy-start) | copy-done | bytes 786456
  1.1 2.9 %shard_map.17 = (f32[104,128]{1,0:T(8,128)S(1)}, f32[104,128]{1,0:T(8,128)S(1)}, f32[80,128]{1,0:T(8,128)S(1)}, f32[12,24,128]{2,1,0:T(8,128)S(1)}) custom-call(f32[3,16,32,128]{3,2,1,0:T(8,128)S(1)} %copy-done), custom_call_target="tpu_custom_call" | custom-call | flops 6000000 | bytes 786432 | tf_op jit(solution)/shard_map/pallas_call | solution.py:30
  4.1 5.5 %shard_map.23 = (f32[27,48,128]{2,1,0:T(8,128)S(1)}, f32[2,48,128]{2,1,0:T(8,128)S(1)}, f32[2,48,128]{2,1,0:T(8,128)S(1)}) custom-call(f32[3,16,32,128]{3,2,1,0:T(8,128)S(1)} %copy-done, f32[80,128]{1,0:T(8,128)S(1)} %get-tuple-element.21.refs_0_.after), custom_call_target="tpu_custom_call" | custom-call | flops 20000000 | bytes 827392 | tf_op jit(solution)/shard_map/pallas_call | solution.py:30
  9.5 5.1 %collective-permute-start.10 = (f32[2,48,128]{2,1,0:T(8,128)S(1)}, f32[2,48,128]{2,1,0:T(8,128)S(1)}, u32[]{:S(2)}, u32[]{:S(2)}) collective-permute-start(f32[2,48,128]{2,1,0:T(8,128)S(1)} %get-tuple-element.32), channel_id=1, source_target_pairs={{0,3},{1,0},{2,1},{3,2},{4,7},{5,4},{6,5},{7,6},{8,11},{9,8},{10,9... | collective-permute-start | bytes 147464 | tf_op jit(solution)/shard_map/ppermute | solution.py:557
  14.6 1.7 %collective-permute-done.10.above = f32[2,48,128]{2,1,0:T(8,128)S(1)} collective-permute-done((f32[2,48,128]{2,1,0:T(8,128)S(1)}, f32[2,48,128]{2,1,0:T(8,128)S(1)}, u32[]{:S(2)}, u32[]{:S(2)}) %collective-permute-start.10) | collective-permute-done | bytes 49184 | tf_op jit(solution)/shard_map/ppermute | solution.py:557
  16.4 4.1 %collective-permute-done.11.below = f32[2,48,128]{2,1,0:T(8,128)S(1)} collective-permute-done((f32[2,48,128]{2,1,0:T(8,128)S(1)}, f32[2,48,128]{2,1,0:T(8,128)S(1)}, u32[]{:S(2)}, u32[]{:S(2)}) %collective-permute-start.11) | collective-permute-done | bytes 49184 | tf_op jit(solution)/shard_map/ppermute | solution.py:557
  20.5 0.7 %shard_map.24 = (f32[27,48,128]{2,1,0:T(8,128)S(1)}, f32[48,128]{1,0:T(8,128)S(1)}, f32[28,8,128]{2,1,0:T(8,128)S(1)}, f32[28,8,128]{2,1,0:T(8,128)S(1)}) custom-call(f32[27,48,128]{2,1,0:T(8,128)S(1)} %get-tuple-element.30.main, f32[2,48,128]{2,1,0:T(8,128)S(1)} %get-tuple-element.31.own, f32[2,48,128]{2,1,0:T(8,128)S(1)} %collective-permute-done.10.above, ...), custom_call_target="tpu_custom_call" | custom-call | flops 1000000 | bytes 811008 | tf_op jit(solution)/shard_map/pallas_call | solution.py:30
  21.3 0.5 collective-permute-start.13
  21.8 2.0 %collective-permute-start.2 = (f32[104,128]{1,0:T(8,128)S(1)}, f32[104,128]{1,0:T(8,128)S(1)}, u32[]{:S(2)}, u32[]{:S(2)}) collective-permute-start(f32[104,128]{1,0:T(8,128)S(1)} %get-tuple-element.24), channel_id=1, source_target_pairs={{0,1},{1,2},{2,3},{3,0},{4,5},{5,6},{6,7},{7,4},{8,9},{9,10},{10,1... | collective-permute-start | bytes 159752 | tf_op jit(solution)/shard_map/ppermute | solution.py:557
  23.8 6.2 %collective-permute-done.1.refs_3_ = f32[80,128]{1,0:T(8,128)S(1)} collective-permute-done((f32[80,128]{1,0:T(8,128)S(1)}, f32[80,128]{1,0:T(8,128)S(1)}, u32[]{:S(2)}, u32[]{:S(2)}) %collective-permute-start.1) | collective-permute-done | bytes 40992 | tf_op jit(solution)/shard_map/ppermute | solution.py:557
  30.3 1.6 %collective-permute-start.7 = (f32[12,24,128]{2,1,0:T(8,128)S(1)}, f32[12,24,128]{2,1,0:T(8,128)S(1)}, u32[]{:S(2)}, u32[]{:S(2)}) collective-permute-start(f32[12,24,128]{2,1,0:T(8,128)S(1)} %get-tuple-element.26.refs_0_), channel_id=1, source_target_pairs={{0,16},{16,0},{1,17},{17,1},{2,18},{18,2},{3,19},{19,3},{4,20},{20... | collective-permute-start | bytes 442376 | tf_op jit(solution)/shard_map/ppermute | solution.py:557
  31.9 0.4 shard_map.25.f0
  32.3 0.6 collective-permute-start.14
  32.9 1.5 %collective-permute-start.3 = (f32[1,10,16,128]{3,2,1,0:T(8,128)S(1)}, f32[1,10,16,128]{3,2,1,0:T(8,128)S(1)}, u32[]{:S(2)}, u32[]{:S(2)}) collective-permute-start(f32[1,10,16,128]{3,2,1,0:T(8,128)S(1)} %get-tuple-element.25.refs_0_), channel_id=1, source_target_pairs={{0,16},{16,0},{1,17},{17,1},{2,18},{18,2},{3,19},{19,3},{4,20},{20... | collective-permute-start | bytes 245768 | tf_op jit(solution)/shard_map/ppermute | solution.py:557
  34.4 8.5 %collective-permute-done.3.refs_1_ = f32[1,10,16,128]{3,2,1,0:T(8,128)S(1)} collective-permute-done((f32[1,10,16,128]{3,2,1,0:T(8,128)S(1)}, f32[1,10,16,128]{3,2,1,0:T(8,128)S(1)}, u32[]{:S(2)}, u32[]{:S(2)}) %collective-permute-start.3) | collective-permute-done | bytes 81952 | tf_op jit(solution)/shard_map/ppermute | solution.py:557
  43.0 1.8 %collective-permute-start.8 = (f32[25,8,128]{2,1,0:T(8,128)S(1)}, f32[25,8,128]{2,1,0:T(8,128)S(1)}, u32[]{:S(2)}, u32[]{:S(2)}) collective-permute-start(f32[25,8,128]{2,1,0:T(8,128)S(1)} %get-tuple-element.28), channel_id=1, source_target_pairs={{0,12},{4,0},{8,4},{12,8},{1,13},{5,1},{9,5},{13,9},{2,14},{6,2},{... | collective-permute-start | bytes 307208 | tf_op jit(solution)/shard_map/ppermute | solution.py:557
  44.8 0.7 %collective-permute-start.5 = (f32[1,8,16,128]{3,2,1,0:T(8,128)S(1)}, f32[1,8,16,128]{3,2,1,0:T(8,128)S(1)}, u32[]{:S(2)}, u32[]{:S(2)}) collective-permute-start(f32[1,8,16,128]{3,2,1,0:T(8,128)S(1)} %shard_map.19.refs_0_), channel_id=1, source_target_pairs={{0,8},{4,12},{8,0},{12,4},{1,9},{5,13},{9,1},{13,5},{2,10},{6,14},... | collective-permute-start | bytes 196616 | tf_op jit(solution)/shard_map/ppermute | solution.py:557
  45.5 1.1 %collective-permute-done.6.refs_3_ = f32[1,8,16,128]{3,2,1,0:T(8,128)S(1)} collective-permute-done((f32[1,8,16,128]{3,2,1,0:T(8,128)S(1)}, f32[1,8,16,128]{3,2,1,0:T(8,128)S(1)}, u32[]{:S(2)}, u32[]{:S(2)}) %collective-permute-start.6) | collective-permute-done | bytes 65568 | tf_op jit(solution)/shard_map/ppermute | solution.py:557
  46.6 0.3 collective-permute-start.4
  46.9 2.9 %collective-permute-done.5.refs_2_ = f32[1,8,16,128]{3,2,1,0:T(8,128)S(1)} collective-permute-done((f32[1,8,16,128]{3,2,1,0:T(8,128)S(1)}, f32[1,8,16,128]{3,2,1,0:T(8,128)S(1)}, u32[]{:S(2)}, u32[]{:S(2)}) %collective-permute-start.5) | collective-permute-done | bytes 65568 | tf_op jit(solution)/shard_map/ppermute | solution.py:557
  49.8 0.4 collective-permute-done.4.refs_1_
  50.2 3.6 %shard_map.20.e2 = f32[10,16,128]{2,1,0:T(8,128)S(1)} custom-call(f32[1,8,16,128]{3,2,1,0:T(8,128)S(1)} %shard_map.19.refs_0_, f32[1,8,16,128]{3,2,1,0:T(8,128)S(1)} %collective-permute-done.4.refs_1_, f32[1,8,16,128]{3,2,1,0:T(8,128)S(1)} %collective-permute-done.5.refs_2_, f32[1,8,16,128]{3,2,1,0:T(8,128)S(1)} %collective-permute-done.6.refs_3_), custom_call_target="tpu_custom_call" | custom-call | flops 5000000 | bytes 262144 | tf_op jit(solution)/shard_map/pallas_call | solution.py:30
  53.8 0.8 %shard_map.22.f1 = f32[12,32,128]{2,1,0:T(8,128)S(1)} custom-call(f32[22,24,128]{2,1,0:T(8,128)S(1)} %get-tuple-element.27.g1, f32[25,8,128]{2,1,0:T(8,128)S(1)} %collective-permute-done.8.above, f32[25,8,128]{2,1,0:T(8,128)S(1)} %collective-permute-done.9.below), custom_call_target="tpu_custom_call" | custom-call | flops 3000000 | bytes 475136 | tf_op jit(solution)/shard_map/pallas_call | solution.py:30
  54.7 3.9 %shard_map.26 = f32[3,16,32,128]{3,2,1,0:T(8,128)} custom-call(f32[3,16,32,128]{3,2,1,0:T(8,128)S(1)} %copy-done.1, f32[10,16,128]{2,1,0:T(8,128)S(1)} %shard_map.20.e2, f32[12,32,128]{2,1,0:T(8,128)S(1)} %shard_map.22.f1, f32[29,32,128]{2,1,0:T(8,128)S(1)} %shard_map.25.f0, f32[8,32,128]{2,1,0:T(8,128)S(1)} %get-tuple-element.38.below, ...), custom_call_target="tpu_custom_call" | custom-call | flops 6000000 | bytes 1802240 | tf_op jit(solution)/shard_map/pallas_call | solution.py:30
  (24 shorter events, 0.5 us)
Async XLA Ops:
  0.0 1.1 %copy-start = (f32[3,16,32,128]{3,2,1,0:T(8,128)S(1)}, f32[3,16,32,128]{3,2,1,0:T(8,128)}, u32[]{:S(2)}) copy-start(f32[3,16,32,128]{3,2,1,0:T(8,128)} %field.5) | copy-start | bytes 2359300
  9.5 6.9 %collective-permute-start.10 = (f32[2,48,128]{2,1,0:T(8,128)S(1)}, f32[2,48,128]{2,1,0:T(8,128)S(1)}, u32[]{:S(2)}, u32[]{:S(2)}) collective-permute-start(f32[2,48,128]{2,1,0:T(8,128)S(1)} %get-tuple-element.32), channel_id=1, source_target_pairs={{0,3},{1,0},{2,1},{3,2},{4,7},{5,4},{6,5},{7,6},{8,11},{9,8},{10,9... | collective-permute-start | bytes 147464 | tf_op jit(solution)/shard_map/ppermute | solution.py:557
  14.6 5.9 %collective-permute-start.11 = (f32[2,48,128]{2,1,0:T(8,128)S(1)}, f32[2,48,128]{2,1,0:T(8,128)S(1)}, u32[]{:S(2)}, u32[]{:S(2)}) collective-permute-start(f32[2,48,128]{2,1,0:T(8,128)S(1)} %get-tuple-element.31.own), channel_id=1, source_target_pairs={{0,1},{1,2},{2,3},{3,0},{4,5},{5,6},{6,7},{7,4},{8,9},{9,10},{10,1... | collective-permute-start | bytes 147464 | tf_op jit(solution)/shard_map/ppermute | solution.py:557
  21.3 10.6 %collective-permute-start.12 = (f32[28,8,128]{2,1,0:T(8,128)S(1)}, f32[28,8,128]{2,1,0:T(8,128)S(1)}, u32[]{:S(2)}, u32[]{:S(2)}) collective-permute-start(f32[28,8,128]{2,1,0:T(8,128)S(1)} %get-tuple-element.35), channel_id=1, source_target_pairs={{0,12},{4,0},{8,4},{12,8},{1,13},{5,1},{9,5},{13,9},{2,14},{6,2},{... | collective-permute-start | bytes 344072 | tf_op jit(solution)/shard_map/ppermute | solution.py:557
  21.3 10.6 %collective-permute-start.13 = (f32[28,8,128]{2,1,0:T(8,128)S(1)}, f32[28,8,128]{2,1,0:T(8,128)S(1)}, u32[]{:S(2)}, u32[]{:S(2)}) collective-permute-start(f32[28,8,128]{2,1,0:T(8,128)S(1)} %get-tuple-element.36), channel_id=1, source_target_pairs={{0,4},{4,8},{8,12},{12,0},{1,5},{5,9},{9,13},{13,1},{2,6},{6,10},{... | collective-permute-start | bytes 344072 | tf_op jit(solution)/shard_map/ppermute | solution.py:557
  21.8 8.3 %collective-permute-start = (f32[104,128]{1,0:T(8,128)S(1)}, f32[104,128]{1,0:T(8,128)S(1)}, u32[]{:S(2)}, u32[]{:S(2)}) collective-permute-start(f32[104,128]{1,0:T(8,128)S(1)} %get-tuple-element.23), channel_id=1, source_target_pairs={{0,3},{1,0},{2,1},{3,2},{4,7},{5,4},{6,5},{7,6},{8,11},{9,8},{10,9... | collective-permute-start | bytes 159752 | tf_op jit(solution)/shard_map/ppermute | solution.py:557
  21.8 8.3 %collective-permute-start.2 = (f32[104,128]{1,0:T(8,128)S(1)}, f32[104,128]{1,0:T(8,128)S(1)}, u32[]{:S(2)}, u32[]{:S(2)}) collective-permute-start(f32[104,128]{1,0:T(8,128)S(1)} %get-tuple-element.24), channel_id=1, source_target_pairs={{0,1},{1,2},{2,3},{3,0},{4,5},{5,6},{6,7},{7,4},{8,9},{9,10},{10,1... | collective-permute-start | bytes 159752 | tf_op jit(solution)/shard_map/ppermute | solution.py:557
  23.8 6.2 %collective-permute-start.1 = (f32[80,128]{1,0:T(8,128)S(1)}, f32[80,128]{1,0:T(8,128)S(1)}, u32[]{:S(2)}, u32[]{:S(2)}) collective-permute-start(f32[80,128]{1,0:T(8,128)S(1)} %get-tuple-element.21.refs_0_.after), channel_id=1, source_target_pairs={{0,2},{1,3},{2,0},{3,1},{4,6},{5,7},{6,4},{7,5},{8,10},{9,11},{10,... | collective-permute-start | bytes 122888 | tf_op jit(solution)/shard_map/ppermute | solution.py:557
  30.3 12.7 %collective-permute-start.7 = (f32[12,24,128]{2,1,0:T(8,128)S(1)}, f32[12,24,128]{2,1,0:T(8,128)S(1)}, u32[]{:S(2)}, u32[]{:S(2)}) collective-permute-start(f32[12,24,128]{2,1,0:T(8,128)S(1)} %get-tuple-element.26.refs_0_), channel_id=1, source_target_pairs={{0,16},{16,0},{1,17},{17,1},{2,18},{18,2},{3,19},{19,3},{4,20},{20... | collective-permute-start | bytes 442376 | tf_op jit(solution)/shard_map/ppermute | solution.py:557
  32.3 22.3 %collective-permute-start.14 = (f32[14,32,128]{2,1,0:T(8,128)S(1)}, f32[14,32,128]{2,1,0:T(8,128)S(1)}, u32[]{:S(2)}, u32[]{:S(2)}) collective-permute-start(f32[14,32,128]{2,1,0:T(8,128)S(1)} %pad_maximum_fusion), channel_id=1, source_target_pairs={{0,16},{16,0},{1,17},{17,1},{2,18},{18,2},{3,19},{19,3},{4,20},{20... | collective-permute-start | bytes 688136 | tf_op jit(solution)/shard_map/ppermute | solution.py:557
  32.9 10.0 %collective-permute-start.3 = (f32[1,10,16,128]{3,2,1,0:T(8,128)S(1)}, f32[1,10,16,128]{3,2,1,0:T(8,128)S(1)}, u32[]{:S(2)}, u32[]{:S(2)}) collective-permute-start(f32[1,10,16,128]{3,2,1,0:T(8,128)S(1)} %get-tuple-element.25.refs_0_), channel_id=1, source_target_pairs={{0,16},{16,0},{1,17},{17,1},{2,18},{18,2},{3,19},{19,3},{4,20},{20... | collective-permute-start | bytes 245768 | tf_op jit(solution)/shard_map/ppermute | solution.py:557
  42.9 3.7 %collective-permute-start.6 = (f32[1,8,16,128]{3,2,1,0:T(8,128)S(1)}, f32[1,8,16,128]{3,2,1,0:T(8,128)S(1)}, u32[]{:S(2)}, u32[]{:S(2)}) collective-permute-start(f32[1,8,16,128]{3,2,1,0:T(8,128)S(1)} %shard_map.19.refs_0_), channel_id=1, source_target_pairs={{0,4},{4,8},{8,12},{12,0},{1,5},{5,9},{9,13},{13,1},{2,6},{6,10},{... | collective-permute-start | bytes 196616 | tf_op jit(solution)/shard_map/ppermute | solution.py:557
  43.0 11.7 %copy-start.1 = (f32[3,16,32,128]{3,2,1,0:T(8,128)S(1)}, f32[3,16,32,128]{3,2,1,0:T(8,128)}, u32[]{:S(2)}) copy-start(f32[3,16,32,128]{3,2,1,0:T(8,128)} %field.5) | copy-start | bytes 2359300
  43.0 10.8 %collective-permute-start.8 = (f32[25,8,128]{2,1,0:T(8,128)S(1)}, f32[25,8,128]{2,1,0:T(8,128)S(1)}, u32[]{:S(2)}, u32[]{:S(2)}) collective-permute-start(f32[25,8,128]{2,1,0:T(8,128)S(1)} %get-tuple-element.28), channel_id=1, source_target_pairs={{0,12},{4,0},{8,4},{12,8},{1,13},{5,1},{9,5},{13,9},{2,14},{6,2},{... | collective-permute-start | bytes 307208 | tf_op jit(solution)/shard_map/ppermute | solution.py:557
  44.8 9.0 %collective-permute-start.9 = (f32[25,8,128]{2,1,0:T(8,128)S(1)}, f32[25,8,128]{2,1,0:T(8,128)S(1)}, u32[]{:S(2)}, u32[]{:S(2)}) collective-permute-start(f32[25,8,128]{2,1,0:T(8,128)S(1)} %get-tuple-element.29), channel_id=1, source_target_pairs={{0,4},{4,8},{8,12},{12,0},{1,5},{5,9},{9,13},{13,1},{2,6},{6,10},{... | collective-permute-start | bytes 307208 | tf_op jit(solution)/shard_map/ppermute | solution.py:557
  44.8 5.0 %collective-permute-start.5 = (f32[1,8,16,128]{3,2,1,0:T(8,128)S(1)}, f32[1,8,16,128]{3,2,1,0:T(8,128)S(1)}, u32[]{:S(2)}, u32[]{:S(2)}) collective-permute-start(f32[1,8,16,128]{3,2,1,0:T(8,128)S(1)} %shard_map.19.refs_0_), channel_id=1, source_target_pairs={{0,8},{4,12},{8,0},{12,4},{1,9},{5,13},{9,1},{13,5},{2,10},{6,14},... | collective-permute-start | bytes 196616 | tf_op jit(solution)/shard_map/ppermute | solution.py:557
  46.6 3.6 %collective-permute-start.4 = (f32[1,8,16,128]{3,2,1,0:T(8,128)S(1)}, f32[1,8,16,128]{3,2,1,0:T(8,128)S(1)}, u32[]{:S(2)}, u32[]{:S(2)}) collective-permute-start(f32[1,8,16,128]{3,2,1,0:T(8,128)S(1)} %shard_map.19.refs_0_), channel_id=1, source_target_pairs={{0,12},{4,0},{8,4},{12,8},{1,13},{5,1},{9,5},{13,9},{2,14},{6,2},{... | collective-permute-start | bytes 196616 | tf_op jit(solution)/shard_map/ppermute | solution.py:557

commit v3 on v2

--- a/solution.py
+++ b/solution.py
@@ -15,6 +15,7 @@
 F32 = jnp.float32
 LANES = 128
 VMEM_LIMIT = 16 * 1024 * 1024
+PEAK_FLOPS_PER_US = 1.15e9
 
 
 def weight(level):
@@ -25,14 +26,14 @@
     return jax.ShapeDtypeStruct(extent, F32)
 
 
-def call(kernel, outs, scratch, flops, *args):
-    bytes_accessed = 4 * sum(a.size for a in args)
+def call(kernel, outs, scratch, microseconds, *args):
+    flops = int(microseconds * PEAK_FLOPS_PER_US)
     return pl.pallas_call(
         kernel,
         out_shape=outs,
         scratch_shapes=[pltpu.VMEM(s, F32) for s in scratch],
         compiler_params=pltpu.CompilerParams(vmem_limit_bytes=VMEM_LIMIT),
-        cost_estimate=pl.CostEstimate(flops=flops, bytes_accessed=bytes_accessed, transcendentals=0),
+        cost_estimate=pl.CostEstimate(flops=flops, bytes_accessed=0, transcendentals=0),
     )(*args)
 
 
@@ -564,7 +565,7 @@
         [shape(packed + rows1, LANES), shape(packed + rows1, LANES), shape(packed, LANES),
          shape(share1, rows1, LANES)],
         [level0, level0, level1, level1],
-        6_000_000,
+        2.9,
         field,
     )
     received = []
@@ -576,7 +577,7 @@
         fine_share_kernel,
         [shape(share0, rows0, LANES), shape(2, rows0, LANES), shape(2, rows0, LANES)],
         [level0, level0, level0],
-        20_000_000,
+        5.4,
         field, far,
     )
     f_above = from_offset(f_down, "gz", 1)
@@ -587,7 +588,7 @@
         functools.partial(gather_z_kernel, size_z),
         [shape(tiles, n1 // 2 + 6, 16, LANES), shape(share1, rows1, LANES)],
         [],
-        500_000,
+        0.2,
         far, g1, *received,
     )
     shares = [g2] + [from_offset(g2, "gx", o) for o in range(1, size_x)]
@@ -609,7 +610,7 @@
         functools.partial(fold_x_kernel, size_x),
         shape(tiles, 4 * size_x, 16, LANES),
         [],
-        100_000,
+        0.05,
         *shares,
     )
     planes1 = n1 + 14
@@ -619,7 +620,7 @@
         [shape(planes1, rows1, LANES), shape(planes1 + extra, 8, LANES),
          shape(planes1 + extra, 8, LANES)],
         [],
-        100_000,
+        0.05,
         *inputs,
     )
     shares = [g2] + [from_offset(g2, "gy", o) for o in range(1, size_y)]
@@ -631,7 +632,7 @@
         [shape(share0, rows0, LANES), shape(rows0, LANES), shape(share0 + 1, 8, LANES),
          shape(share0 + 1, 8, LANES)],
         [],
-        1_000_000,
+        0.7,
         main, f_up, f_above, f_below,
     )
     f_above = from_offset(f_down, "gy", 1)
@@ -640,7 +641,7 @@
         fine_y_kernel,
         shape(share0 + 2, ny, LANES),
         [(rows0, LANES)],
-        500_000,
+        0.4,
         main, column, f_above, f_below,
     )
     f_down, f_up = f0[0:8], jnp.concatenate([f0[6:8], f0[share0 + 2 - 6 :]], axis=0)
@@ -660,7 +661,7 @@
         functools.partial(coarse_kernel, size_y),
         shape(n1 // 2 + 6, 16, LANES),
         scratch,
-        5_000_000,
+        3.5,
         *shares,
     )
     window = (1, planes1, ny // 2 + 16, LANES)
@@ -668,7 +669,7 @@
         fine_tail_kernel,
         shape(share1, ny // 2 + 16, LANES),
         [window, window, window],
-        3_000_000,
+        0.8,
         g1, g1_above, g1_below,
     )
     return call(
@@ -676,7 +677,7 @@
         shape(*field.shape),
         [level1, level1, (2, nx + 8, rows0, LANES), (2, nx + 8, rows0, LANES),
          (nx + 1, ny + 8, LANES)],
-        6_000_000,
+        3.9,
         field, e2, f1, f0, f_below, f_above,
     )
 

time: 59.2 us -> 44.1 us (0.74)
  waiting for transfers between devices: 25 us -> 7.71 us
  starting transfers between devices: 14.2 us -> 16.6 us
    ppermute x15, waiting for transfers between devices: 25 us -> 7.71 us  [from_offset(): return lax.ppermute(value, axis, pairs)]
    ppermute x15, starting transfers between devices: 14.2 us -> 16.6 us  [from_offset(): return lax.ppermute(value, axis, pairs)]
  transfers between devices with their start and end apart: 15 -> 15, of which waited for: 7 -> 6; matrix products, arithmetic and copies ran while one was open for 0% -> 0% of each run, Pallas kernels for 9% -> 13%
where the time goes in v3:
time: 44.1 us; the launch traced here: 43.9 us
  Pallas kernels  18 us (41%)
  starting transfers between devices  16.6 us (38%)
  waiting for transfers between devices  7.71 us (17%)
  local copies, waits for them, and re-layouts  1.41 us (3%)
    pallas_call x10, Pallas kernels, call(): pl.pallas_call(kernel, out_shape=outs, scratch_shapes=[pltpu.VMEM(s, F32)...  18 us
    ppermute x15, starting transfers between devices, from_offset(): return lax.ppermute(value, axis, pairs)  16.6 us
    ppermute x15, waiting for transfers between devices, from_offset(): return lax.ppermute(value, axis, pairs)  7.71 us
    unnamed x4, local copies, waits for them, and re-layouts  1.37 us
  transfers between devices with their start and end apart: 15, of which 6 were waited for; matrix products, arithmetic and copies ran while one was open for 0% of the time, Pallas kernels for 13%

profile of v3, /device:TPU:0, one launch (start us, length us, event | category | flops | bytes accessed | tf_op | source)
XLA Modules:
  0.0 43.9 jit_solution(9424706045580437240)
XLA Ops:
  0.0 1.1 %copy-done = f32[3,16,32,128]{3,2,1,0:T(8,128)S(1)} copy-done((f32[3,16,32,128]{3,2,1,0:T(8,128)S(1)}, f32[3,16,32,128]{3,2,1,0:T(8,128)}, u32[]{:S(2)}) %copy-start) | copy-done | bytes 786456
  1.1 2.9 %shard_map.17 = (f32[104,128]{1,0:T(8,128)S(1)}, f32[104,128]{1,0:T(8,128)S(1)}, f32[80,128]{1,0:T(8,128)S(1)}, f32[12,24,128]{2,1,0:T(8,128)S(1)}) custom-call(f32[3,16,32,128]{3,2,1,0:T(8,128)S(1)} %copy-done), custom_call_target="tpu_custom_call" | custom-call | flops 3335000064 | tf_op jit(solution)/shard_map/pallas_call | solution.py:31
  4.1 5.5 %shard_map.23 = (f32[27,48,128]{2,1,0:T(8,128)S(1)}, f32[2,48,128]{2,1,0:T(8,128)S(1)}, f32[2,48,128]{2,1,0:T(8,128)S(1)}) custom-call(f32[3,16,32,128]{3,2,1,0:T(8,128)S(1)} %copy-done, f32[80,128]{1,0:T(8,128)S(1)} %get-tuple-element.21.refs_0_.after), custom_call_target="tpu_custom_call" | custom-call | flops 6209999872 | tf_op jit(solution)/shard_map/pallas_call | solution.py:31
  9.5 5.1 %collective-permute-start.10 = (f32[2,48,128]{2,1,0:T(8,128)S(1)}, f32[2,48,128]{2,1,0:T(8,128)S(1)}, u32[]{:S(2)}, u32[]{:S(2)}) collective-permute-start(f32[2,48,128]{2,1,0:T(8,128)S(1)} %get-tuple-element.32), channel_id=1, source_target_pairs={{0,3},{1,0},{2,1},{3,2},{4,7},{5,4},{6,5},{7,6},{8,11},{9,8},{10,9... | collective-permute-start | bytes 147464 | tf_op jit(solution)/shard_map/ppermute | solution.py:558
  14.6 1.0 %collective-permute-start.1 = (f32[80,128]{1,0:T(8,128)S(1)}, f32[80,128]{1,0:T(8,128)S(1)}, u32[]{:S(2)}, u32[]{:S(2)}) collective-permute-start(f32[80,128]{1,0:T(8,128)S(1)} %get-tuple-element.21.refs_0_.after), channel_id=1, source_target_pairs={{0,2},{1,3},{2,0},{3,1},{4,6},{5,7},{6,4},{7,5},{8,10},{9,11},{10,... | collective-permute-start | bytes 122888 | tf_op jit(solution)/shard_map/ppermute | solution.py:558
  15.6 2.8 %collective-permute-start = (f32[104,128]{1,0:T(8,128)S(1)}, f32[104,128]{1,0:T(8,128)S(1)}, u32[]{:S(2)}, u32[]{:S(2)}) collective-permute-start(f32[104,128]{1,0:T(8,128)S(1)} %get-tuple-element.23), channel_id=1, source_target_pairs={{0,3},{1,0},{2,1},{3,2},{4,7},{5,4},{6,5},{7,6},{8,11},{9,8},{10,9... | collective-permute-start | bytes 159752 | tf_op jit(solution)/shard_map/ppermute | solution.py:558
  18.5 0.6 %collective-permute-start.2 = (f32[104,128]{1,0:T(8,128)S(1)}, f32[104,128]{1,0:T(8,128)S(1)}, u32[]{:S(2)}, u32[]{:S(2)}) collective-permute-start(f32[104,128]{1,0:T(8,128)S(1)} %get-tuple-element.24), channel_id=1, source_target_pairs={{0,1},{1,2},{2,3},{3,0},{4,5},{5,6},{6,7},{7,4},{8,9},{9,10},{10,1... | collective-permute-start | bytes 159752 | tf_op jit(solution)/shard_map/ppermute | solution.py:558
  19.0 1.7 %collective-permute-done.11.below = f32[2,48,128]{2,1,0:T(8,128)S(1)} collective-permute-done((f32[2,48,128]{2,1,0:T(8,128)S(1)}, f32[2,48,128]{2,1,0:T(8,128)S(1)}, u32[]{:S(2)}, u32[]{:S(2)}) %collective-permute-start.11) | collective-permute-done | bytes 49184 | tf_op jit(solution)/shard_map/ppermute | solution.py:558
  20.8 0.7 %shard_map.24 = (f32[27,48,128]{2,1,0:T(8,128)S(1)}, f32[48,128]{1,0:T(8,128)S(1)}, f32[28,8,128]{2,1,0:T(8,128)S(1)}, f32[28,8,128]{2,1,0:T(8,128)S(1)}) custom-call(f32[27,48,128]{2,1,0:T(8,128)S(1)} %get-tuple-element.30.main, f32[2,48,128]{2,1,0:T(8,128)S(1)} %get-tuple-element.31.own, f32[2,48,128]{2,1,0:T(8,128)S(1)} %collective-permute-done.10.above, ...), custom_call_target="tpu_custom_call" | custom-call | flops 805000000 | tf_op jit(solution)/shard_map/pallas_call | solution.py:31
  21.6 0.5 %collective-permute-start.13 = (f32[28,8,128]{2,1,0:T(8,128)S(1)}, f32[28,8,128]{2,1,0:T(8,128)S(1)}, u32[]{:S(2)}, u32[]{:S(2)}) collective-permute-start(f32[28,8,128]{2,1,0:T(8,128)S(1)} %get-tuple-element.36), channel_id=1, source_target_pairs={{0,4},{4,8},{8,12},{12,0},{1,5},{5,9},{9,13},{13,1},{2,6},{6,10},{... | collective-permute-start | bytes 344072 | tf_op jit(solution)/shard_map/ppermute | solution.py:558
  22.1 2.3 %collective-permute-done.2.refs_4_ = f32[104,128]{1,0:T(8,128)S(1)} collective-permute-done((f32[104,128]{1,0:T(8,128)S(1)}, f32[104,128]{1,0:T(8,128)S(1)}, u32[]{:S(2)}, u32[]{:S(2)}) %collective-permute-start.2) | collective-permute-done | bytes 53280 | tf_op jit(solution)/shard_map/ppermute | solution.py:558
  24.6 1.6 %collective-permute-start.3 = (f32[1,10,16,128]{3,2,1,0:T(8,128)S(1)}, f32[1,10,16,128]{3,2,1,0:T(8,128)S(1)}, u32[]{:S(2)}, u32[]{:S(2)}) collective-permute-start(f32[1,10,16,128]{3,2,1,0:T(8,128)S(1)} %get-tuple-element.25.refs_0_), channel_id=1, source_target_pairs={{0,16},{16,0},{1,17},{17,1},{2,18},{18,2},{3,19},{19,3},{4,20},{20... | collective-permute-start | bytes 245768 | tf_op jit(solution)/shard_map/ppermute | solution.py:558
  26.2 0.5 %collective-permute-start.7 = (f32[12,24,128]{2,1,0:T(8,128)S(1)}, f32[12,24,128]{2,1,0:T(8,128)S(1)}, u32[]{:S(2)}, u32[]{:S(2)}) collective-permute-start(f32[12,24,128]{2,1,0:T(8,128)S(1)} %get-tuple-element.26.refs_0_), channel_id=1, source_target_pairs={{0,16},{16,0},{1,17},{17,1},{2,18},{18,2},{3,19},{19,3},{4,20},{20... | collective-permute-start | bytes 442376 | tf_op jit(solution)/shard_map/ppermute | solution.py:558
  26.7 3.1 %collective-permute-done.3.refs_1_ = f32[1,10,16,128]{3,2,1,0:T(8,128)S(1)} collective-permute-done((f32[1,10,16,128]{3,2,1,0:T(8,128)S(1)}, f32[1,10,16,128]{3,2,1,0:T(8,128)S(1)}, u32[]{:S(2)}, u32[]{:S(2)}) %collective-permute-start.3) | collective-permute-done | bytes 81952 | tf_op jit(solution)/shard_map/ppermute | solution.py:558
  29.9 0.9 %collective-permute-start.5 = (f32[1,8,16,128]{3,2,1,0:T(8,128)S(1)}, f32[1,8,16,128]{3,2,1,0:T(8,128)S(1)}, u32[]{:S(2)}, u32[]{:S(2)}) collective-permute-start(f32[1,8,16,128]{3,2,1,0:T(8,128)S(1)} %shard_map.19.refs_0_), channel_id=1, source_target_pairs={{0,8},{4,12},{8,0},{12,4},{1,9},{5,13},{9,1},{13,5},{2,10},{6,14},... | collective-permute-start | bytes 196616 | tf_op jit(solution)/shard_map/ppermute | solution.py:558
  30.7 1.4 %collective-permute-start.4 = (f32[1,8,16,128]{3,2,1,0:T(8,128)S(1)}, f32[1,8,16,128]{3,2,1,0:T(8,128)S(1)}, u32[]{:S(2)}, u32[]{:S(2)}) collective-permute-start(f32[1,8,16,128]{3,2,1,0:T(8,128)S(1)} %shard_map.19.refs_0_), channel_id=1, source_target_pairs={{0,12},{4,0},{8,4},{12,8},{1,13},{5,1},{9,5},{13,9},{2,14},{6,2},{... | collective-permute-start | bytes 196616 | tf_op jit(solution)/shard_map/ppermute | solution.py:558
  32.1 0.4 shard_map.25.f0
  32.6 1.6 %collective-permute-start.14 = (f32[14,32,128]{2,1,0:T(8,128)S(1)}, f32[14,32,128]{2,1,0:T(8,128)S(1)}, u32[]{:S(2)}, u32[]{:S(2)}) collective-permute-start(f32[14,32,128]{2,1,0:T(8,128)S(1)} %pad_maximum_fusion), channel_id=1, source_target_pairs={{0,16},{16,0},{1,17},{17,1},{2,18},{18,2},{3,19},{19,3},{4,20},{20... | collective-permute-start | bytes 688136 | tf_op jit(solution)/shard_map/ppermute | solution.py:558
  34.3 0.5 %collective-permute-start.9 = (f32[25,8,128]{2,1,0:T(8,128)S(1)}, f32[25,8,128]{2,1,0:T(8,128)S(1)}, u32[]{:S(2)}, u32[]{:S(2)}) collective-permute-start(f32[25,8,128]{2,1,0:T(8,128)S(1)} %get-tuple-element.29), channel_id=1, source_target_pairs={{0,4},{4,8},{8,12},{12,0},{1,5},{5,9},{9,13},{13,1},{2,6},{6,10},{... | collective-permute-start | bytes 307208 | tf_op jit(solution)/shard_map/ppermute | solution.py:558
  34.9 3.6 %shard_map.20.e2 = f32[10,16,128]{2,1,0:T(8,128)S(1)} custom-call(f32[1,8,16,128]{3,2,1,0:T(8,128)S(1)} %shard_map.19.refs_0_, f32[1,8,16,128]{3,2,1,0:T(8,128)S(1)} %collective-permute-done.4.refs_1_, f32[1,8,16,128]{3,2,1,0:T(8,128)S(1)} %collective-permute-done.5.refs_2_, f32[1,8,16,128]{3,2,1,0:T(8,128)S(1)} %collective-permute-done.6.refs_3_), custom_call_target="tpu_custom_call" | custom-call | flops 4024999936 | tf_op jit(solution)/shard_map/pallas_call | solution.py:31
  38.5 0.4 collective-permute-done.9.below
  38.9 0.8 %shard_map.22.f1 = f32[12,32,128]{2,1,0:T(8,128)S(1)} custom-call(f32[22,24,128]{2,1,0:T(8,128)S(1)} %get-tuple-element.27.g1, f32[25,8,128]{2,1,0:T(8,128)S(1)} %collective-permute-done.8.above, f32[25,8,128]{2,1,0:T(8,128)S(1)} %collective-permute-done.9.below), custom_call_target="tpu_custom_call" | custom-call | flops 920000000 | tf_op jit(solution)/shard_map/pallas_call | solution.py:31
  39.8 0.2 copy-done.1
  40.0 3.9 %shard_map.26 = f32[3,16,32,128]{3,2,1,0:T(8,128)} custom-call(f32[3,16,32,128]{3,2,1,0:T(8,128)S(1)} %copy-done.1, f32[10,16,128]{2,1,0:T(8,128)S(1)} %shard_map.20.e2, f32[12,32,128]{2,1,0:T(8,128)S(1)} %shard_map.22.f1, f32[29,32,128]{2,1,0:T(8,128)S(1)} %shard_map.25.f0, f32[8,32,128]{2,1,0:T(8,128)S(1)} %get-tuple-element.38.below, ...), custom_call_target="tpu_custom_call" | custom-call | flops 4485000192 | tf_op jit(solution)/shard_map/pallas_call | solution.py:31
  (24 shorter events, 0.7 us)
Async XLA Ops:
  0.0 1.1 %copy-start = (f32[3,16,32,128]{3,2,1,0:T(8,128)S(1)}, f32[3,16,32,128]{3,2,1,0:T(8,128)}, u32[]{:S(2)}) copy-start(f32[3,16,32,128]{3,2,1,0:T(8,128)} %field.5) | copy-start | bytes 2359300
  9.5 9.5 %collective-permute-start.10 = (f32[2,48,128]{2,1,0:T(8,128)S(1)}, f32[2,48,128]{2,1,0:T(8,128)S(1)}, u32[]{:S(2)}, u32[]{:S(2)}) collective-permute-start(f32[2,48,128]{2,1,0:T(8,128)S(1)} %get-tuple-element.32), channel_id=1, source_target_pairs={{0,3},{1,0},{2,1},{3,2},{4,7},{5,4},{6,5},{7,6},{8,11},{9,8},{10,9... | collective-permute-start | bytes 147464 | tf_op jit(solution)/shard_map/ppermute | solution.py:558
  14.6 6.1 %collective-permute-start.11 = (f32[2,48,128]{2,1,0:T(8,128)S(1)}, f32[2,48,128]{2,1,0:T(8,128)S(1)}, u32[]{:S(2)}, u32[]{:S(2)}) collective-permute-start(f32[2,48,128]{2,1,0:T(8,128)S(1)} %get-tuple-element.31.own), channel_id=1, source_target_pairs={{0,1},{1,2},{2,3},{3,0},{4,5},{5,6},{6,7},{7,4},{8,9},{9,10},{10,1... | collective-permute-start | bytes 147464 | tf_op jit(solution)/shard_map/ppermute | solution.py:558
  14.6 7.4 %collective-permute-start.1 = (f32[80,128]{1,0:T(8,128)S(1)}, f32[80,128]{1,0:T(8,128)S(1)}, u32[]{:S(2)}, u32[]{:S(2)}) collective-permute-start(f32[80,128]{1,0:T(8,128)S(1)} %get-tuple-element.21.refs_0_.after), channel_id=1, source_target_pairs={{0,2},{1,3},{2,0},{3,1},{4,6},{5,7},{6,4},{7,5},{8,10},{9,11},{10,... | collective-permute-start | bytes 122888 | tf_op jit(solution)/shard_map/ppermute | solution.py:558
  15.6 6.4 %collective-permute-start = (f32[104,128]{1,0:T(8,128)S(1)}, f32[104,128]{1,0:T(8,128)S(1)}, u32[]{:S(2)}, u32[]{:S(2)}) collective-permute-start(f32[104,128]{1,0:T(8,128)S(1)} %get-tuple-element.23), channel_id=1, source_target_pairs={{0,3},{1,0},{2,1},{3,2},{4,7},{5,4},{6,5},{7,6},{8,11},{9,8},{10,9... | collective-permute-start | bytes 159752 | tf_op jit(solution)/shard_map/ppermute | solution.py:558
  18.5 5.9 %collective-permute-start.2 = (f32[104,128]{1,0:T(8,128)S(1)}, f32[104,128]{1,0:T(8,128)S(1)}, u32[]{:S(2)}, u32[]{:S(2)}) collective-permute-start(f32[104,128]{1,0:T(8,128)S(1)} %get-tuple-element.24), channel_id=1, source_target_pairs={{0,1},{1,2},{2,3},{3,0},{4,5},{5,6},{6,7},{7,4},{8,9},{9,10},{10,1... | collective-permute-start | bytes 159752 | tf_op jit(solution)/shard_map/ppermute | solution.py:558
  21.5 9.2 %collective-permute-start.12 = (f32[28,8,128]{2,1,0:T(8,128)S(1)}, f32[28,8,128]{2,1,0:T(8,128)S(1)}, u32[]{:S(2)}, u32[]{:S(2)}) collective-permute-start(f32[28,8,128]{2,1,0:T(8,128)S(1)} %get-tuple-element.35), channel_id=1, source_target_pairs={{0,12},{4,0},{8,4},{12,8},{1,13},{5,1},{9,5},{13,9},{2,14},{6,2},{... | collective-permute-start | bytes 344072 | tf_op jit(solution)/shard_map/ppermute | solution.py:558
  21.6 10.6 %collective-permute-start.13 = (f32[28,8,128]{2,1,0:T(8,128)S(1)}, f32[28,8,128]{2,1,0:T(8,128)S(1)}, u32[]{:S(2)}, u32[]{:S(2)}) collective-permute-start(f32[28,8,128]{2,1,0:T(8,128)S(1)} %get-tuple-element.36), channel_id=1, source_target_pairs={{0,4},{4,8},{8,12},{12,0},{1,5},{5,9},{9,13},{13,1},{2,6},{6,10},{... | collective-permute-start | bytes 344072 | tf_op jit(solution)/shard_map/ppermute | solution.py:558
  24.6 5.2 %collective-permute-start.3 = (f32[1,10,16,128]{3,2,1,0:T(8,128)S(1)}, f32[1,10,16,128]{3,2,1,0:T(8,128)S(1)}, u32[]{:S(2)}, u32[]{:S(2)}) collective-permute-start(f32[1,10,16,128]{3,2,1,0:T(8,128)S(1)} %get-tuple-element.25.refs_0_), channel_id=1, source_target_pairs={{0,16},{16,0},{1,17},{17,1},{2,18},{18,2},{3,19},{19,3},{4,20},{20... | collective-permute-start | bytes 245768 | tf_op jit(solution)/shard_map/ppermute | solution.py:558
  26.2 8.0 %collective-permute-start.7 = (f32[12,24,128]{2,1,0:T(8,128)S(1)}, f32[12,24,128]{2,1,0:T(8,128)S(1)}, u32[]{:S(2)}, u32[]{:S(2)}) collective-permute-start(f32[12,24,128]{2,1,0:T(8,128)S(1)} %get-tuple-element.26.refs_0_), channel_id=1, source_target_pairs={{0,16},{16,0},{1,17},{17,1},{2,18},{18,2},{3,19},{19,3},{4,20},{20... | collective-permute-start | bytes 442376 | tf_op jit(solution)/shard_map/ppermute | solution.py:558
  29.8 4.5 %collective-permute-start.6 = (f32[1,8,16,128]{3,2,1,0:T(8,128)S(1)}, f32[1,8,16,128]{3,2,1,0:T(8,128)S(1)}, u32[]{:S(2)}, u32[]{:S(2)}) collective-permute-start(f32[1,8,16,128]{3,2,1,0:T(8,128)S(1)} %shard_map.19.refs_0_), channel_id=1, source_target_pairs={{0,4},{4,8},{8,12},{12,0},{1,5},{5,9},{9,13},{13,1},{2,6},{6,10},{... | collective-permute-start | bytes 196616 | tf_op jit(solution)/shard_map/ppermute | solution.py:558
  29.9 5.0 %collective-permute-start.5 = (f32[1,8,16,128]{3,2,1,0:T(8,128)S(1)}, f32[1,8,16,128]{3,2,1,0:T(8,128)S(1)}, u32[]{:S(2)}, u32[]{:S(2)}) collective-permute-start(f32[1,8,16,128]{3,2,1,0:T(8,128)S(1)} %shard_map.19.refs_0_), channel_id=1, source_target_pairs={{0,8},{4,12},{8,0},{12,4},{1,9},{5,13},{9,1},{13,5},{2,10},{6,14},... | collective-permute-start | bytes 196616 | tf_op jit(solution)/shard_map/ppermute | solution.py:558
  30.7 4.1 %collective-permute-start.4 = (f32[1,8,16,128]{3,2,1,0:T(8,128)S(1)}, f32[1,8,16,128]{3,2,1,0:T(8,128)S(1)}, u32[]{:S(2)}, u32[]{:S(2)}) collective-permute-start(f32[1,8,16,128]{3,2,1,0:T(8,128)S(1)} %shard_map.19.refs_0_), channel_id=1, source_target_pairs={{0,12},{4,0},{8,4},{12,8},{1,13},{5,1},{9,5},{13,9},{2,14},{6,2},{... | collective-permute-start | bytes 196616 | tf_op jit(solution)/shard_map/ppermute | solution.py:558
  32.6 7.2 %collective-permute-start.14 = (f32[14,32,128]{2,1,0:T(8,128)S(1)}, f32[14,32,128]{2,1,0:T(8,128)S(1)}, u32[]{:S(2)}, u32[]{:S(2)}) collective-permute-start(f32[14,32,128]{2,1,0:T(8,128)S(1)} %pad_maximum_fusion), channel_id=1, source_target_pairs={{0,16},{16,0},{1,17},{17,1},{2,18},{18,2},{3,19},{19,3},{4,20},{20... | collective-permute-start | bytes 688136 | tf_op jit(solution)/shard_map/ppermute | solution.py:558
  34.2 4.3 %collective-permute-start.8 = (f32[25,8,128]{2,1,0:T(8,128)S(1)}, f32[25,8,128]{2,1,0:T(8,128)S(1)}, u32[]{:S(2)}, u32[]{:S(2)}) collective-permute-start(f32[25,8,128]{2,1,0:T(8,128)S(1)} %get-tuple-element.28), channel_id=1, source_target_pairs={{0,12},{4,0},{8,4},{12,8},{1,13},{5,1},{9,5},{13,9},{2,14},{6,2},{... | collective-permute-start | bytes 307208 | tf_op jit(solution)/shard_map/ppermute | solution.py:558
  34.3 4.6 %collective-permute-start.9 = (f32[25,8,128]{2,1,0:T(8,128)S(1)}, f32[25,8,128]{2,1,0:T(8,128)S(1)}, u32[]{:S(2)}, u32[]{:S(2)}) collective-permute-start(f32[25,8,128]{2,1,0:T(8,128)S(1)} %get-tuple-element.29), channel_id=1, source_target_pairs={{0,4},{4,8},{8,12},{12,0},{1,5},{5,9},{9,13},{13,1},{2,6},{6,10},{... | collective-permute-start | bytes 307208 | tf_op jit(solution)/shard_map/ppermute | solution.py:558
  38.9 1.1 %copy-start.1 = (f32[3,16,32,128]{3,2,1,0:T(8,128)S(1)}, f32[3,16,32,128]{3,2,1,0:T(8,128)}, u32[]{:S(2)}) copy-start(f32[3,16,32,128]{3,2,1,0:T(8,128)} %field.5) | copy-start | bytes 2359300

commit v4 on v3

v4 whole, which is shorter than its diff:
```python
import functools

import jax
import jax.numpy as jnp
import numpy as np
from jax import lax
from jax.experimental import pallas as pl
from jax.experimental.pallas import tpu as pltpu
from jax.sharding import PartitionSpec as P

LEVELS = 5
SWEEPS = 3
COARSE_ITERS = 24


F32 = jnp.float32
LANES = 128
VMEM_LIMIT = 16 * 1024 * 1024
PEAK_FLOPS_PER_US = 1150000000.0


def weight(level):
    return 4.0**level / 7.0


def shape(*extent):
    return jax.ShapeDtypeStruct(extent, F32)


def call(kernel, outs, scratch, microseconds, *args):
    flops = int(microseconds * PEAK_FLOPS_PER_US)
    return pl.pallas_call(
        kernel,
        out_shape=outs,
        scratch_shapes=[pltpu.VMEM(s, F32) for s in scratch],
        compiler_params=pltpu.CompilerParams(vmem_limit_bytes=VMEM_LIMIT),
        cost_estimate=pl.CostEstimate(flops=flops, bytes_accessed=0, transcendentals=0),
    )(*args)


def iota(extent, dim):
    return lax.broadcasted_iota(jnp.int32, extent, dim)


def one_hot(condition):
    rows = iota((LANES, LANES), 0)
    columns = iota((LANES, LANES), 1)
    return jnp.where(condition(rows, columns), 1.0, 0.0).astype(jnp.bfloat16)


def dot(left, right):
    return lax.dot_general(
        left,
        right,
        (((1,), (0,)), ((), ())),
        precision=lax.Precision.HIGHEST,
        preferred_element_type=F32,
    )


def dot_ones(left, right):
    dims = (((1,), (0,)), ((), ()))
    large = left.astype(jnp.bfloat16)
    small = (left - large.astype(F32)).astype(jnp.bfloat16)
    total = lax.dot_general(large, right, dims, preferred_element_type=F32)
    return total + lax.dot_general(small, right, dims, preferred_element_type=F32)


def seven_sum(source, plane, below, above, wanted=None):
    tiles = source.shape[0]
    rows = source.shape[2]
    center = [source[t, plane] for t in range(tiles)]
    left = [pltpu.roll(v, 1, 1) for v in center]
    right = [pltpu.roll(v, LANES - 1, 1) for v in center]
    if tiles > 1:
        lane = iota((rows, LANES), 1)
        left = [jnp.where(lane == 0, left[t - 1], left[t]) for t in range(tiles)]
        right = [
            jnp.where(lane == LANES - 1, right[(t + 1) % tiles], right[t]) for t in range(tiles)
        ]
    out = []
    for t in range(tiles if wanted is None else wanted):
        v = center[t]
        total = v + (source[t, below] + source[t, above])
        total = total + (pltpu.roll(v, 1, 0) + pltpu.roll(v, rows - 1, 0))
        out.append(total + (left[t] + right[t]))
    return out


def sweep(target, source, low, high, base=None, scale=None, period=None, span=None):
    for plane in range(low, high):
        below, above = plane - 1, plane + 1
        if period is not None:
            below, above = below % period, above % period
        for t, value in enumerate(seven_sum(source, plane, below, above)):
            if scale is not None:
                value = value * scale
            if base is not None and (span is None or span[0] <= plane < span[1]):
                value = value + base[t, plane]
            target[t, plane] = value


PLANE0 = 6
ROW0 = 8
SPILL = 5


def fill_source(field, target):
    planes, rows = field.shape[1], field.shape[2]
    lane = iota((rows, LANES), 1)
    row = iota((rows, LANES), 0)
    row8 = iota((8, LANES), 0)
    zero8 = jnp.zeros((8, LANES), F32)
    zeros = jnp.zeros((rows, LANES), F32)

    def one_plane(i, before):
        along_x, along_y, along_z = field[0, i], field[1, i], field[2, i]
        value = before - along_x - along_y - along_z
        value = value + jnp.where(row == 0, 0.0, pltpu.roll(along_y, 1, 0))
        turned = pltpu.roll(along_z, 1, 1)
        value = value + jnp.where(lane == 0, 0.0, turned)
        p = PLANE0 + i
        target[0, p, 0:ROW0] = zero8
        target[0, p, ROW0 : ROW0 + rows] = value
        last = pltpu.roll(along_y[rows - 8 : rows], 1, 0)
        target[0, p, ROW0 + rows : ROW0 + rows + 8] = jnp.where(row8 == 0, last, 0.0)
        target[1, p, 0:ROW0] = zero8
        target[1, p, ROW0 : ROW0 + rows] = jnp.where(lane == 0, turned, 0.0)
        target[1, p, ROW0 + rows : ROW0 + rows + 8] = zero8

    for i in range(planes):
        one_plane(i, field[0, i - 1] if i else zeros)
    p = PLANE0 + planes
    target[0, p] = jnp.zeros(target.shape[2:], F32)
    target[1, p] = jnp.zeros(target.shape[2:], F32)
    target[0, p, ROW0 : ROW0 + rows] = field[0, planes - 1]


def clear_planes(target, planes):
    for t in range(target.shape[0]):
        for p in planes:
            target[t, p] = jnp.zeros(target.shape[2:], F32)


def pack_lanes(read, count, first, width, spacing, rows):
    lane = iota((rows, LANES), 1)
    per_tile = LANES // spacing
    tiles = []
    for start in range(0, count, per_tile):
        packed = jnp.zeros((rows, LANES), F32)
        for k in range(min(per_tile, count - start)):
            turned = pltpu.roll(read(start + k), (spacing * k - first) % LANES, 1)
            inside = (lane >= spacing * k) & (lane < spacing * k + width)
            packed = jnp.where(inside, turned, packed)
        tiles.append(packed)
    return tiles


def unpacked(packed, k, spacing, offset, width, first, rows):
    lane = iota((rows, LANES), 1)
    turned = pltpu.roll(packed, (first - spacing * k - offset) % LANES, 1)
    inside = (lane >= first) & (lane < first + width)
    return jnp.where(inside, turned, 0.0)


def clear_margin(target, low, high):
    clear_planes(target, (low - 2, low - 1, high, high + 1))


def spread_kernel(field, up, down, far, g1_out, zeroth, first, second, third, g1_a, g1_b):
    planes = field.shape[1]
    fill_source(field, zeroth)
    low, high = PLANE0, PLANE0 + planes + 1
    clear_margin(zeroth, low, high)
    powers = (zeroth, first, second, third)
    for k in (1, 2, 3):
        sweep(powers[k], powers[k - 1], low - k, high + k)
        clear_margin(powers[k], low - k, high + k)

    n1 = planes // 2
    rows1 = first.shape[2] // 2
    pieces = []
    for t in range(2):
        parts = []
        for c in range(-2, n1 + 2):
            p = PLANE0 + 2 * c
            total = third[t, p, pl.ds(0, rows1, stride=2), :]
            total = total + third[t, p, pl.ds(1, rows1, stride=2), :]
            total = total + third[t, p + 1, pl.ds(0, rows1, stride=2), :]
            total = total + third[t, p + 1, pl.ds(1, rows1, stride=2), :]
            parts.append(total)
        pieces.append(jnp.concatenate(parts, axis=0))
    main = one_hot(lambda r, c: c == 32 + r // 2)
    side = one_hot(lambda r, c: c == jnp.where(r < 64, 96 + r // 2, r // 2 - 32))
    g1 = (dot_ones(pieces[0], main) + dot_ones(pieces[1], side)) * (0.125 / 343.0)
    share = n1 + 4
    g1 = g1.reshape(share, rows1, LANES)
    g1_out[...] = g1

    clear_planes(g1_a, range(g1_a.shape[1]))
    clear_planes(g1_b, range(g1_b.shape[1]))
    for c in range(share):
        g1_a[0, 4 + c, 4 : 4 + rows1] = g1[c]
    sweep(g1_b, g1_a, 3, 5 + share)
    sweep(g1_a, g1_b, 2, 6 + share)
    sweep(g1_b, g1_a, 1, 7 + share)
    rows2 = g1_a.shape[2] // 2
    parts = []
    for c in range(g1_a.shape[1] // 2):
        total = g1_b[0, 2 * c, pl.ds(0, rows2, stride=2), :]
        total = total + g1_b[0, 2 * c, pl.ds(1, rows2, stride=2), :]
        total = total + g1_b[0, 2 * c + 1, pl.ds(0, rows2, stride=2), :]
        total = total + g1_b[0, 2 * c + 1, pl.ds(1, rows2, stride=2), :]
        parts.append(total)
    even = jnp.concatenate(parts[0::2], axis=0)
    odd = jnp.concatenate(parts[1::2], axis=0)
    g2 = dot_ones(even, one_hot(lambda r, c: c == r // 2))
    g2 = g2 + dot_ones(odd, one_hot(lambda r, c: c == 64 + r // 2))
    g2 = g2 * (0.125 / 343.0)
    size = g2.shape[0]
    far[...] = g2
    up[0:size] = g2
    down[0:size] = g2
    up[size : size + rows1] = pack_lanes(lambda c: g1[c], share, 89, 9, 10, rows1)[0]
    down[size : size + rows1] = pack_lanes(lambda c: g1[c], share, 30, 9, 10, rows1)[0]
    rows0 = zeroth.shape[2] - ROW0
    lane = iota((rows0, LANES), 1)

    def last_columns(i):
        p = PLANE0 + i
        return jnp.where(lane == 0, zeroth[1, p, ROW0:], zeroth[0, p, ROW0:])

    def first_columns(i):
        return zeroth[0, PLANE0 + i, ROW0:]

    size = size + rows1
    up[size:] = pack_lanes(last_columns, planes + 1, LANES - SPILL, SPILL + 1, 7, rows0)[0]
    down[size:] = pack_lanes(first_columns, planes + 1, 0, SPILL + 1, 7, rows0)[0]


def gather_z_kernel(count, *refs):
    own, g1, up, received = refs[0], refs[1], refs[2], refs[3 : 2 + count]
    g2_out, g1_out, message = refs[2 + count :]
    size = own.shape[0]
    period = 32 * count
    rows2 = 16
    tiles, planes = g2_out.shape[0], g2_out.shape[1]
    lane = iota((size, LANES), 1)
    for parity in range(2):
        totals = [jnp.zeros((size, LANES), F32) for _ in range(tiles)]
        for o in range(count):
            value = own[...] if o == 0 else received[o - 1][0:size]
            shift = (32 * o - 64 * parity) % LANES
            turned = pltpu.roll(value, shift, 1) if shift else value
            position = ((lane - shift) & (LANES - 1)) - 64 * parity
            inside = (position >= 0) & (position < 64)
            for t in range(tiles):
                lands = lax.rem(position + (32 * o + period), period) == lane + LANES * t
                totals[t] = totals[t] + jnp.where(inside & lands, turned, 0.0)
        for t in range(tiles):
            for k in range(planes // 2):
                g2_out[t, 2 * k + parity] = totals[t][rows2 * k : rows2 * (k + 1)]
    rows1 = g1.shape[1]
    above = received[0][size : size + rows1]
    below = received[count - 2][size : size + rows1]
    share = g1.shape[0]
    for c in range(share):
        value = g1[c] + unpacked(below, c, 10, 0, 9, 25, rows1)
        g1_out[c] = value + unpacked(above, c, 10, 0, 9, 94, rows1)
    lane = iota((ROWS_SENT, LANES), 1)
    for q in range(share // 2):
        even, odd = g1_out[2 * q, 2 : 2 + ROWS_SENT], g1_out[2 * q + 1, 2 : 2 + ROWS_SENT]
        value = jnp.where(lane < 64, pltpu.roll(even, LANES - 32, 1), pltpu.roll(odd, 32, 1))
        message[ROWS_SENT * q : ROWS_SENT * (q + 1)] = value
    start = ROWS_SENT * (share // 2)
    for q in range(-(-share // 8)):
        packed = jnp.zeros((ROWS_SENT, LANES), F32)
        for k in range(min(8, share - 8 * q)):
            value = g1_out[8 * q + k, 2 : 2 + ROWS_SENT]
            low = pltpu.roll(value, (16 * k - 24) % LANES, 1)
            high = pltpu.roll(value, (16 * k + 8 - 96) % LANES, 1)
            packed = jnp.where((lane >= 16 * k) & (lane < 16 * k + 8), low, packed)
            packed = jnp.where((lane >= 16 * k + 8) & (lane < 16 * k + 16), high, packed)
        message[start : start + ROWS_SENT] = packed
        start += ROWS_SENT
    rows0 = (message.shape[0] - start) // 3
    for k, strip in enumerate((received[count - 2], received[0], up)):
        message[start + rows0 * k : start + rows0 * (k + 1)] = strip[size + rows1 :]


ROWS_SENT = 20


def plane_sent(message, share, c):
    lane = iota((ROWS_SENT, LANES), 1)
    pair = message[ROWS_SENT * (c // 2) : ROWS_SENT * (c // 2 + 1)]
    inside = (lane >= 32) & (lane < 96)
    value = jnp.where(inside, pltpu.roll(pair, LANES - 32 if c % 2 else 32, 1), 0.0)
    start = ROWS_SENT * (share // 2 + c // 8)
    sides = message[start : start + ROWS_SENT]
    k = c % 8
    low = pltpu.roll(sides, (24 - 16 * k) % LANES, 1)
    high = pltpu.roll(sides, (88 - 16 * k) % LANES, 1)
    value = jnp.where((lane >= 24) & (lane < 32), low, value)
    return jnp.where((lane >= 96) & (lane < 104), high, value)


def fold_x_kernel(count, *refs):
    shares, out = refs[:count], refs[count]
    tiles, period = out.shape[0], out.shape[1]
    for t in range(tiles):
        for x in range(period):
            total = None
            for o in range(count):
                for c in range(10):
                    if (c - 3 + 4 * o) % period == x:
                        value = shares[o][t, c]
                        total = value if total is None else total + value
            out[t, x] = total


def window_x_kernel(sources, *refs):
    own, inputs, (out, down, up, base, first, second) = refs[0], refs[1:-6], refs[-6:]
    planes, share = base.shape[1], out.shape[0]
    read = {}
    for p in range(planes):
        total = None
        for index, offset in sources:
            c = p - 7 - 8 * offset + 2
            if not 0 <= c < share:
                continue
            if (index, c) not in read:
                if index == 0:
                    read[index, c] = own[c, 2 : 2 + ROWS_SENT]
                else:
                    read[index, c] = plane_sent(inputs[index - 1], share, c)
            value = read[index, c]
            total = value if total is None else total + value
        base[0, p, 0:8] = jnp.zeros((8, LANES), F32)
        base[0, p, 24:32] = jnp.zeros((8, LANES), F32)
        base[0, p, 6 : 6 + ROWS_SENT] = total
    seventh = 1.0 / 7.0
    sweep(first, base, 1, planes - 1, base, seventh)
    sweep(second, first, 2, planes - 2, base, seventh)
    sweep(first, second, 3, planes - 3, base, seventh)
    sweep(second, first, 4, planes - 4, base, seventh)
    share = out.shape[0]
    for c in range(share):
        p = 5 + c
        value = (seven_sum(second, p, p - 1, p + 1)[0] * seventh + base[0, p]) * weight(1)
        out[c] = value
        down[c] = value[1:9]
        up[c] = value[22:30]
        down[share + c // 8, c % 8 : c % 8 + 1] = value[9:10]
        up[share + c // 8, c % 8 : c % 8 + 1] = value[30:31]


def restrict_lanes(values, width, coarse_width, coarse_tiles):
    out = []
    for s in range(coarse_tiles):
        total = None
        for t, value in enumerate(values):
            matrix = one_hot(
                lambda r, c: ((LANES * t + r) // 2 == lax.rem(LANES * s + c, coarse_width))
                & (LANES * t + r < width)
            )
            term = dot_ones(value, matrix)
            total = term if total is None else total + term
        out.append(total)
    return out


def prolong_lanes(values, width, fine_tiles):
    out = []
    for s in range(fine_tiles):
        total = None
        for t, value in enumerate(values):
            matrix = one_hot(lambda r, c: LANES * t + r == lax.rem(LANES * s + c, width) // 2)
            term = dot_ones(value, matrix)
            total = term if total is None else total + term
        out.append(total)
    return out


def real_waves(count):
    cells = np.arange(count)
    rows, eigenvalues = [], []
    for k in range(count // 2 + 1):
        angle = 2.0 * np.pi * k / count
        rows.append(np.cos(angle * cells))
        eigenvalues.append(2.0 * np.cos(angle))
        if 0 < k < count / 2:
            rows.append(np.sin(angle * cells))
            eigenvalues.append(2.0 * np.cos(angle))
    basis = np.stack(rows)
    basis = basis / np.sqrt(np.sum(basis * basis, axis=1, keepdims=True))
    return basis, np.array(eigenvalues)


def last_level_matrices(planes, rows, width):
    wave_x, value_x = real_waves(planes)
    wave_y, value_y = real_waves(rows)
    wave_z, value_z = real_waves(width)
    into = np.kron(wave_x, np.repeat(wave_y, 1, axis=1))
    level_values = value_x[:, None, None] + value_y[None, :, None] + value_z[None, None, :]
    factor = (1.0 + level_values) / 7.0
    total = sum(factor**k for k in range(COARSE_ITERS)) * weight(LEVELS - 1) * 0.125
    scale = np.zeros((planes * rows, LANES))
    scale[:, :width] = total.reshape(planes * rows, width)
    fine = 2 * width
    tiles = max(1, fine // LANES)
    lanes = np.arange(LANES * tiles)
    to_waves = np.zeros((LANES * tiles, LANES))
    to_waves[:fine, :width] = wave_z.T[lanes[:fine] // 2]
    from_waves = np.zeros((LANES, LANES * tiles))
    from_waves[:width] = wave_z[:, (lanes % fine) // 2]
    to_waves = to_waves.reshape(tiles, LANES, LANES)
    from_waves = from_waves.reshape(LANES, tiles, LANES).transpose(1, 0, 2)
    arrays = (into, into.T, to_waves, from_waves, scale)
    return [jnp.asarray(np.ascontiguousarray(a), F32) for a in arrays]


def solve_last(values, into, back, to_waves, from_waves, scale):
    total = None
    for t, value in enumerate(values):
        term = dot(dot(into[...], value), to_waves[t])
        total = term if total is None else total + term
    total = dot(back[...], total * scale[...])
    return [dot(total, from_waves[t]) for t in range(len(values))]


def solve(level, width, buffers, spectral):
    g, a, b = buffers[level]
    tiles, planes, rows = g.shape[0], g.shape[1], g.shape[2]
    seventh = 1.0 / 7.0
    w = weight(level)
    sweep(a, g, 0, planes, None, seventh, planes)
    sweep(b, a, 0, planes, None, seventh, planes)
    for t in range(tiles):
        for p in range(planes):
            g[t, p] = (g[t, p] + a[t, p] + b[t, p]) * w
    sweep(a, b, 0, planes, None, seventh, planes)
    half = rows // 2
    values = []
    for t in range(tiles):
        parts = []
        for c in range(planes // 2):
            total = a[t, 2 * c, pl.ds(0, half, stride=2), :]
            total = total + a[t, 2 * c, pl.ds(1, half, stride=2), :]
            total = total + a[t, 2 * c + 1, pl.ds(0, half, stride=2), :]
            total = total + a[t, 2 * c + 1, pl.ds(1, half, stride=2), :]
            parts.append(total)
        values.append(jnp.concatenate(parts, axis=0))
    if level == LEVELS - 2:
        values = solve_last(values, *spectral)
    else:
        coarse = buffers[level + 1][0]
        values = restrict_lanes(values, width, width // 2, coarse.shape[0])
        for t, value in enumerate(values):
            for c in range(planes // 2):
                coarse[t, c] = value[half * c : half * (c + 1)] * 0.125
        solve(level + 1, width // 2, buffers, spectral)
        values = [
            jnp.concatenate([coarse[t, c] for c in range(planes // 2)], axis=0)
            for t in range(coarse.shape[0])
        ]
        values = prolong_lanes(values, width, tiles)
    for t, value in enumerate(values):
        for c in range(planes // 2):
            part = value[half * c : half * (c + 1)]
            for p in (2 * c, 2 * c + 1):
                b[t, p, pl.ds(0, half, stride=2), :] = part
                b[t, p, pl.ds(1, half, stride=2), :] = part
        for p in range(planes):
            b[t, p] = b[t, p] + g[t, p]
    sweep(a, b, 0, planes, None, seventh, planes)
    sweep(b, a, 0, planes, None, seventh, planes)
    sweep(a, b, 0, planes, None, seventh, planes)
    for t in range(tiles):
        for p in range(planes):
            g[t, p] = g[t, p] + a[t, p]


def coarse_kernel(count, *refs):
    shares, spectral = refs[:count], refs[count : count + 5]
    out, scratch = refs[count + 5], refs[count + 6 :]
    buffers = {level: scratch[3 * (level - 2) : 3 * (level - 1)] for level in (2, 3)}
    g = buffers[2][0]
    tiles, planes = g.shape[0], g.shape[1]
    for t in range(tiles):
        for p in range(planes):
            for b in range(count):
                value = shares[b][t, p, 0:8] + shares[(b - 1) % count][t, p, 8:16]
                g[t, p, 8 * b : 8 * b + 8] = value
    solve(2, LANES * tiles, buffers, spectral)
    for c in range(out.shape[0]):
        out[c] = g[0, (c - 3) % planes, 0:16]


def correct_kernel(e2, f1_own, f1_above, f1_below, u0_b, u1_a, u1_b, f1, u0_a):
    share1 = f1_own.shape[0]
    for c in range(share1):
        f1[c] = f1_own[c]
        f1[c, 17:25] = f1[c, 17:25] + f1_above[c]
        f1[c, 6:14] = f1[c, 6:14] + f1_below[c]
        ninth, k = share1 + c // 8, c % 8
        f1[c, 25:26] = f1[c, 25:26] + f1_above[ninth, k : k + 1]
        f1[c, 14:15] = f1[c, 14:15] + f1_below[ninth, k : k + 1]
    share2 = e2.shape[0]
    rows2 = e2.shape[1]
    value = e2[...].reshape(share2 * rows2, LANES)
    value = dot_ones(value, one_hot(lambda r, c: r == c // 2))
    for c in range(share2):
        part = value[rows2 * c : rows2 * (c + 1)]
        for p in (2 * c, 2 * c + 1):
            u1_a[0, p, pl.ds(0, rows2, stride=2), :] = part
            u1_a[0, p, pl.ds(1, rows2, stride=2), :] = part
    count1 = 2 * share2
    sweep(u1_b, u1_a, 1, count1 - 1)
    sweep(u1_a, u1_b, 2, count1 - 2)
    sweep(u1_b, u1_a, 3, count1 - 3)
    rows1 = 24
    parts = []
    for c in range(share1):
        parts.append(f1[c, 4 : 4 + rows1] + u1_b[0, 4 + c, 4 : 4 + rows1] * (1.0 / 343.0))
    value = jnp.concatenate(parts, axis=0)
    main = dot_ones(value, one_hot(lambda r, c: r == 32 + c // 2))
    side = dot_ones(value, one_hot(lambda r, c: r == jnp.where(c < 64, 96 + c // 2, c // 2 - 32)))
    for t, value in enumerate((main, side)):
        for c in range(share1):
            part = value[rows1 * c : rows1 * (c + 1)]
            for p in (2 * c, 2 * c + 1):
                u0_a[t, p, pl.ds(0, rows1, stride=2), :] = part
                u0_a[t, p, pl.ds(1, rows1, stride=2), :] = part
    count0 = 2 * share1
    sweep(u0_b, u0_a, 1, count0 - 1)
    sweep(u0_a, u0_b, 2, count0 - 2)
    sweep(u0_b, u0_a, 3, count0 - 3)


def finish_kernel(field, u0_b, f0, beyond, out, pot):
    planes, rows = field.shape[1], field.shape[2]
    scale = 1.0 / 343.0
    for i in range(planes + 1):
        pot[i, 0:rows] = u0_b[0, 4 + i, ROW0 : ROW0 + rows] * scale + f0[i, 0:rows]
        if i < planes:
            edge = u0_b[0, 4 + i, ROW0 + rows : ROW0 + rows + 1] * scale
            pot[i, rows : rows + 1] = edge + f0[i, rows : rows + 1]
    lane = iota((rows, LANES), 1)
    for i in range(planes):
        here = pot[i, 0:rows]
        out[0, i] = field[0, i] - (pot[i + 1, 0:rows] - here)
        out[1, i] = field[1, i] - (pot[i, 1 : rows + 1] - here)
        last = pltpu.roll(u0_b[1, 4 + i, ROW0 : ROW0 + rows], LANES - 1, 1) * scale + beyond[i]
        next_z = jnp.where(lane == LANES - 1, last, pltpu.roll(here, LANES - 1, 1))
        out[2, i] = field[2, i] - (next_z - here)


def fine_place(p, share):
    if p <= SPILL:
        return p
    return p - share + 13 if p >= share - 6 else p + 7


def fine_own_kernel(zeroth, first, second, third, field, after, main, down, up, field_out, fourth):
    share = main.shape[0]
    field_out[...] = field[...]
    low, high = PLANE0, zeroth.shape[1] - 6
    sweep(fourth, third, low - 4, high + 4)
    clear_margin(fourth, low - 4, high + 4)
    powers = (zeroth, first, second, third, fourth)
    for k in range(share):
        p = low - SPILL + k
        total = seven_sum(fourth, p, p - 1, p + 1, 1)[0] * (weight(0) / 7.0**5)
        for n, power in enumerate(powers):
            if low - n <= p < high + n:
                total = total + power[0, p] * (weight(0) / 7.0**n)
        main[k] = total
        down[k] = total[1:9]
        up[k] = total[40:48]


EDGE = 64
BEYOND = 96


def fine_edge_kernel(start, *refs):
    strips, (out, down, up, base, first, second) = refs[:3], refs[3:]
    share, rows = out.shape[0], out.shape[1]
    planes = share - 1
    inner = rows - ROW0
    lane = iota((inner, LANES), 1)
    sources = [
        [r[start + inner * k : start + inner * (k + 1)] for k in range(3)] for r in strips
    ]
    for k in range(base.shape[1]):
        value = jnp.zeros((inner, LANES), F32)
        for d, offset in ((0, 0), (1, -planes), (2, planes)):
            i = k - SPILL - offset
            if not 0 <= i <= planes:
                continue
            below, above, own = sources[d]
            turned = pltpu.roll(below, (LANES - SPILL - 7 * i) % LANES, 1)
            value = value + jnp.where((lane >= LANES - SPILL) | (lane == 0), turned, 0.0)
            turned = pltpu.roll(above, (EDGE - 7 * i) % LANES, 1)
            value = value + jnp.where((lane >= EDGE) & (lane <= EDGE + SPILL), turned, 0.0)
            turned = pltpu.roll(above, (BEYOND - 7 * i) % LANES, 1)
            value = value + jnp.where((lane >= BEYOND) & (lane <= BEYOND + SPILL), turned, 0.0)
            turned = pltpu.roll(own, (BEYOND - SPILL - 7 * i) % LANES, 1)
            value = value + jnp.where((lane >= BEYOND - SPILL) & (lane <= BEYOND), turned, 0.0)
        base[0, k, 0:ROW0] = jnp.zeros((ROW0, LANES), F32)
        base[0, k, ROW0:] = value
    seventh = 1.0 / 7.0
    high = base.shape[1]
    sweep(first, base, 1, high - 1, base, seventh)
    sweep(second, first, 2, high - 2, base, seventh)
    sweep(first, second, 3, high - 3, base, seventh)
    sweep(second, first, 4, high - 4, base, seventh)
    for i in range(share):
        p = SPILL + i
        value = (seven_sum(second, p, p - 1, p + 1)[0] * seventh + base[0, p]) * weight(0)
        out[i] = value
        down[i] = value[1:9]
        up[i] = value[40:48]


def fine_sum_kernel(f0, below_x, above_x, edge, above, below, out, beyond, work):
    planes, rows = beyond.shape[0], beyond.shape[1]
    lane = iota((rows, LANES), 1)
    lane1 = iota((1, LANES), 1)
    work[:, 0:rows] = edge[:, ROW0 : ROW0 + rows]
    work[:, rows : rows + 8] = edge[:, ROW0 + rows : ROW0 + rows + 8]
    for i in range(planes + 1):
        work[i, 25:33] = work[i, 25:33] + above[i]
        work[i, 0:8] = work[i, 0:8] + below[i]
    for i in range(planes + 1):
        value = f0[fine_place(i + SPILL, planes + 11)]
        if i <= SPILL:
            value = value + below_x[1 + i]
        if i >= planes - SPILL:
            value = value + above_x[i - (planes - SPILL)]
        part = work[i, 0:rows]
        turned = pltpu.roll(part, EDGE, 1)
        value = value + jnp.where(lane <= SPILL, part, 0.0)
        out[i, 0:rows] = value + jnp.where(lane >= LANES - SPILL, turned, 0.0)
        if i < planes:
            beyond[i] = pltpu.roll(part, LANES - 1 - BEYOND, 1)
            row = f0[6, i + SPILL : i + SPILL + 1]
            if i <= SPILL:
                row = row + below_x[0, i + SPILL + planes : i + SPILL + planes + 1]
            if i >= planes - SPILL:
                row = row + above_x[6, i + SPILL - planes : i + SPILL - planes + 1]
            part = work[i, rows : rows + 1]
            row = row + jnp.where(lane1 <= SPILL, part, 0.0)
            row = row + jnp.where(lane1 >= LANES - SPILL, pltpu.roll(part, EDGE, 1), 0.0)
            out[i, rows : rows + 1] = row


def fine_y_kernel(main, above, below, out, work):
    share = main.shape[0]
    rows = out.shape[1]
    out[6] = jnp.zeros((rows, LANES), F32)
    for p in range(share):
        work[p] = main[p]
        work[p, 33:41] = work[p, 33:41] + above[p]
        work[p, 8:16] = work[p, 8:16] + below[p]
        out[fine_place(p, share)] = work[p, ROW0 : ROW0 + rows]
        out[6, p : p + 1] = work[p, ROW0 + rows : ROW0 + rows + 1]


EARLIER = {1: (), -1: (1,), 2: (1, -1), -2: (1, -1, 2)}


def body(field):
    nx, ny, nz = field.shape[1:]
    size_x, size_y, size_z = lax.axis_size("gx"), lax.axis_size("gy"), lax.axis_size("gz")
    n1 = nx // 2
    share1 = n1 + 4
    rows0 = ny + 16
    rows1 = ny // 2 + 8
    planes0 = nx + 13

    def from_offset(value, axis, offset):
        count = lax.axis_size(axis)
        pairs = [(source, (source - offset) % count) for source in range(count)]
        return lax.ppermute(value, axis, pairs)

    level0 = (2, planes0, rows0, LANES)
    level1 = (1, n1 + 12, ny // 2 + 16, LANES)
    packed = ((n1 // 2 + 6) // 2) * 16
    near = packed + rows1 + rows0 - ROW0
    up, down, far, g1, *powers = call(
        spread_kernel,
        [shape(near, LANES), shape(near, LANES), shape(packed, LANES),
         shape(share1, rows1, LANES)] + [shape(*level0)] * 4,
        [level1, level1],
        2.9,
        field,
    )
    received = []
    for o in range(1, size_z):
        message = down if o == 1 else (up if o == size_z - 1 else far)
        received.append(from_offset(message, "gz", o))
    share0 = nx + 11
    main, f_down, f_up, kept = call(
        fine_own_kernel,
        [shape(share0, rows0, LANES), shape(share0, 8, LANES), shape(share0, 8, LANES),
         shape(*field.shape)],
        [level0],
        3.0,
        *powers, field, received[size_z // 2 - 1],
    )
    f_above = from_offset(f_down, "gy", 1)
    f_below = from_offset(f_up, "gy", -1)

    tiles = size_z * 32 // LANES
    inner0 = rows0 - ROW0
    sent1 = ROWS_SENT * (share1 // 2 - (-share1 // 8))
    g2, g1, message = call(
        functools.partial(gather_z_kernel, size_z),
        [shape(tiles, n1 // 2 + 6, 16, LANES), shape(share1, rows1, LANES),
         shape(sent1 + 3 * inner0, LANES)],
        [],
        0.2,
        far, g1, up, *received,
    )
    shares = [g2] + [from_offset(g2, "gx", o) for o in range(1, size_x)]
    messages = {o: from_offset(message, "gx", o) for o in sorted({1, -1, 2, -2}, key=abs)
                if o % size_x and not any(o % size_x == q % size_x for q in EARLIER[o])}
    keys = [0] + list(messages)
    sources = []
    for o in (0, 1, -1, 2, -2):
        index = [k for k, key in enumerate(keys) if key % size_x == o % size_x][0]
        sources.append((index, o))
    g2 = call(
        functools.partial(fold_x_kernel, size_x),
        shape(tiles, 4 * size_x, 16, LANES),
        [],
        0.05,
        *shares,
    )
    window = (1, n1 + 14, ny // 2 + 16, LANES)
    edge1 = share1 + -(-share1 // 8)
    f1, f1_down, f1_up = call(
        functools.partial(window_x_kernel, tuple(sources)),
        [shape(share1, ny // 2 + 16, LANES), shape(edge1, 8, LANES), shape(edge1, 8, LANES)],
        [window, window, window],
        1.0,
        g1, *messages.values(),
    )
    shares = [g2] + [from_offset(g2, "gy", o) for o in range(1, size_y)]
    f1_above = from_offset(f1_down, "gy", 1)
    f1_below = from_offset(f1_up, "gy", -1)

    f0 = call(
        fine_y_kernel,
        shape(share0 + 1, ny, LANES),
        [(share0, rows0, LANES)],
        0.4,
        main, f_above, f_below,
    )
    if size_x == 2:
        other = from_offset(f0[0:13], "gx", 1)
        f_above, f_below = other[0:7], other[6:13]
    else:
        f_above = from_offset(f0[0:7], "gx", 1)
        f_below = from_offset(f0[6:13], "gx", -1)
    edges = (1, nx + 11, rows0, LANES)
    edge, e_down, e_up = call(
        functools.partial(fine_edge_kernel, sent1),
        [shape(nx + 1, rows0, LANES), shape(nx + 1, 8, LANES), shape(nx + 1, 8, LANES)],
        [edges, edges, edges],
        2.0,
        message, messages[-1 if -1 in messages else 1], messages[1],
    )
    e_above = from_offset(e_down, "gy", 1)
    e_below = from_offset(e_up, "gy", -1)
    f0, beyond = call(
        fine_sum_kernel,
        [shape(nx + 1, ny + 8, LANES), shape(nx, ny, LANES)],
        [(nx + 1, ny + 8, LANES)],
        0.4,
        f0, f_below, f_above, edge, e_above, e_below,
    )

    scratch = []
    for level in (2, 3):
        cut = 2 ** (level - 2)
        extent = (max(1, tiles // cut), 4 * size_x // cut, 8 * size_y // cut, LANES)
        scratch.extend([extent] * 3)
    e2 = call(
        functools.partial(coarse_kernel, size_y),
        shape(n1 // 2 + 6, 16, LANES),
        scratch,
        2.2,
        *shares, *last_level_matrices(size_x, 2 * size_y, 8 * size_z),
    )
    fine = (2, nx + 8, rows0, LANES)
    correction = call(
        correct_kernel,
        shape(*fine),
        [level1, level1, (share1, ny // 2 + 16, LANES), fine],
        2.6,
        e2, f1, f1_above, f1_below,
    )
    return call(
        finish_kernel,
        shape(*field.shape),
        [(nx + 1, ny + 8, LANES)],
        0.9,
        kept, correction, f0, beyond,
    )


def solution(mesh):
    in_specs = (P(None, "gx", "gy", "gz"),)
    out_specs = P(None, "gx", "gy", "gz")
    return jax.shard_map(body, mesh=mesh, in_specs=in_specs, out_specs=out_specs, check_vma=False)
```

time: 44.1 us -> 38.3 us (0.87)
  Pallas kernels: 18 us -> 13.6 us
  starting transfers between devices: 16.6 us -> 15.7 us
  waiting for transfers between devices: 7.71 us -> 7.12 us
    pallas_call x10 -> x11, Pallas kernels: 18 us -> 13.6 us  [call(): pl.pallas_call(kernel, out_shape=outs, scratch_shapes=[pltpu.VMEM(s, F32)...]
    ppermute x15, starting transfers between devices: 16.6 us -> 15.7 us  [from_offset(): return lax.ppermute(value, axis, pairs)]
    ppermute x15, waiting for transfers between devices: 7.71 us -> 7.12 us  [from_offset(): return lax.ppermute(value, axis, pairs)]
    unnamed x4 -> x12, local copies, waits for them, and re-layouts: 1.37 us -> 1.17 us
  transfers between devices with their start and end apart: 15 -> 15, of which waited for: 6 -> 3; matrix products, arithmetic and copies ran while one was open for 0% -> 0% of each run, Pallas kernels for 13% -> 25%
where the time goes in v4:
time: 38.3 us; the launch traced here: 37.8 us
  starting transfers between devices  15.7 us (41%)
  Pallas kernels  13.6 us (36%)
  waiting for transfers between devices  7.12 us (19%)
  local copies, waits for them, and re-layouts  1.2 us (3%)
    ppermute x15, starting transfers between devices, from_offset(): return lax.ppermute(value, axis, pairs)  15.7 us
    pallas_call x11, Pallas kernels, call(): pl.pallas_call(kernel, out_shape=outs, scratch_shapes=[pltpu.VMEM(s, F32)...  13.6 us
    ppermute x15, waiting for transfers between devices, from_offset(): return lax.ppermute(value, axis, pairs)  7.12 us
    unnamed x12, local copies, waits for them, and re-layouts  1.17 us
  transfers between devices with their start and end apart: 15, of which 3 were waited for; matrix products, arithmetic and copies ran while one was open for 0% of the time, Pallas kernels for 25%

profile of v4, /device:TPU:0, one launch (start us, length us, event | category | flops | bytes accessed | tf_op | source)
XLA Modules:
  0.0 37.8 jit_solution(1630345779423887138)
XLA Ops:
  0.0 1.1 %copy-done = f32[3,16,32,128]{3,2,1,0:T(8,128)S(1)} copy-done((f32[3,16,32,128]{3,2,1,0:T(8,128)S(1)}, f32[3,16,32,128]{3,2,1,0:T(8,128)}, u32[]{:S(2)}) %copy-start) | copy-done | bytes 786456
  1.1 2.7 %shard_map.64 = (f32[144,128]{1,0:T(8,128)S(1)}, f32[144,128]{1,0:T(8,128)S(1)}, f32[80,128]{1,0:T(8,128)S(1)}, f32[12,24,128]{2,1,0:T(8,128)S(1)}, f32[2,29,48,...) custom-call(f32[3,16,32,128]{3,2,1,0:T(8,128)S(1)} %copy-done), custom_call_target="tpu_custom_call" | custom-call | flops 3335000064 | tf_op jit(solution)/shard_map/pallas_call | solution.py:32
  3.8 4.1 %collective-permute-start = (f32[80,128]{1,0:T(8,128)S(1)}, f32[80,128]{1,0:T(8,128)S(1)}, u32[]{:S(2)}, u32[]{:S(2)}) collective-permute-start(f32[80,128]{1,0:T(8,128)S(1)} %get-tuple-element.32.refs_0_), channel_id=1, source_target_pairs={{0,2},{1,3},{2,0},{3,1},{4,6},{5,7},{6,4},{7,5},{8,10},{9,11},{10,... | collective-permute-start | bytes 122888 | tf_op jit(solution)/shard_map/ppermute | solution.py:686
  7.9 1.3 %collective-permute-start.1 = (f32[144,128]{1,0:T(8,128)S(1)}, f32[144,128]{1,0:T(8,128)S(1)}, u32[]{:S(2)}, u32[]{:S(2)}) collective-permute-start(f32[144,128]{1,0:T(8,128)S(1)} %get-tuple-element.36), channel_id=1, source_target_pairs={{0,3},{1,0},{2,1},{3,2},{4,7},{5,4},{6,5},{7,6},{8,11},{9,8},{10,9... | collective-permute-start | bytes 221192 | tf_op jit(solution)/shard_map/ppermute | solution.py:686
  9.3 0.7 %collective-permute-start.2 = (f32[144,128]{1,0:T(8,128)S(1)}, f32[144,128]{1,0:T(8,128)S(1)}, u32[]{:S(2)}, u32[]{:S(2)}) collective-permute-start(f32[144,128]{1,0:T(8,128)S(1)} %get-tuple-element.35.refs_2_), channel_id=1, source_target_pairs={{0,1},{1,2},{2,3},{3,0},{4,5},{5,6},{6,7},{7,4},{8,9},{9,10},{10,1... | collective-permute-start | bytes 221192 | tf_op jit(solution)/shard_map/ppermute | solution.py:686
  9.9 0.5 %collective-permute-done.after.refs_4_ = f32[80,128]{1,0:T(8,128)S(1)} collective-permute-done((f32[80,128]{1,0:T(8,128)S(1)}, f32[80,128]{1,0:T(8,128)S(1)}, u32[]{:S(2)}, u32[]{:S(2)}) %collective-permute-start) | collective-permute-done | bytes 40992 | tf_op jit(solution)/shard_map/ppermute | solution.py:686
  10.4 1.6 %shard_map.65 = (f32[27,48,128]{2,1,0:T(8,128)S(1)}, f32[27,8,128]{2,1,0:T(8,128)S(1)}, f32[27,8,128]{2,1,0:T(8,128)S(1)}, f32[3,16,32,128]{3,2,1,0:T(8,128)S(1)}) custom-call(f32[2,29,48,128]{3,2,1,0:T(8,128)S(1)} %get-tuple-element.28.zeroth, f32[2,29,48,128]{3,2,1,0:T(8,128)S(1)} %get-tuple-element.29.first, ...), custom_call_target="tpu_custom_call" | custom-call | flops 3449999872 | tf_op jit(solution)/shard_map/pallas_call | solution.py:32
  12.1 0.5 %collective-permute-start.11 = (f32[27,8,128]{2,1,0:T(8,128)S(1)}, f32[27,8,128]{2,1,0:T(8,128)S(1)}, u32[]{:S(2)}, u32[]{:S(2)}) collective-permute-start(f32[27,8,128]{2,1,0:T(8,128)S(1)} %get-tuple-element.45), channel_id=1, source_target_pairs={{0,4},{4,8},{8,12},{12,0},{1,5},{5,9},{9,13},{13,1},{2,6},{6,10},{... | collective-permute-start | bytes 331784 | tf_op jit(solution)/shard_map/ppermute | solution.py:686
  12.6 2.8 %collective-permute-done.2.refs_5_ = f32[144,128]{1,0:T(8,128)S(1)} collective-permute-done((f32[144,128]{1,0:T(8,128)S(1)}, f32[144,128]{1,0:T(8,128)S(1)}, u32[]{:S(2)}, u32[]{:S(2)}) %collective-permute-start.2) | collective-permute-done | bytes 73760 | tf_op jit(solution)/shard_map/ppermute | solution.py:686
  15.4 0.4 shard_map.66
  15.8 1.6 %collective-permute-start.7 = (f32[280,128]{1,0:T(8,128)S(1)}, f32[280,128]{1,0:T(8,128)S(1)}, u32[]{:S(2)}, u32[]{:S(2)}) collective-permute-start(f32[280,128]{1,0:T(8,128)S(1)} %get-tuple-element.39.refs_0_), channel_id=1, source_target_pairs={{0,16},{16,0},{1,17},{17,1},{2,18},{18,2},{3,19},{19,3},{4,20},{20... | collective-permute-start | bytes 430088 | tf_op jit(solution)/shard_map/ppermute | solution.py:686
  17.4 0.5 %collective-permute-start.3 = (f32[1,10,16,128]{3,2,1,0:T(8,128)S(1)}, f32[1,10,16,128]{3,2,1,0:T(8,128)S(1)}, u32[]{:S(2)}, u32[]{:S(2)}) collective-permute-start(f32[1,10,16,128]{3,2,1,0:T(8,128)S(1)} %get-tuple-element.37.refs_0_), channel_id=1, source_target_pairs={{0,16},{16,0},{1,17},{17,1},{2,18},{18,2},{3,19},{19,3},{4,20},{20... | collective-permute-start | bytes 245768 | tf_op jit(solution)/shard_map/ppermute | solution.py:686
  18.0 1.6 %collective-permute-start.12 = (f32[13,32,128]{2,1,0:T(8,128)S(1)}, f32[13,32,128]{2,1,0:T(8,128)S(1)}, u32[]{:S(2)}, u32[]{:S(2)}) collective-permute-start(f32[13,32,128]{2,1,0:T(8,128)S(1)} %slice.12), channel_id=1, source_target_pairs={{0,16},{16,0},{1,17},{17,1},{2,18},{18,2},{3,19},{19,3},{4,20},{20... | collective-permute-start | bytes 638984 | tf_op jit(solution)/shard_map/ppermute | solution.py:686
  19.6 3.7 %collective-permute-done.3.refs_1_ = f32[1,10,16,128]{3,2,1,0:T(8,128)S(1)} collective-permute-done((f32[1,10,16,128]{3,2,1,0:T(8,128)S(1)}, f32[1,10,16,128]{3,2,1,0:T(8,128)S(1)}, u32[]{:S(2)}, u32[]{:S(2)}) %collective-permute-start.3) | collective-permute-done | bytes 81952 | tf_op jit(solution)/shard_map/ppermute | solution.py:686
  23.4 2.0 %collective-permute-start.5 = (f32[1,8,16,128]{3,2,1,0:T(8,128)S(1)}, f32[1,8,16,128]{3,2,1,0:T(8,128)S(1)}, u32[]{:S(2)}, u32[]{:S(2)}) collective-permute-start(f32[1,8,16,128]{3,2,1,0:T(8,128)S(1)} %shard_map.67.refs_0_), channel_id=1, source_target_pairs={{0,8},{4,12},{8,0},{12,4},{1,9},{5,13},{9,1},{13,5},{2,10},{6,14},... | collective-permute-start | bytes 196616 | tf_op jit(solution)/shard_map/ppermute | solution.py:686
  25.4 1.4 %collective-permute-start.4 = (f32[1,8,16,128]{3,2,1,0:T(8,128)S(1)}, f32[1,8,16,128]{3,2,1,0:T(8,128)S(1)}, u32[]{:S(2)}, u32[]{:S(2)}) collective-permute-start(f32[1,8,16,128]{3,2,1,0:T(8,128)S(1)} %shard_map.67.refs_0_), channel_id=1, source_target_pairs={{0,12},{4,0},{8,4},{12,8},{1,13},{5,1},{9,5},{13,9},{2,14},{6,2},{... | collective-permute-start | bytes 196616 | tf_op jit(solution)/shard_map/ppermute | solution.py:686
  26.8 0.9 %shard_map.69 = (f32[12,32,128]{2,1,0:T(8,128)S(1)}, f32[14,8,128]{2,1,0:T(8,128)S(1)}, f32[14,8,128]{2,1,0:T(8,128)S(1)}) custom-call(f32[12,24,128]{2,1,0:T(8,128)S(1)} %get-tuple-element.38.refs_0_, f32[280,128]{1,0:T(8,128)S(1)} %collective-permute-done.7.refs_1_.refs_2_), custom_call_target="tpu_custom_call" | custom-call | flops 1150000000 | tf_op jit(solution)/shard_map/pallas_call | solution.py:32
  27.8 2.0 %shard_map.72 = (f32[17,48,128]{2,1,0:T(8,128)S(1)}, f32[17,8,128]{2,1,0:T(8,128)S(1)}, f32[17,8,128]{2,1,0:T(8,128)S(1)}) custom-call(f32[280,128]{1,0:T(8,128)S(1)} %get-tuple-element.39.refs_0_, f32[280,128]{1,0:T(8,128)S(1)} %collective-permute-done.7.refs_1_.refs_2_, f32[280,128]{1,0:T(8,128)S(1)} %collective-permute-done.7.refs_1_.refs_2_), custom_call_target="tpu_custom_call" | custom-call | flops 2300000000 | tf_op jit(solution)/shard_map/pallas_call | solution.py:32
  29.9 0.5 %collective-permute-start.9 = (f32[14,8,128]{2,1,0:T(8,128)S(1)}, f32[14,8,128]{2,1,0:T(8,128)S(1)}, u32[]{:S(2)}, u32[]{:S(2)}) collective-permute-start(f32[14,8,128]{2,1,0:T(8,128)S(1)} %get-tuple-element.42), channel_id=1, source_target_pairs={{0,4},{4,8},{8,12},{12,0},{1,5},{5,9},{9,13},{13,1},{2,6},{6,10},{... | collective-permute-start | bytes 172040 | tf_op jit(solution)/shard_map/ppermute | solution.py:686
  30.4 1.3 %collective-permute-start.13 = (f32[17,8,128]{2,1,0:T(8,128)S(1)}, f32[17,8,128]{2,1,0:T(8,128)S(1)}, u32[]{:S(2)}, u32[]{:S(2)}) collective-permute-start(f32[17,8,128]{2,1,0:T(8,128)S(1)} %get-tuple-element.47), channel_id=1, source_target_pairs={{0,12},{4,0},{8,4},{12,8},{1,13},{5,1},{9,5},{13,9},{2,14},{6,2},{... | collective-permute-start | bytes 208904 | tf_op jit(solution)/shard_map/ppermute | solution.py:686
  31.7 2.1 %shard_map.68.e2 = f32[10,16,128]{2,1,0:T(8,128)S(1)} custom-call(f32[1,8,16,128]{3,2,1,0:T(8,128)S(1)} %shard_map.67.refs_0_, f32[1,8,16,128]{3,2,1,0:T(8,128)S(1)} %collective-permute-done.4.refs_1_, f32[1,8,16,128]{3,2,1,0:T(8,128)S(1)} %collective-permute-done.5.refs_2_, f32[1,8,16,128]{3,2,1,0:T(8,128)S(1)} %collective-permute-done.6.refs_3_, ...), custom_call_target="tpu_custom_call" | custom-call | flops 2529999872 | tf_op jit(solution)/shard_map/pallas_call | solution.py:32
  33.8 2.5 %shard_map.70.u0_b = f32[2,24,48,128]{3,2,1,0:T(8,128)S(1)} custom-call(f32[10,16,128]{2,1,0:T(8,128)S(1)} %shard_map.68.e2, f32[12,32,128]{2,1,0:T(8,128)S(1)} %get-tuple-element.40.f1_own, f32[14,8,128]{2,1,0:T(8,128)S(1)} %collective-permute-done.8.f1_above, f32[14,8,128]{2,1,0:T(8,128)S(1)} %collective-permute-done.9.f1_below), custom_call_target="tpu_custom_call" | custom-call | flops 2990000128 | tf_op jit(solution)/shard_map/pallas_call | solution.py:32
  36.4 0.2 shard_map.73
  36.6 1.1 %shard_map.74 = f32[3,16,32,128]{3,2,1,0:T(8,128)} custom-call(f32[3,16,32,128]{3,2,1,0:T(8,128)S(1)} %get-tuple-element.33.field, f32[2,24,48,128]{3,2,1,0:T(8,128)S(1)} %shard_map.70.u0_b, f32[17,40,128]{2,1,0:T(8,128)S(1)} %get-tuple-element.49.f0, f32[16,32,128]{2,1,0:T(8,128)S(1)} %get-tuple-element.50.beyond), custom_call_target="tpu_custom_call" | custom-call | flops 1035000000 | tf_op jit(solution)/shard_map/pallas_call | solution.py:32
  (31 shorter events, 0.4 us)
Async XLA Ops:
  0.0 1.1 %copy-start = (f32[3,16,32,128]{3,2,1,0:T(8,128)S(1)}, f32[3,16,32,128]{3,2,1,0:T(8,128)}, u32[]{:S(2)}) copy-start(f32[3,16,32,128]{3,2,1,0:T(8,128)} %field.3) | copy-start | bytes 2359300
  3.8 6.6 %collective-permute-start = (f32[80,128]{1,0:T(8,128)S(1)}, f32[80,128]{1,0:T(8,128)S(1)}, u32[]{:S(2)}, u32[]{:S(2)}) collective-permute-start(f32[80,128]{1,0:T(8,128)S(1)} %get-tuple-element.32.refs_0_), channel_id=1, source_target_pairs={{0,2},{1,3},{2,0},{3,1},{4,6},{5,7},{6,4},{7,5},{8,10},{9,11},{10,... | collective-permute-start | bytes 122888 | tf_op jit(solution)/shard_map/ppermute | solution.py:686
  7.9 4.7 %collective-permute-start.1 = (f32[144,128]{1,0:T(8,128)S(1)}, f32[144,128]{1,0:T(8,128)S(1)}, u32[]{:S(2)}, u32[]{:S(2)}) collective-permute-start(f32[144,128]{1,0:T(8,128)S(1)} %get-tuple-element.36), channel_id=1, source_target_pairs={{0,3},{1,0},{2,1},{3,2},{4,7},{5,4},{6,5},{7,6},{8,11},{9,8},{10,9... | collective-permute-start | bytes 221192 | tf_op jit(solution)/shard_map/ppermute | solution.py:686
  9.3 6.2 %collective-permute-start.2 = (f32[144,128]{1,0:T(8,128)S(1)}, f32[144,128]{1,0:T(8,128)S(1)}, u32[]{:S(2)}, u32[]{:S(2)}) collective-permute-start(f32[144,128]{1,0:T(8,128)S(1)} %get-tuple-element.35.refs_2_), channel_id=1, source_target_pairs={{0,1},{1,2},{2,3},{3,0},{4,5},{5,6},{6,7},{7,4},{8,9},{9,10},{10,1... | collective-permute-start | bytes 221192 | tf_op jit(solution)/shard_map/ppermute | solution.py:686
  12.0 5.9 %collective-permute-start.10 = (f32[27,8,128]{2,1,0:T(8,128)S(1)}, f32[27,8,128]{2,1,0:T(8,128)S(1)}, u32[]{:S(2)}, u32[]{:S(2)}) collective-permute-start(f32[27,8,128]{2,1,0:T(8,128)S(1)} %get-tuple-element.44), channel_id=1, source_target_pairs={{0,12},{4,0},{8,4},{12,8},{1,13},{5,1},{9,5},{13,9},{2,14},{6,2},{... | collective-permute-start | bytes 331784 | tf_op jit(solution)/shard_map/ppermute | solution.py:686
  12.1 5.8 %collective-permute-start.11 = (f32[27,8,128]{2,1,0:T(8,128)S(1)}, f32[27,8,128]{2,1,0:T(8,128)S(1)}, u32[]{:S(2)}, u32[]{:S(2)}) collective-permute-start(f32[27,8,128]{2,1,0:T(8,128)S(1)} %get-tuple-element.45), channel_id=1, source_target_pairs={{0,4},{4,8},{8,12},{12,0},{1,5},{5,9},{9,13},{13,1},{2,6},{6,10},{... | collective-permute-start | bytes 331784 | tf_op jit(solution)/shard_map/ppermute | solution.py:686
  15.8 11.0 %collective-permute-start.7 = (f32[280,128]{1,0:T(8,128)S(1)}, f32[280,128]{1,0:T(8,128)S(1)}, u32[]{:S(2)}, u32[]{:S(2)}) collective-permute-start(f32[280,128]{1,0:T(8,128)S(1)} %get-tuple-element.39.refs_0_), channel_id=1, source_target_pairs={{0,16},{16,0},{1,17},{17,1},{2,18},{18,2},{3,19},{19,3},{4,20},{20... | collective-permute-start | bytes 430088 | tf_op jit(solution)/shard_map/ppermute | solution.py:686
  17.4 6.0 %collective-permute-start.3 = (f32[1,10,16,128]{3,2,1,0:T(8,128)S(1)}, f32[1,10,16,128]{3,2,1,0:T(8,128)S(1)}, u32[]{:S(2)}, u32[]{:S(2)}) collective-permute-start(f32[1,10,16,128]{3,2,1,0:T(8,128)S(1)} %get-tuple-element.37.refs_0_), channel_id=1, source_target_pairs={{0,16},{16,0},{1,17},{17,1},{2,18},{18,2},{3,19},{19,3},{4,20},{20... | collective-permute-start | bytes 245768 | tf_op jit(solution)/shard_map/ppermute | solution.py:686
  18.0 18.3 %collective-permute-start.12 = (f32[13,32,128]{2,1,0:T(8,128)S(1)}, f32[13,32,128]{2,1,0:T(8,128)S(1)}, u32[]{:S(2)}, u32[]{:S(2)}) collective-permute-start(f32[13,32,128]{2,1,0:T(8,128)S(1)} %slice.12), channel_id=1, source_target_pairs={{0,16},{16,0},{1,17},{17,1},{2,18},{18,2},{3,19},{19,3},{4,20},{20... | collective-permute-start | bytes 638984 | tf_op jit(solution)/shard_map/ppermute | solution.py:686
  23.4 6.5 %collective-permute-start.6 = (f32[1,8,16,128]{3,2,1,0:T(8,128)S(1)}, f32[1,8,16,128]{3,2,1,0:T(8,128)S(1)}, u32[]{:S(2)}, u32[]{:S(2)}) collective-permute-start(f32[1,8,16,128]{3,2,1,0:T(8,128)S(1)} %shard_map.67.refs_0_), channel_id=1, source_target_pairs={{0,4},{4,8},{8,12},{12,0},{1,5},{5,9},{9,13},{13,1},{2,6},{6,10},{... | collective-permute-start | bytes 196616 | tf_op jit(solution)/shard_map/ppermute | solution.py:686
  23.4 7.0 %collective-permute-start.5 = (f32[1,8,16,128]{3,2,1,0:T(8,128)S(1)}, f32[1,8,16,128]{3,2,1,0:T(8,128)S(1)}, u32[]{:S(2)}, u32[]{:S(2)}) collective-permute-start(f32[1,8,16,128]{3,2,1,0:T(8,128)S(1)} %shard_map.67.refs_0_), channel_id=1, source_target_pairs={{0,8},{4,12},{8,0},{12,4},{1,9},{5,13},{9,1},{13,5},{2,10},{6,14},... | collective-permute-start | bytes 196616 | tf_op jit(solution)/shard_map/ppermute | solution.py:686
  25.4 6.2 %collective-permute-start.4 = (f32[1,8,16,128]{3,2,1,0:T(8,128)S(1)}, f32[1,8,16,128]{3,2,1,0:T(8,128)S(1)}, u32[]{:S(2)}, u32[]{:S(2)}) collective-permute-start(f32[1,8,16,128]{3,2,1,0:T(8,128)S(1)} %shard_map.67.refs_0_), channel_id=1, source_target_pairs={{0,12},{4,0},{8,4},{12,8},{1,13},{5,1},{9,5},{13,9},{2,14},{6,2},{... | collective-permute-start | bytes 196616 | tf_op jit(solution)/shard_map/ppermute | solution.py:686
  27.7 4.0 %copy-start.1 = (f32[1,128,128]{2,1,0:T(8,128)S(1)}, f32[1,128,128]{2,1,0:T(8,128)}, u32[]{:S(2)}) copy-start(f32[1,128,128]{2,1,0:T(8,128)} %constant.13.clone.refs_7_) | copy-start | bytes 196612
  27.7 4.0 %copy-start.2 = (f32[1,128,128]{2,1,0:T(8,128)S(1)}, f32[1,128,128]{2,1,0:T(8,128)}, u32[]{:S(2)}) copy-start(f32[1,128,128]{2,1,0:T(8,128)} %constant.12.clone.refs_6_) | copy-start | bytes 196612
  27.7 4.0 %copy-start.3 = (f32[16,128]{1,0:T(8,128)S(1)}, f32[16,128]{1,0:T(8,128)}, u32[]{:S(2)}) copy-start(f32[16,128]{1,0:T(8,128)} %constant.14.clone.refs_8_) | copy-start | bytes 24580
  27.7 4.0 %copy-start.4 = (f32[16,16]{1,0:T(8,128)S(1)}, f32[16,16]{1,0:T(8,128)}, u32[]{:S(2)}) copy-start(f32[16,16]{1,0:T(8,128)} %constant.11.clone.refs_5_) | copy-start | bytes 3076
  27.8 4.0 %copy-start.5 = (f32[16,16]{1,0:T(8,128)S(1)}, f32[16,16]{1,0:T(8,128)}, u32[]{:S(2)}) copy-start(f32[16,16]{1,0:T(8,128)} %constant.10.clone.refs_4_) | copy-start | bytes 3076
  27.8 6.0 %collective-permute-start.8 = (f32[14,8,128]{2,1,0:T(8,128)S(1)}, f32[14,8,128]{2,1,0:T(8,128)S(1)}, u32[]{:S(2)}, u32[]{:S(2)}) collective-permute-start(f32[14,8,128]{2,1,0:T(8,128)S(1)} %get-tuple-element.41), channel_id=1, source_target_pairs={{0,12},{4,0},{8,4},{12,8},{1,13},{5,1},{9,5},{13,9},{2,14},{6,2},{... | collective-permute-start | bytes 172040 | tf_op jit(solution)/shard_map/ppermute | solution.py:686
  29.9 3.9 %collective-permute-start.9 = (f32[14,8,128]{2,1,0:T(8,128)S(1)}, f32[14,8,128]{2,1,0:T(8,128)S(1)}, u32[]{:S(2)}, u32[]{:S(2)}) collective-permute-start(f32[14,8,128]{2,1,0:T(8,128)S(1)} %get-tuple-element.42), channel_id=1, source_target_pairs={{0,4},{4,8},{8,12},{12,0},{1,5},{5,9},{9,13},{13,1},{2,6},{6,10},{... | collective-permute-start | bytes 172040 | tf_op jit(solution)/shard_map/ppermute | solution.py:686
  30.4 5.9 %collective-permute-start.13 = (f32[17,8,128]{2,1,0:T(8,128)S(1)}, f32[17,8,128]{2,1,0:T(8,128)S(1)}, u32[]{:S(2)}, u32[]{:S(2)}) collective-permute-start(f32[17,8,128]{2,1,0:T(8,128)S(1)} %get-tuple-element.47), channel_id=1, source_target_pairs={{0,12},{4,0},{8,4},{12,8},{1,13},{5,1},{9,5},{13,9},{2,14},{6,2},{... | collective-permute-start | bytes 208904 | tf_op jit(solution)/shard_map/ppermute | solution.py:686
  31.7 4.7 %collective-permute-start.14 = (f32[17,8,128]{2,1,0:T(8,128)S(1)}, f32[17,8,128]{2,1,0:T(8,128)S(1)}, u32[]{:S(2)}, u32[]{:S(2)}) collective-permute-start(f32[17,8,128]{2,1,0:T(8,128)S(1)} %get-tuple-element.48), channel_id=1, source_target_pairs={{0,4},{4,8},{8,12},{12,0},{1,5},{5,9},{9,13},{13,1},{2,6},{6,10},{... | collective-permute-start | bytes 208904 | tf_op jit(solution)/shard_map/ppermute | solution.py:686

commit v5 on v4

--- a/solution.py
+++ b/solution.py
@@ -27,8 +27,15 @@
     return jax.ShapeDtypeStruct(extent, F32)
 
 
-def call(kernel, outs, scratch, microseconds, *args):
+def call(kernel, outs, scratch, microseconds, *args, after=()):
     flops = int(microseconds * PEAK_FLOPS_PER_US)
+    if after:
+        inner, first, last = kernel, len(args), len(args) + len(after)
+
+        def kernel(*refs):
+            inner(*refs[:first], *refs[last:])
+
+        args = (*args, *after)
     return pl.pallas_call(
         kernel,
         out_shape=outs,
@@ -59,11 +66,16 @@
 
 
 def dot_ones(left, right):
-    dims = (((1,), (0,)), ((), ()))
     large = left.astype(jnp.bfloat16)
-    small = (left - large.astype(F32)).astype(jnp.bfloat16)
-    total = lax.dot_general(large, right, dims, preferred_element_type=F32)
-    return total + lax.dot_general(small, right, dims, preferred_element_type=F32)
+    rest = left - large.astype(F32)
+    middle = rest.astype(jnp.bfloat16)
+    small = (rest - middle.astype(F32)).astype(jnp.bfloat16)
+    return lax.dot_general(
+        jnp.concatenate([large, middle, small], axis=1),
+        jnp.concatenate([right, right, right], axis=0),
+        (((1,), (0,)), ((), ())),
+        preferred_element_type=F32,
+    )
 
 
 def seven_sum(source, plane, below, above, wanted=None):
@@ -167,7 +179,7 @@
     clear_planes(target, (low - 2, low - 1, high, high + 1))
 
 
-def spread_kernel(field, up, down, far, g1_out, zeroth, first, second, third, g1_a, g1_b):
+def spread_kernel(field, message, g2_out, g1_out, zeroth, first, second, third, g1_a, g1_b):
     planes = field.shape[1]
     fill_source(field, zeroth)
     low, high = PLANE0, PLANE0 + planes + 1
@@ -212,80 +224,66 @@
         total = total + g1_b[0, 2 * c + 1, pl.ds(0, rows2, stride=2), :]
         total = total + g1_b[0, 2 * c + 1, pl.ds(1, rows2, stride=2), :]
         parts.append(total)
-    even = jnp.concatenate(parts[0::2], axis=0)
-    odd = jnp.concatenate(parts[1::2], axis=0)
-    g2 = dot_ones(even, one_hot(lambda r, c: c == r // 2))
-    g2 = g2 + dot_ones(odd, one_hot(lambda r, c: c == 64 + r // 2))
-    g2 = g2 * (0.125 / 343.0)
-    size = g2.shape[0]
-    far[...] = g2
-    up[0:size] = g2
-    down[0:size] = g2
-    up[size : size + rows1] = pack_lanes(lambda c: g1[c], share, 89, 9, 10, rows1)[0]
-    down[size : size + rows1] = pack_lanes(lambda c: g1[c], share, 30, 9, 10, rows1)[0]
-    rows0 = zeroth.shape[2] - ROW0
-    lane = iota((rows0, LANES), 1)
-
-    def last_columns(i):
-        p = PLANE0 + i
-        return jnp.where(lane == 0, zeroth[1, p, ROW0:], zeroth[0, p, ROW0:])
-
-    def first_columns(i):
-        return zeroth[0, PLANE0 + i, ROW0:]
-
-    size = size + rows1
-    up[size:] = pack_lanes(last_columns, planes + 1, LANES - SPILL, SPILL + 1, 7, rows0)[0]
-    down[size:] = pack_lanes(first_columns, planes + 1, 0, SPILL + 1, 7, rows0)[0]
-
-
-def gather_z_kernel(count, *refs):
-    own, g1, up, received = refs[0], refs[1], refs[2], refs[3 : 2 + count]
-    g2_out, g1_out, message = refs[2 + count :]
-    size = own.shape[0]
-    period = 32 * count
-    rows2 = 16
-    tiles, planes = g2_out.shape[0], g2_out.shape[1]
-    lane = iota((size, LANES), 1)
-    for parity in range(2):
-        totals = [jnp.zeros((size, LANES), F32) for _ in range(tiles)]
-        for o in range(count):
-            value = own[...] if o == 0 else received[o - 1][0:size]
-            shift = (32 * o - 64 * parity) % LANES
-            turned = pltpu.roll(value, shift, 1) if shift else value
-            position = ((lane - shift) & (LANES - 1)) - 64 * parity
-            inside = (position >= 0) & (position < 64)
-            for t in range(tiles):
-                lands = lax.rem(position + (32 * o + period), period) == lane + LANES * t
-                totals[t] = totals[t] + jnp.where(inside & lands, turned, 0.0)
-        for t in range(tiles):
-            for k in range(planes // 2):
-                g2_out[t, 2 * k + parity] = totals[t][rows2 * k : rows2 * (k + 1)]
-    rows1 = g1.shape[1]
-    above = received[0][size : size + rows1]
-    below = received[count - 2][size : size + rows1]
-    share = g1.shape[0]
-    for c in range(share):
-        value = g1[c] + unpacked(below, c, 10, 0, 9, 25, rows1)
-        g1_out[c] = value + unpacked(above, c, 10, 0, 9, 94, rows1)
+    groups = -(-len(parts) // 3)
+    parts.extend([jnp.zeros((rows2, LANES), F32)] * (3 * groups - len(parts)))
+    g2 = None
+    for slot in range(3):
+        matrix = one_hot(
+            lambda r, c: (c == r // 2 - 13 + 42 * slot) & (r // 2 >= 13) & (r // 2 < 51)
+        )
+        term = dot_ones(jnp.concatenate(parts[slot::3], axis=0), matrix)
+        g2 = term if g2 is None else g2 + term
+    g2_out[...] = g2 * (0.125 / 343.0)
     lane = iota((ROWS_SENT, LANES), 1)
+    sides = jnp.zeros((ROWS_SENT, LANES), F32)
     for q in range(share // 2):
         even, odd = g1_out[2 * q, 2 : 2 + ROWS_SENT], g1_out[2 * q + 1, 2 : 2 + ROWS_SENT]
         value = jnp.where(lane < 64, pltpu.roll(even, LANES - 32, 1), pltpu.roll(odd, 32, 1))
         message[ROWS_SENT * q : ROWS_SENT * (q + 1)] = value
-    start = ROWS_SENT * (share // 2)
-    for q in range(-(-share // 8)):
-        packed = jnp.zeros((ROWS_SENT, LANES), F32)
-        for k in range(min(8, share - 8 * q)):
-            value = g1_out[8 * q + k, 2 : 2 + ROWS_SENT]
-            low = pltpu.roll(value, (16 * k - 24) % LANES, 1)
-            high = pltpu.roll(value, (16 * k + 8 - 96) % LANES, 1)
-            packed = jnp.where((lane >= 16 * k) & (lane < 16 * k + 8), low, packed)
-            packed = jnp.where((lane >= 16 * k + 8) & (lane < 16 * k + 16), high, packed)
-        message[start : start + ROWS_SENT] = packed
-        start += ROWS_SENT
-    rows0 = (message.shape[0] - start) // 3
-    for k, strip in enumerate((received[count - 2], received[0], up)):
-        message[start + rows0 * k : start + rows0 * (k + 1)] = strip[size + rows1 :]
+        for c, value in ((2 * q, even), (2 * q + 1, odd)):
+            low = pltpu.roll(value, (8 * c - 28) % LANES, 1)
+            high = pltpu.roll(value, (8 * c + 4 - 96) % LANES, 1)
+            sides = jnp.where((lane >= 8 * c) & (lane < 8 * c + 4), low, sides)
+            sides = jnp.where((lane >= 8 * c + 4) & (lane < 8 * c + 8), high, sides)
+    size = ROWS_SENT * (share // 2)
+    message[size : size + ROWS_SENT] = sides
+    size = size + ROWS_SENT
+    rows0 = zeroth.shape[2] - ROW0
+    lane = iota((rows0, LANES), 1)
+
+    def last_columns(i):
+        p = PLANE0 + i
+        return jnp.where(lane == 0, zeroth[1, p, ROW0:], zeroth[0, p, ROW0:])
+
+    def first_columns(i):
+        return zeroth[0, PLANE0 + i, ROW0:]
+
+    last = pack_lanes(last_columns, planes + 1, LANES - SPILL, SPILL + 1, 7, rows0)[0]
+    message[size : size + rows0] = last
+    first = pack_lanes(first_columns, planes + 1, 0, SPILL + 1, 7, rows0)[0]
+    message[size + rows0 :] = first
+
+
+def gather_z_kernel(count, *refs):
+    shares, out = refs[:count], refs[count]
+    size = shares[0].shape[0]
+    period = 32 * count
+    rows2 = 16
+    tiles, planes = out.shape[0], out.shape[1]
+    lane = iota((size, LANES), 1)
+    for slot in range(3):
+        totals = [jnp.zeros((size, LANES), F32) for _ in range(tiles)]
+        for o in range(count):
+            shift = (32 * o + 13 - 42 * slot) % LANES
+            turned = pltpu.roll(shares[o][...], shift, 1) if shift else shares[o][...]
+            position = ((lane - shift) & (LANES - 1)) - 42 * slot
+            inside = (position >= 0) & (position < 38)
+            for t in range(tiles):
+                lands = lax.rem(position + (32 * o + 13 + period), period) == lane + LANES * t
+                totals[t] = totals[t] + jnp.where(inside & lands, turned, 0.0)
+        for t in range(tiles):
+            for c in range(slot, planes, 3):
+                out[t, c] = totals[t][rows2 * (c // 3) : rows2 * (c // 3 + 1)]
 
 
 ROWS_SENT = 20
@@ -296,13 +294,73 @@
     pair = message[ROWS_SENT * (c // 2) : ROWS_SENT * (c // 2 + 1)]
     inside = (lane >= 32) & (lane < 96)
     value = jnp.where(inside, pltpu.roll(pair, LANES - 32 if c % 2 else 32, 1), 0.0)
-    start = ROWS_SENT * (share // 2 + c // 8)
+    start = ROWS_SENT * (share // 2)
     sides = message[start : start + ROWS_SENT]
-    k = c % 8
-    low = pltpu.roll(sides, (24 - 16 * k) % LANES, 1)
-    high = pltpu.roll(sides, (88 - 16 * k) % LANES, 1)
-    value = jnp.where((lane >= 24) & (lane < 32), low, value)
-    return jnp.where((lane >= 96) & (lane < 104), high, value)
+    low = pltpu.roll(sides, (28 - 8 * c) % LANES, 1)
+    high = pltpu.roll(sides, (92 - 8 * c) % LANES, 1)
+    value = jnp.where((lane >= 28) & (lane < 32), low, value)
+    return jnp.where((lane >= 96) & (lane < 100), high, value)
+
+
+def rows_kernel(sources, strips, *refs):
+    inputs, (out, up, down) = refs[:-3], refs[-3:]
+    own, messages = inputs[0], inputs[1:]
+    planes, share = out.shape[0], own.shape[0]
+    read = {}
+    for p in range(planes):
+        total = None
+        for index, offset in sources:
+            c = p - 7 - 8 * offset + 2
+            if not 0 <= c < share:
+                continue
+            if (index, c) not in read:
+                if index == 0:
+                    read[index, c] = own[c, 2 : 2 + ROWS_SENT]
+                else:
+                    read[index, c] = plane_sent(messages[index], share, c)
+            value = read[index, c]
+            total = value if total is None else total + value
+        out[p] = total
+        down[9 * p : 9 * p + 9] = total[0:9]
+        up[9 * p : 9 * p + 9] = total[11:20]
+    start = ROWS_SENT * (share // 2 + 1)
+    inner = (messages[0].shape[0] - start) // 2
+    place = 9 * planes
+    for k in range(strips):
+        for part in range(2):
+            begin = start + inner * part
+            down[place : place + 6] = messages[k][begin : begin + 6]
+            last = begin + inner - 8 - SPILL
+            up[place : place + 6] = messages[k][last : last + 6]
+            place += 6
+
+
+def columns_kernel(strips, g1, *refs):
+    messages, (above, below), (out, up, down) = refs[:-5], refs[-5:-3], refs[-3:]
+    planes, rows = out.shape[0], out.shape[1]
+    for p in range(planes):
+        out[p] = jnp.zeros((rows, LANES), F32)
+        out[p, 6 : 6 + ROWS_SENT] = g1[p]
+        out[p, 22:31] = out[p, 22:31] + above[9 * p : 9 * p + 9]
+        out[p, 1:10] = out[p, 1:10] + below[9 * p : 9 * p + 9]
+    share = planes - 10
+    start = ROWS_SENT * (share // 2 + 1)
+    inner = (messages[0].shape[0] - start) // 2
+    for target, first, part in ((up, 89, 0), (down, 30, 1)):
+        place = 0
+        for packed in pack_lanes(lambda p: out[p], planes, first, 9, 9, rows):
+            target[place : place + rows] = packed
+            place += rows
+        for k in range(strips):
+            begin = start + inner * part
+            six = 9 * planes + 6 * (2 * k + part)
+            target[place : place + ROW0] = jnp.zeros((ROW0, LANES), F32)
+            target[place + ROW0 : place + ROW0 + inner] = messages[k][begin : begin + inner]
+            at = place + ROW0 - SPILL
+            target[at : at + 6] = target[at : at + 6] + below[six : six + 6]
+            at = place + ROW0 + inner - 8
+            target[at : at + 6] = target[at : at + 6] + above[six : six + 6]
+            place += ROW0 + inner
 
 
 def fold_x_kernel(count, *refs):
@@ -319,40 +377,22 @@
             out[t, x] = total
 
 
-def window_x_kernel(sources, *refs):
-    own, inputs, (out, down, up, base, first, second) = refs[0], refs[1:-6], refs[-6:]
-    planes, share = base.shape[1], out.shape[0]
-    read = {}
+def window_kernel(g1, above, below, out, base, first, second):
+    planes, rows = base.shape[1], base.shape[2]
     for p in range(planes):
-        total = None
-        for index, offset in sources:
-            c = p - 7 - 8 * offset + 2
-            if not 0 <= c < share:
-                continue
-            if (index, c) not in read:
-                if index == 0:
-                    read[index, c] = own[c, 2 : 2 + ROWS_SENT]
-                else:
-                    read[index, c] = plane_sent(inputs[index - 1], share, c)
-            value = read[index, c]
-            total = value if total is None else total + value
-        base[0, p, 0:8] = jnp.zeros((8, LANES), F32)
-        base[0, p, 24:32] = jnp.zeros((8, LANES), F32)
-        base[0, p, 6 : 6 + ROWS_SENT] = total
+        begin = rows * (p // 14)
+        lower = below[begin : begin + rows]
+        upper = above[begin : begin + rows]
+        total = g1[p] + unpacked(lower, p % 14, 9, 0, 9, 25, rows)
+        base[0, p] = total + unpacked(upper, p % 14, 9, 0, 9, 94, rows)
     seventh = 1.0 / 7.0
     sweep(first, base, 1, planes - 1, base, seventh)
     sweep(second, first, 2, planes - 2, base, seventh)
     sweep(first, second, 3, planes - 3, base, seventh)
     sweep(second, first, 4, planes - 4, base, seventh)
-    share = out.shape[0]
-    for c in range(share):
+    for c in range(out.shape[0]):
         p = 5 + c
-        value = (seven_sum(second, p, p - 1, p + 1)[0] * seventh + base[0, p]) * weight(1)
-        out[c] = value
-        down[c] = value[1:9]
-        up[c] = value[22:30]
-        down[share + c // 8, c % 8 : c % 8 + 1] = value[9:10]
-        up[share + c // 8, c % 8 : c % 8 + 1] = value[30:31]
+        out[c] = (seven_sum(second, p, p - 1, p + 1)[0] * seventh + base[0, p]) * weight(1)
 
 
 def restrict_lanes(values, width, coarse_width, coarse_tiles):
@@ -497,15 +537,8 @@
         out[c] = g[0, (c - 3) % planes, 0:16]
 
 
-def correct_kernel(e2, f1_own, f1_above, f1_below, u0_b, u1_a, u1_b, f1, u0_a):
-    share1 = f1_own.shape[0]
-    for c in range(share1):
-        f1[c] = f1_own[c]
-        f1[c, 17:25] = f1[c, 17:25] + f1_above[c]
-        f1[c, 6:14] = f1[c, 6:14] + f1_below[c]
-        ninth, k = share1 + c // 8, c % 8
-        f1[c, 25:26] = f1[c, 25:26] + f1_above[ninth, k : k + 1]
-        f1[c, 14:15] = f1[c, 14:15] + f1_below[ninth, k : k + 1]
+def correct_kernel(e2, f1, u0_b, u1_a, u1_b, u0_a):
+    share1 = f1.shape[0]
     share2 = e2.shape[0]
     rows2 = e2.shape[1]
     value = e2[...].reshape(share2 * rows2, LANES)
@@ -519,19 +552,19 @@
     sweep(u1_b, u1_a, 1, count1 - 1)
     sweep(u1_a, u1_b, 2, count1 - 2)
     sweep(u1_b, u1_a, 3, count1 - 3)
-    rows1 = 24
+    rows1, sent = 24, 20
     parts = []
     for c in range(share1):
-        parts.append(f1[c, 4 : 4 + rows1] + u1_b[0, 4 + c, 4 : 4 + rows1] * (1.0 / 343.0))
+        parts.append(f1[c, 6 : 6 + rows1] + u1_b[0, 4 + c, 6 : 6 + rows1] * (1.0 / 343.0))
     value = jnp.concatenate(parts, axis=0)
     main = dot_ones(value, one_hot(lambda r, c: r == 32 + c // 2))
     side = dot_ones(value, one_hot(lambda r, c: r == jnp.where(c < 64, 96 + c // 2, c // 2 - 32)))
     for t, value in enumerate((main, side)):
         for c in range(share1):
-            part = value[rows1 * c : rows1 * (c + 1)]
+            part = value[rows1 * c : rows1 * c + sent]
             for p in (2 * c, 2 * c + 1):
-                u0_a[t, p, pl.ds(0, rows1, stride=2), :] = part
-                u0_a[t, p, pl.ds(1, rows1, stride=2), :] = part
+                u0_a[t, p, pl.ds(0, sent, stride=2), :] = part
+                u0_a[t, p, pl.ds(1, sent, stride=2), :] = part
     count0 = 2 * share1
     sweep(u0_b, u0_a, 1, count0 - 1)
     sweep(u0_a, u0_b, 2, count0 - 2)
@@ -542,16 +575,16 @@
     planes, rows = field.shape[1], field.shape[2]
     scale = 1.0 / 343.0
     for i in range(planes + 1):
-        pot[i, 0:rows] = u0_b[0, 4 + i, ROW0 : ROW0 + rows] * scale + f0[i, 0:rows]
+        pot[i, 0:rows] = u0_b[0, 4 + i, 4 : 4 + rows] * scale + f0[i, 0:rows]
         if i < planes:
-            edge = u0_b[0, 4 + i, ROW0 + rows : ROW0 + rows + 1] * scale
+            edge = u0_b[0, 4 + i, 4 + rows : 5 + rows] * scale
             pot[i, rows : rows + 1] = edge + f0[i, rows : rows + 1]
     lane = iota((rows, LANES), 1)
     for i in range(planes):
         here = pot[i, 0:rows]
         out[0, i] = field[0, i] - (pot[i + 1, 0:rows] - here)
         out[1, i] = field[1, i] - (pot[i, 1 : rows + 1] - here)
-        last = pltpu.roll(u0_b[1, 4 + i, ROW0 : ROW0 + rows], LANES - 1, 1) * scale + beyond[i]
+        last = pltpu.roll(u0_b[1, 4 + i, 4 : 4 + rows], LANES - 1, 1) * scale + beyond[i]
         next_z = jnp.where(lane == LANES - 1, last, pltpu.roll(here, LANES - 1, 1))
         out[2, i] = field[2, i] - (next_z - here)
 
@@ -562,7 +595,7 @@
     return p - share + 13 if p >= share - 6 else p + 7
 
 
-def fine_own_kernel(zeroth, first, second, third, field, after, main, down, up, field_out, fourth):
+def fine_own_kernel(zeroth, first, second, third, field, main, down, up, field_out, fourth):
     share = main.shape[0]
     field_out[...] = field[...]
     low, high = PLANE0, zeroth.shape[1] - 6
@@ -584,55 +617,46 @@
 BEYOND = 96
 
 
-def fine_edge_kernel(start, *refs):
-    strips, (out, down, up, base, first, second) = refs[:3], refs[3:]
-    share, rows = out.shape[0], out.shape[1]
-    planes = share - 1
-    inner = rows - ROW0
-    lane = iota((inner, LANES), 1)
-    sources = [
-        [r[start + inner * k : start + inner * (k + 1)] for k in range(3)] for r in strips
-    ]
+def fine_edge_kernel(sources, above, below, own, out, base, first, second):
+    planes, rows = out.shape[0] - 1, base.shape[2]
+    lane = iota((rows, LANES), 1)
+    strips = 1 + max(index for index, offset in sources)
+    start = above.shape[0] - rows * strips
     for k in range(base.shape[1]):
-        value = jnp.zeros((inner, LANES), F32)
-        for d, offset in ((0, 0), (1, -planes), (2, planes)):
-            i = k - SPILL - offset
+        value = jnp.zeros((rows, LANES), F32)
+        for index, offset in sources:
+            i = k - SPILL - offset * planes
             if not 0 <= i <= planes:
                 continue
-            below, above, own = sources[d]
-            turned = pltpu.roll(below, (LANES - SPILL - 7 * i) % LANES, 1)
+            begin = start + rows * index
+            turned = pltpu.roll(below[begin : begin + rows], (LANES - SPILL - 7 * i) % LANES, 1)
             value = value + jnp.where((lane >= LANES - SPILL) | (lane == 0), turned, 0.0)
-            turned = pltpu.roll(above, (EDGE - 7 * i) % LANES, 1)
+            turned = pltpu.roll(above[begin : begin + rows], (EDGE - 7 * i) % LANES, 1)
             value = value + jnp.where((lane >= EDGE) & (lane <= EDGE + SPILL), turned, 0.0)
-            turned = pltpu.roll(above, (BEYOND - 7 * i) % LANES, 1)
-            value = value + jnp.where((lane >= BEYOND) & (lane <= BEYOND + SPILL), turned, 0.0)
-            turned = pltpu.roll(own, (BEYOND - SPILL - 7 * i) % LANES, 1)
+            turned = pltpu.roll(own[begin : begin + rows], (BEYOND - SPILL - 7 * i) % LANES, 1)
             value = value + jnp.where((lane >= BEYOND - SPILL) & (lane <= BEYOND), turned, 0.0)
-        base[0, k, 0:ROW0] = jnp.zeros((ROW0, LANES), F32)
-        base[0, k, ROW0:] = value
+        base[0, k] = value
     seventh = 1.0 / 7.0
     high = base.shape[1]
     sweep(first, base, 1, high - 1, base, seventh)
     sweep(second, first, 2, high - 2, base, seventh)
     sweep(first, second, 3, high - 3, base, seventh)
     sweep(second, first, 4, high - 4, base, seventh)
-    for i in range(share):
+    kept = out.shape[1]
+    for i in range(planes + 1):
         p = SPILL + i
         value = (seven_sum(second, p, p - 1, p + 1)[0] * seventh + base[0, p]) * weight(0)
-        out[i] = value
-        down[i] = value[1:9]
-        up[i] = value[40:48]
-
-
-def fine_sum_kernel(f0, below_x, above_x, edge, above, below, out, beyond, work):
+        out[i] = value[ROW0 : ROW0 + kept]
+
+
+def turned_to_last(value, lane):
+    return pltpu.roll(value, LANES - 1 - lane, 1)
+
+
+def fine_sum_kernel(f0, below_x, above_x, work, out, beyond):
     planes, rows = beyond.shape[0], beyond.shape[1]
     lane = iota((rows, LANES), 1)
     lane1 = iota((1, LANES), 1)
-    work[:, 0:rows] = edge[:, ROW0 : ROW0 + rows]
-    work[:, rows : rows + 8] = edge[:, ROW0 + rows : ROW0 + rows + 8]
-    for i in range(planes + 1):
-        work[i, 25:33] = work[i, 25:33] + above[i]
-        work[i, 0:8] = work[i, 0:8] + below[i]
     for i in range(planes + 1):
         value = f0[fine_place(i + SPILL, planes + 11)]
         if i <= SPILL:
@@ -644,7 +668,7 @@
         value = value + jnp.where(lane <= SPILL, part, 0.0)
         out[i, 0:rows] = value + jnp.where(lane >= LANES - SPILL, turned, 0.0)
         if i < planes:
-            beyond[i] = pltpu.roll(part, LANES - 1 - BEYOND, 1)
+            beyond[i] = turned_to_last(part, EDGE) + turned_to_last(part, BEYOND)
             row = f0[6, i + SPILL : i + SPILL + 1]
             if i <= SPILL:
                 row = row + below_x[0, i + SPILL + planes : i + SPILL + planes + 1]
@@ -668,9 +692,6 @@
         out[6, p : p + 1] = work[p, ROW0 + rows : ROW0 + rows + 1]
 
 
-EARLIER = {1: (), -1: (1,), 2: (1, -1), -2: (1, -1, 2)}
-
-
 def body(field):
     nx, ny, nz = field.shape[1:]
     size_x, size_y, size_z = lax.axis_size("gx"), lax.axis_size("gy"), lax.axis_size("gz")
@@ -687,20 +708,55 @@
 
     level0 = (2, planes0, rows0, LANES)
     level1 = (1, n1 + 12, ny // 2 + 16, LANES)
-    packed = ((n1 // 2 + 6) // 2) * 16
-    near = packed + rows1 + rows0 - ROW0
-    up, down, far, g1, *powers = call(
+    packed = -(-(n1 // 2 + 6) // 3) * 16
+    inner0 = rows0 - ROW0
+    sent1 = ROWS_SENT * (share1 // 2 + 1)
+    message, g2, g1, *powers = call(
         spread_kernel,
-        [shape(near, LANES), shape(near, LANES), shape(packed, LANES),
+        [shape(sent1 + 2 * inner0, LANES), shape(packed, LANES),
          shape(share1, rows1, LANES)] + [shape(*level0)] * 4,
         [level1, level1],
         2.9,
         field,
     )
-    received = []
-    for o in range(1, size_z):
-        message = down if o == 1 else (up if o == size_z - 1 else far)
-        received.append(from_offset(message, "gz", o))
+    shares = [g2] + [from_offset(g2, "gz", o) for o in range(1, size_z)]
+    messages = {0: message}
+    sources = []
+    for o in (0, 1, -1, 2, -2):
+        key = [k for k in messages if k % size_x == o % size_x]
+        if not key:
+            messages[o] = from_offset(message, "gx", o)
+            key = [o]
+        sources.append((list(messages).index(key[0]), o))
+    messages = list(messages.values())
+    strips = min(3, size_x)
+    planes1 = n1 + 14
+    sent_y = 9 * planes1 + 12 * strips
+    rows_g1, up, down = call(
+        functools.partial(rows_kernel, tuple(sources), strips),
+        [shape(planes1, ROWS_SENT, LANES), shape(sent_y, LANES), shape(sent_y, LANES)],
+        [],
+        0.2,
+        g1, *messages,
+    )
+    window = (1, planes1, ny // 2 + 16, LANES)
+    sent_z = window[2] * -(-planes1 // 14) + rows0 * strips
+    window_g1, up, down = call(
+        functools.partial(columns_kernel, strips),
+        [shape(*window[1:]), shape(sent_z, LANES), shape(sent_z, LANES)],
+        [],
+        0.3,
+        rows_g1, *messages[:strips], from_offset(down, "gy", 1), from_offset(up, "gy", -1),
+    )
+    above = from_offset(down, "gz", 1)
+    below = from_offset(up, "gz", -1)
+    f1 = call(
+        window_kernel,
+        shape(share1, *window[2:]),
+        [window, window, window],
+        0.9,
+        window_g1, above, below,
+    )
     share0 = nx + 11
     main, f_down, f_up, kept = call(
         fine_own_kernel,
@@ -708,49 +764,31 @@
          shape(*field.shape)],
         [level0],
         3.0,
-        *powers, field, received[size_z // 2 - 1],
+        *powers, field,
+        after=(messages[1],),
     )
     f_above = from_offset(f_down, "gy", 1)
     f_below = from_offset(f_up, "gy", -1)
 
     tiles = size_z * 32 // LANES
-    inner0 = rows0 - ROW0
-    sent1 = ROWS_SENT * (share1 // 2 - (-share1 // 8))
-    g2, g1, message = call(
+    g2 = call(
         functools.partial(gather_z_kernel, size_z),
-        [shape(tiles, n1 // 2 + 6, 16, LANES), shape(share1, rows1, LANES),
-         shape(sent1 + 3 * inner0, LANES)],
+        shape(tiles, n1 // 2 + 6, 16, LANES),
         [],
-        0.2,
-        far, g1, up, *received,
+        0.15,
+        *shares,
+        after=(rows_g1, main,),
     )
     shares = [g2] + [from_offset(g2, "gx", o) for o in range(1, size_x)]
-    messages = {o: from_offset(message, "gx", o) for o in sorted({1, -1, 2, -2}, key=abs)
-                if o % size_x and not any(o % size_x == q % size_x for q in EARLIER[o])}
-    keys = [0] + list(messages)
-    sources = []
-    for o in (0, 1, -1, 2, -2):
-        index = [k for k, key in enumerate(keys) if key % size_x == o % size_x][0]
-        sources.append((index, o))
     g2 = call(
         functools.partial(fold_x_kernel, size_x),
         shape(tiles, 4 * size_x, 16, LANES),
         [],
         0.05,
         *shares,
-    )
-    window = (1, n1 + 14, ny // 2 + 16, LANES)
-    edge1 = share1 + -(-share1 // 8)
-    f1, f1_down, f1_up = call(
-        functools.partial(window_x_kernel, tuple(sources)),
-        [shape(share1, ny // 2 + 16, LANES), shape(edge1, 8, LANES), shape(edge1, 8, LANES)],
-        [window, window, window],
-        1.0,
-        g1, *messages.values(),
+        after=(window_g1,),
     )
     shares = [g2] + [from_offset(g2, "gy", o) for o in range(1, size_y)]
-    f1_above = from_offset(f1_down, "gy", 1)
-    f1_below = from_offset(f1_up, "gy", -1)
 
     f0 = call(
         fine_y_kernel,
@@ -766,21 +804,19 @@
         f_above = from_offset(f0[0:7], "gx", 1)
         f_below = from_offset(f0[6:13], "gx", -1)
     edges = (1, nx + 11, rows0, LANES)
-    edge, e_down, e_up = call(
-        functools.partial(fine_edge_kernel, sent1),
-        [shape(nx + 1, rows0, LANES), shape(nx + 1, 8, LANES), shape(nx + 1, 8, LANES)],
+    edge = call(
+        functools.partial(fine_edge_kernel, tuple(sources[:3])),
+        shape(nx + 1, ny + 8, LANES),
         [edges, edges, edges],
-        2.0,
-        message, messages[-1 if -1 in messages else 1], messages[1],
-    )
-    e_above = from_offset(e_down, "gy", 1)
-    e_below = from_offset(e_up, "gy", -1)
+        1.9,
+        above, below, up,
+    )
     f0, beyond = call(
         fine_sum_kernel,
         [shape(nx + 1, ny + 8, LANES), shape(nx, ny, LANES)],
-        [(nx + 1, ny + 8, LANES)],
-        0.4,
-        f0, f_below, f_above, edge, e_above, e_below,
+        [],
+        0.3,
+        f0, f_below, f_above, edge,
     )
 
     scratch = []
@@ -794,14 +830,15 @@
         scratch,
         2.2,
         *shares, *last_level_matrices(size_x, 2 * size_y, 8 * size_z),
-    )
-    fine = (2, nx + 8, rows0, LANES)
+        after=(f1,),
+    )
+    fine = (2, nx + 8, ny + 8, LANES)
     correction = call(
         correct_kernel,
         shape(*fine),
-        [level1, level1, (share1, ny // 2 + 16, LANES), fine],
-        2.6,
-        e2, f1, f1_above, f1_below,
+        [level1, level1, fine],
+        2.2,
+        e2, f1,
     )
     return call(
         finish_kernel,

time: 38.3 us -> 35.5 us (0.927); the launches traced: 37.8 us -> 35.4 us
  waiting for transfers between devices: 7.12 us -> 4.98 us
    ppermute x15, waiting for transfers between devices: 7.12 us -> 4.98 us  [from_offset(): return lax.ppermute(value, axis, pairs)]
    pallas_call x11 -> x13, Pallas kernels: 13.6 us -> 13.4 us  [call(): pl.pallas_call(kernel, out_shape=outs, scratch_shapes=[pltpu.VMEM(s, F32)...]
    unnamed x12 -> x14, local copies, waits for them, and re-layouts: 1.17 us -> 1.17 us
  transfers between devices with their start and end apart: 15 -> 15, of which waited for: 3 -> 5; matrix products, arithmetic and copies ran while one was open for 0% -> 0% of each run, Pallas kernels for 25% -> 26%
where the time goes in v5:
time: 35.5 us; the launch traced here: 35.4 us
  starting transfers between devices  15.6 us (44%)
  Pallas kernels  13.4 us (38%)
  waiting for transfers between devices  4.98 us (14%)
  local copies, waits for them, and re-layouts  1.2 us (3%)
    ppermute x15, starting transfers between devices, from_offset(): return lax.ppermute(value, axis, pairs)  15.6 us
    pallas_call x13, Pallas kernels, call(): pl.pallas_call(kernel, out_shape=outs, scratch_shapes=[pltpu.VMEM(s, F32)...  13.4 us
    ppermute x15, waiting for transfers between devices, from_offset(): return lax.ppermute(value, axis, pairs)  4.98 us
    unnamed x14, local copies, waits for them, and re-layouts  1.17 us
  transfers between devices with their start and end apart: 15, of which 5 were waited for; matrix products, arithmetic and copies ran while one was open for 0% of the time, Pallas kernels for 26%

profile of v5, /device:TPU:0, one launch (start us, length us, event | category | flops | bytes accessed | tf_op | source)
XLA Modules:
  0.0 35.4 jit_solution(2948278403941640597)
XLA Ops:
  0.0 1.1 %copy-done = f32[3,16,32,128]{3,2,1,0:T(8,128)S(1)} copy-done((f32[3,16,32,128]{3,2,1,0:T(8,128)S(1)}, f32[3,16,32,128]{3,2,1,0:T(8,128)}, u32[]{:S(2)}) %copy-start) | copy-done | bytes 786456
  1.1 2.6 %shard_map.64 = (f32[220,128]{1,0:T(8,128)S(1)}, f32[64,128]{1,0:T(8,128)S(1)}, f32[12,24,128]{2,1,0:T(8,128)S(1)}, f32[2,29,48,128]{3,2,1,0:T(8,128)S(1)}, f32[...) custom-call(f32[3,16,32,128]{3,2,1,0:T(8,128)S(1)} %copy-done), custom_call_target="tpu_custom_call" | custom-call | flops 3335000064 | tf_op jit(solution)/shard_map/pallas_call | solution.py:39
  3.8 3.0 %collective-permute-start = (f32[220,128]{1,0:T(8,128)S(1)}, f32[220,128]{1,0:T(8,128)S(1)}, u32[]{:S(2)}, u32[]{:S(2)}) collective-permute-start(f32[220,128]{1,0:T(8,128)S(1)} %get-tuple-element.28.refs_1_.refs_0_), channel_id=1, source_target_pairs={{0,16},{16,0},{1,17},{17,1},{2,18},{18,2},{3,19},{19,3},{4,20},{20... | collective-permute-start | bytes 337928 | tf_op jit(solution)/shard_map/ppermute | solution.py:707
  6.8 3.6 %collective-permute-start.1 = (f32[64,128]{1,0:T(8,128)S(1)}, f32[64,128]{1,0:T(8,128)S(1)}, u32[]{:S(2)}, u32[]{:S(2)}) collective-permute-start(f32[64,128]{1,0:T(8,128)S(1)} %get-tuple-element.30.refs_0_), channel_id=1, source_target_pairs={{0,3},{1,0},{2,1},{3,2},{4,7},{5,4},{6,5},{7,6},{8,11},{9,8},{10,9... | collective-permute-start | bytes 98312 | tf_op jit(solution)/shard_map/ppermute | solution.py:707
  10.4 1.0 %collective-permute-start.3 = (f32[64,128]{1,0:T(8,128)S(1)}, f32[64,128]{1,0:T(8,128)S(1)}, u32[]{:S(2)}, u32[]{:S(2)}) collective-permute-start(f32[64,128]{1,0:T(8,128)S(1)} %get-tuple-element.30.refs_0_), channel_id=1, source_target_pairs={{0,1},{1,2},{2,3},{3,0},{4,5},{5,6},{6,7},{7,4},{8,9},{9,10},{10,1... | collective-permute-start | bytes 98312 | tf_op jit(solution)/shard_map/ppermute | solution.py:707
  11.4 0.2 shard_map.66
  11.7 0.5 %collective-permute-start.6 = (f32[222,128]{1,0:T(8,128)S(1)}, f32[222,128]{1,0:T(8,128)S(1)}, u32[]{:S(2)}, u32[]{:S(2)}) collective-permute-start(f32[222,128]{1,0:T(8,128)S(1)} %get-tuple-element.35), channel_id=1, source_target_pairs={{0,4},{4,8},{8,12},{12,0},{1,5},{5,9},{9,13},{13,1},{2,6},{6,10},{... | collective-permute-start | bytes 341000 | tf_op jit(solution)/shard_map/ppermute | solution.py:707
  12.2 1.6 %shard_map.65 = (f32[27,48,128]{2,1,0:T(8,128)S(1)}, f32[27,8,128]{2,1,0:T(8,128)S(1)}, f32[27,8,128]{2,1,0:T(8,128)S(1)}, f32[3,16,32,128]{3,2,1,0:T(8,128)S(1)}) custom-call(f32[2,29,48,128]{3,2,1,0:T(8,128)S(1)} %get-tuple-element.24.refs_0_, f32[2,29,48,128]{3,2,1,0:T(8,128)S(1)} %get-tuple-element.25.refs_1_, ...), custom_call_target="tpu_custom_call" | custom-call | flops 3449999872 | tf_op jit(solution)/shard_map/pallas_call | solution.py:39
  13.8 1.4 %collective-permute-start.12 = (f32[27,8,128]{2,1,0:T(8,128)S(1)}, f32[27,8,128]{2,1,0:T(8,128)S(1)}, u32[]{:S(2)}, u32[]{:S(2)}) collective-permute-start(f32[27,8,128]{2,1,0:T(8,128)S(1)} %get-tuple-element.39), channel_id=1, source_target_pairs={{0,12},{4,0},{8,4},{12,8},{1,13},{5,1},{9,5},{13,9},{2,14},{6,2},{... | collective-permute-start | bytes 331784 | tf_op jit(solution)/shard_map/ppermute | solution.py:707
  15.2 0.9 %collective-permute-done.3.refs_3_ = f32[64,128]{1,0:T(8,128)S(1)} collective-permute-done((f32[64,128]{1,0:T(8,128)S(1)}, f32[64,128]{1,0:T(8,128)S(1)}, u32[]{:S(2)}, u32[]{:S(2)}) %collective-permute-start.3) | collective-permute-done | bytes 32800 | tf_op jit(solution)/shard_map/ppermute | solution.py:707
  16.3 0.6 %collective-permute-start.4 = (f32[1,10,16,128]{3,2,1,0:T(8,128)S(1)}, f32[1,10,16,128]{3,2,1,0:T(8,128)S(1)}, u32[]{:S(2)}, u32[]{:S(2)}) collective-permute-start(f32[1,10,16,128]{3,2,1,0:T(8,128)S(1)} %shard_map.67.refs_0_), channel_id=1, source_target_pairs={{0,16},{16,0},{1,17},{17,1},{2,18},{18,2},{3,19},{19,3},{4,20},{20... | collective-permute-start | bytes 245768 | tf_op jit(solution)/shard_map/ppermute | solution.py:707
  16.9 0.3 collective-permute-done.6.refs_3_
  17.2 0.3 shard_map.68
  17.5 2.9 %collective-permute-start.10 = (f32[160,128]{1,0:T(8,128)S(1)}, f32[160,128]{1,0:T(8,128)S(1)}, u32[]{:S(2)}, u32[]{:S(2)}) collective-permute-start(f32[160,128]{1,0:T(8,128)S(1)} %get-tuple-element.37), channel_id=1, source_target_pairs={{0,3},{1,0},{2,1},{3,2},{4,7},{5,4},{6,5},{7,6},{8,11},{9,8},{10,9... | collective-permute-start | bytes 245768 | tf_op jit(solution)/shard_map/ppermute | solution.py:707
  20.3 0.2 collective-permute-done.13.below
  20.6 1.0 %collective-permute-start.14 = (f32[13,32,128]{2,1,0:T(8,128)S(1)}, f32[13,32,128]{2,1,0:T(8,128)S(1)}, u32[]{:S(2)}, u32[]{:S(2)}) collective-permute-start(f32[13,32,128]{2,1,0:T(8,128)S(1)} %slice.12), channel_id=1, source_target_pairs={{0,16},{16,0},{1,17},{17,1},{2,18},{18,2},{3,19},{19,3},{4,20},{20... | collective-permute-start | bytes 638984 | tf_op jit(solution)/shard_map/ppermute | solution.py:707
  21.8 1.5 %collective-permute-start.8 = (f32[1,8,16,128]{3,2,1,0:T(8,128)S(1)}, f32[1,8,16,128]{3,2,1,0:T(8,128)S(1)}, u32[]{:S(2)}, u32[]{:S(2)}) collective-permute-start(f32[1,8,16,128]{3,2,1,0:T(8,128)S(1)} %shard_map.69.refs_0_), channel_id=1, source_target_pairs={{0,8},{4,12},{8,0},{12,4},{1,9},{5,13},{9,1},{13,5},{2,10},{6,14},... | collective-permute-start | bytes 196616 | tf_op jit(solution)/shard_map/ppermute | solution.py:707
  23.3 3.5 %collective-permute-done.11.below = f32[160,128]{1,0:T(8,128)S(1)} collective-permute-done((f32[160,128]{1,0:T(8,128)S(1)}, f32[160,128]{1,0:T(8,128)S(1)}, u32[]{:S(2)}, u32[]{:S(2)}) %collective-permute-start.11) | collective-permute-done | bytes 81952 | tf_op jit(solution)/shard_map/ppermute | solution.py:707
  26.8 0.9 %shard_map.70.refs_9_.f1 = f32[12,32,128]{2,1,0:T(8,128)S(1)} custom-call(f32[22,32,128]{2,1,0:T(8,128)S(1)} %get-tuple-element.36.refs_2_.g1, f32[160,128]{1,0:T(8,128)S(1)} %collective-permute-done.10.above, f32[160,128]{1,0:T(8,128)S(1)} %collective-permute-done.11.below), custom_call_target="tpu_custom_call" | custom-call | flops 1035000000 | tf_op jit(solution)/shard_map/pallas_call | solution.py:39
  27.8 2.1 %shard_map.71.e2 = f32[10,16,128]{2,1,0:T(8,128)S(1)} custom-call(f32[1,8,16,128]{3,2,1,0:T(8,128)S(1)} %shard_map.69.refs_0_, f32[1,8,16,128]{3,2,1,0:T(8,128)S(1)} %collective-permute-done.7.refs_1_, f32[1,8,16,128]{3,2,1,0:T(8,128)S(1)} %collective-permute-done.8.refs_2_, f32[1,8,16,128]{3,2,1,0:T(8,128)S(1)} %collective-permute-done.9.refs_3_, ...), custom_call_target="tpu_custom_call" | custom-call | flops 2529999872 | tf_op jit(solution)/shard_map/pallas_call | solution.py:39
  29.9 2.1 %shard_map.72.u0_b = f32[2,24,40,128]{3,2,1,0:T(8,128)S(1)} custom-call(f32[10,16,128]{2,1,0:T(8,128)S(1)} %shard_map.71.e2, f32[12,32,128]{2,1,0:T(8,128)S(1)} %shard_map.70.refs_9_.f1), custom_call_target="tpu_custom_call" | custom-call | flops 2529999872 | tf_op jit(solution)/shard_map/pallas_call | solution.py:39
  32.0 1.9 %shard_map.74.work = f32[17,40,128]{2,1,0:T(8,128)S(1)} custom-call(f32[160,128]{1,0:T(8,128)S(1)} %collective-permute-done.10.above, f32[160,128]{1,0:T(8,128)S(1)} %collective-permute-done.11.below, f32[160,128]{1,0:T(8,128)S(1)} %get-tuple-element.38.own), custom_call_target="tpu_custom_call" | custom-call | flops 2184999936 | tf_op jit(solution)/shard_map/pallas_call | solution.py:39
  33.9 0.3 shard_map.75
  34.2 1.1 %shard_map.76 = f32[3,16,32,128]{3,2,1,0:T(8,128)} custom-call(f32[3,16,32,128]{3,2,1,0:T(8,128)S(1)} %get-tuple-element.29.field, f32[2,24,40,128]{3,2,1,0:T(8,128)S(1)} %shard_map.72.u0_b, f32[17,40,128]{2,1,0:T(8,128)S(1)} %get-tuple-element.41.f0, f32[16,32,128]{2,1,0:T(8,128)S(1)} %get-tuple-element.42.beyond), custom_call_target="tpu_custom_call" | custom-call | flops 1035000000 | tf_op jit(solution)/shard_map/pallas_call | solution.py:39
  (35 shorter events, 0.7 us)
Async XLA Ops:
  0.0 1.1 %copy-start = (f32[3,16,32,128]{3,2,1,0:T(8,128)S(1)}, f32[3,16,32,128]{3,2,1,0:T(8,128)}, u32[]{:S(2)}) copy-start(f32[3,16,32,128]{3,2,1,0:T(8,128)} %refs_4_.2) | copy-start | bytes 2359300
  1.1 11.0 %copy-start.1 = (f32[3,16,32,128]{3,2,1,0:T(8,128)S(1)}, f32[3,16,32,128]{3,2,1,0:T(8,128)}, u32[]{:S(2)}) copy-start(f32[3,16,32,128]{3,2,1,0:T(8,128)} %refs_4_.2) | copy-start | bytes 2359300
  3.8 7.7 %collective-permute-start = (f32[220,128]{1,0:T(8,128)S(1)}, f32[220,128]{1,0:T(8,128)S(1)}, u32[]{:S(2)}, u32[]{:S(2)}) collective-permute-start(f32[220,128]{1,0:T(8,128)S(1)} %get-tuple-element.28.refs_1_.refs_0_), channel_id=1, source_target_pairs={{0,16},{16,0},{1,17},{17,1},{2,18},{18,2},{3,19},{19,3},{4,20},{20... | collective-permute-start | bytes 337928 | tf_op jit(solution)/shard_map/ppermute | solution.py:707
  6.8 7.0 %collective-permute-start.1 = (f32[64,128]{1,0:T(8,128)S(1)}, f32[64,128]{1,0:T(8,128)S(1)}, u32[]{:S(2)}, u32[]{:S(2)}) collective-permute-start(f32[64,128]{1,0:T(8,128)S(1)} %get-tuple-element.30.refs_0_), channel_id=1, source_target_pairs={{0,3},{1,0},{2,1},{3,2},{4,7},{5,4},{6,5},{7,6},{8,11},{9,8},{10,9... | collective-permute-start | bytes 98312 | tf_op jit(solution)/shard_map/ppermute | solution.py:707
  10.4 4.8 %collective-permute-start.2 = (f32[64,128]{1,0:T(8,128)S(1)}, f32[64,128]{1,0:T(8,128)S(1)}, u32[]{:S(2)}, u32[]{:S(2)}) collective-permute-start(f32[64,128]{1,0:T(8,128)S(1)} %get-tuple-element.30.refs_0_), channel_id=1, source_target_pairs={{0,2},{1,3},{2,0},{3,1},{4,6},{5,7},{6,4},{7,5},{8,10},{9,11},{10,... | collective-permute-start | bytes 98312 | tf_op jit(solution)/shard_map/ppermute | solution.py:707
  10.4 5.7 %collective-permute-start.3 = (f32[64,128]{1,0:T(8,128)S(1)}, f32[64,128]{1,0:T(8,128)S(1)}, u32[]{:S(2)}, u32[]{:S(2)}) collective-permute-start(f32[64,128]{1,0:T(8,128)S(1)} %get-tuple-element.30.refs_0_), channel_id=1, source_target_pairs={{0,1},{1,2},{2,3},{3,0},{4,5},{5,6},{6,7},{7,4},{8,9},{9,10},{10,1... | collective-permute-start | bytes 98312 | tf_op jit(solution)/shard_map/ppermute | solution.py:707
  11.6 5.2 %collective-permute-start.5 = (f32[222,128]{1,0:T(8,128)S(1)}, f32[222,128]{1,0:T(8,128)S(1)}, u32[]{:S(2)}, u32[]{:S(2)}) collective-permute-start(f32[222,128]{1,0:T(8,128)S(1)} %get-tuple-element.34), channel_id=1, source_target_pairs={{0,12},{4,0},{8,4},{12,8},{1,13},{5,1},{9,5},{13,9},{2,14},{6,2},{... | collective-permute-start | bytes 341000 | tf_op jit(solution)/shard_map/ppermute | solution.py:707
  11.7 5.5 %collective-permute-start.6 = (f32[222,128]{1,0:T(8,128)S(1)}, f32[222,128]{1,0:T(8,128)S(1)}, u32[]{:S(2)}, u32[]{:S(2)}) collective-permute-start(f32[222,128]{1,0:T(8,128)S(1)} %get-tuple-element.35), channel_id=1, source_target_pairs={{0,4},{4,8},{8,12},{12,0},{1,5},{5,9},{9,13},{13,1},{2,6},{6,10},{... | collective-permute-start | bytes 341000 | tf_op jit(solution)/shard_map/ppermute | solution.py:707
  13.8 6.6 %collective-permute-start.12 = (f32[27,8,128]{2,1,0:T(8,128)S(1)}, f32[27,8,128]{2,1,0:T(8,128)S(1)}, u32[]{:S(2)}, u32[]{:S(2)}) collective-permute-start(f32[27,8,128]{2,1,0:T(8,128)S(1)} %get-tuple-element.39), channel_id=1, source_target_pairs={{0,12},{4,0},{8,4},{12,8},{1,13},{5,1},{9,5},{13,9},{2,14},{6,2},{... | collective-permute-start | bytes 331784 | tf_op jit(solution)/shard_map/ppermute | solution.py:707
  15.2 5.3 %collective-permute-start.13 = (f32[27,8,128]{2,1,0:T(8,128)S(1)}, f32[27,8,128]{2,1,0:T(8,128)S(1)}, u32[]{:S(2)}, u32[]{:S(2)}) collective-permute-start(f32[27,8,128]{2,1,0:T(8,128)S(1)} %get-tuple-element.40), channel_id=1, source_target_pairs={{0,4},{4,8},{8,12},{12,0},{1,5},{5,9},{9,13},{13,1},{2,6},{6,10},{... | collective-permute-start | bytes 331784 | tf_op jit(solution)/shard_map/ppermute | solution.py:707
  16.3 5.3 %collective-permute-start.4 = (f32[1,10,16,128]{3,2,1,0:T(8,128)S(1)}, f32[1,10,16,128]{3,2,1,0:T(8,128)S(1)}, u32[]{:S(2)}, u32[]{:S(2)}) collective-permute-start(f32[1,10,16,128]{3,2,1,0:T(8,128)S(1)} %shard_map.67.refs_0_), channel_id=1, source_target_pairs={{0,16},{16,0},{1,17},{17,1},{2,18},{18,2},{3,19},{19,3},{4,20},{20... | collective-permute-start | bytes 245768 | tf_op jit(solution)/shard_map/ppermute | solution.py:707
  17.5 5.8 %collective-permute-start.10 = (f32[160,128]{1,0:T(8,128)S(1)}, f32[160,128]{1,0:T(8,128)S(1)}, u32[]{:S(2)}, u32[]{:S(2)}) collective-permute-start(f32[160,128]{1,0:T(8,128)S(1)} %get-tuple-element.37), channel_id=1, source_target_pairs={{0,3},{1,0},{2,1},{3,2},{4,7},{5,4},{6,5},{7,6},{8,11},{9,8},{10,9... | collective-permute-start | bytes 245768 | tf_op jit(solution)/shard_map/ppermute | solution.py:707
  20.3 6.5 %collective-permute-start.11 = (f32[160,128]{1,0:T(8,128)S(1)}, f32[160,128]{1,0:T(8,128)S(1)}, u32[]{:S(2)}, u32[]{:S(2)}) collective-permute-start(f32[160,128]{1,0:T(8,128)S(1)} %get-tuple-element.38.own), channel_id=1, source_target_pairs={{0,1},{1,2},{2,3},{3,0},{4,5},{5,6},{6,7},{7,4},{8,9},{9,10},{10,1... | collective-permute-start | bytes 245768 | tf_op jit(solution)/shard_map/ppermute | solution.py:707
  20.6 13.3 %collective-permute-start.14 = (f32[13,32,128]{2,1,0:T(8,128)S(1)}, f32[13,32,128]{2,1,0:T(8,128)S(1)}, u32[]{:S(2)}, u32[]{:S(2)}) collective-permute-start(f32[13,32,128]{2,1,0:T(8,128)S(1)} %slice.12), channel_id=1, source_target_pairs={{0,16},{16,0},{1,17},{17,1},{2,18},{18,2},{3,19},{19,3},{4,20},{20... | collective-permute-start | bytes 638984 | tf_op jit(solution)/shard_map/ppermute | solution.py:707
  21.6 6.2 %copy-start.2 = (f32[1,128,128]{2,1,0:T(8,128)S(1)}, f32[1,128,128]{2,1,0:T(8,128)}, u32[]{:S(2)}) copy-start(f32[1,128,128]{2,1,0:T(8,128)} %constant.12.clone.refs_6_) | copy-start | bytes 196612
  21.6 6.1 %copy-start.3 = (f32[1,128,128]{2,1,0:T(8,128)S(1)}, f32[1,128,128]{2,1,0:T(8,128)}, u32[]{:S(2)}) copy-start(f32[1,128,128]{2,1,0:T(8,128)} %constant.13.clone.refs_7_) | copy-start | bytes 196612
  21.6 6.1 %copy-start.4 = (f32[16,16]{1,0:T(8,128)S(1)}, f32[16,16]{1,0:T(8,128)}, u32[]{:S(2)}) copy-start(f32[16,16]{1,0:T(8,128)} %constant.10.clone.refs_4_) | copy-start | bytes 3076
  21.7 6.1 %copy-start.5 = (f32[16,16]{1,0:T(8,128)S(1)}, f32[16,16]{1,0:T(8,128)}, u32[]{:S(2)}) copy-start(f32[16,16]{1,0:T(8,128)} %constant.11.clone.refs_5_) | copy-start | bytes 3076
  21.7 6.1 %copy-start.6 = (f32[16,128]{1,0:T(8,128)S(1)}, f32[16,128]{1,0:T(8,128)}, u32[]{:S(2)}) copy-start(f32[16,128]{1,0:T(8,128)} %constant.14.clone.refs_8_) | copy-start | bytes 24580
  21.7 6.1 %collective-permute-start.7 = (f32[1,8,16,128]{3,2,1,0:T(8,128)S(1)}, f32[1,8,16,128]{3,2,1,0:T(8,128)S(1)}, u32[]{:S(2)}, u32[]{:S(2)}) collective-permute-start(f32[1,8,16,128]{3,2,1,0:T(8,128)S(1)} %shard_map.69.refs_0_), channel_id=1, source_target_pairs={{0,12},{4,0},{8,4},{12,8},{1,13},{5,1},{9,5},{13,9},{2,14},{6,2},{... | collective-permute-start | bytes 196616 | tf_op jit(solution)/shard_map/ppermute | solution.py:707
  21.8 5.9 %collective-permute-start.8 = (f32[1,8,16,128]{3,2,1,0:T(8,128)S(1)}, f32[1,8,16,128]{3,2,1,0:T(8,128)S(1)}, u32[]{:S(2)}, u32[]{:S(2)}) collective-permute-start(f32[1,8,16,128]{3,2,1,0:T(8,128)S(1)} %shard_map.69.refs_0_), channel_id=1, source_target_pairs={{0,8},{4,12},{8,0},{12,4},{1,9},{5,13},{9,1},{13,5},{2,10},{6,14},... | collective-permute-start | bytes 196616 | tf_op jit(solution)/shard_map/ppermute | solution.py:707
  23.3 4.5 %collective-permute-start.9 = (f32[1,8,16,128]{3,2,1,0:T(8,128)S(1)}, f32[1,8,16,128]{3,2,1,0:T(8,128)S(1)}, u32[]{:S(2)}, u32[]{:S(2)}) collective-permute-start(f32[1,8,16,128]{3,2,1,0:T(8,128)S(1)} %shard_map.69.refs_0_), channel_id=1, source_target_pairs={{0,4},{4,8},{8,12},{12,0},{1,5},{5,9},{9,13},{13,1},{2,6},{6,10},{... | collective-permute-start | bytes 196616 | tf_op jit(solution)/shard_map/ppermute | solution.py:707

commit v6 on v5

--- a/solution.py
+++ b/solution.py
@@ -379,12 +379,18 @@
 
 def window_kernel(g1, above, below, out, base, first, second):
     planes, rows = base.shape[1], base.shape[2]
+    lane = iota((rows, LANES), 1)
+    kept_lanes = ((lane >= 25) & (lane < 34)) | ((lane >= 94) & (lane < 103))
+    turned = []
+    for begin in range(0, rows * -(-planes // 14), rows):
+        turned.append((pltpu.roll(below[begin : begin + rows], 25, 1),
+                       pltpu.roll(above[begin : begin + rows], 94, 1)))
     for p in range(planes):
-        begin = rows * (p // 14)
-        lower = below[begin : begin + rows]
-        upper = above[begin : begin + rows]
-        total = g1[p] + unpacked(lower, p % 14, 9, 0, 9, 25, rows)
-        base[0, p] = total + unpacked(upper, p % 14, 9, 0, 9, 94, rows)
+        lower, upper = turned[p // 14]
+        shift = 9 * (p % 14)
+        term = jnp.where(((lane - shift) & (LANES - 1)) < 64, lower, upper)
+        term = pltpu.roll(term, (LANES - shift) % LANES, 1) if shift else term
+        base[0, p] = g1[p] + jnp.where(kept_lanes, term, 0.0)
     seventh = 1.0 / 7.0
     sweep(first, base, 1, planes - 1, base, seventh)
     sweep(second, first, 2, planes - 2, base, seventh)
@@ -422,6 +428,16 @@
     return out
 
 
+def swept(values):
+    rows = values[0].shape[0]
+    out = []
+    for p, v in enumerate(values):
+        total = v + (values[p - 1] + values[(p + 1) % len(values)])
+        total = total + (pltpu.roll(v, 1, 0) + pltpu.roll(v, rows - 1, 0))
+        out.append((total + (pltpu.roll(v, 1, 1) + pltpu.roll(v, LANES - 1, 1))) * (1.0 / 7.0))
+    return out
+
+
 def real_waves(count):
     cells = np.arange(count)
     rows, eigenvalues = [], []
@@ -441,7 +457,7 @@
     wave_x, value_x = real_waves(planes)
     wave_y, value_y = real_waves(rows)
     wave_z, value_z = real_waves(width)
-    into = np.kron(wave_x, np.repeat(wave_y, 1, axis=1))
+    into = np.kron(np.repeat(wave_x, 2, axis=1), np.repeat(wave_y, 2, axis=1))
     level_values = value_x[:, None, None] + value_y[None, :, None] + value_z[None, None, :]
     factor = (1.0 + level_values) / 7.0
     total = sum(factor**k for k in range(COARSE_ITERS)) * weight(LEVELS - 1) * 0.125
@@ -461,12 +477,8 @@
 
 
 def solve_last(values, into, back, to_waves, from_waves, scale):
-    total = None
-    for t, value in enumerate(values):
-        term = dot(dot(into[...], value), to_waves[t])
-        total = term if total is None else total + term
-    total = dot(back[...], total * scale[...])
-    return [dot(total, from_waves[t]) for t in range(len(values))]
+    waves = dot(dot(into[...], values), to_waves[0])
+    return dot(dot(back[...], waves * scale[...]), from_waves[0])
 
 
 def solve(level, width, buffers, spectral):
@@ -474,6 +486,18 @@
     tiles, planes, rows = g.shape[0], g.shape[1], g.shape[2]
     seventh = 1.0 / 7.0
     w = weight(level)
+    if level == LEVELS - 2:
+        source = [g[0, p] for p in range(planes)]
+        first = swept(source)
+        second = swept(first)
+        third = swept(second)
+        before = [(x + y + z) * w for x, y, z in zip(source, first, second)]
+        values = solve_last(jnp.concatenate(third, axis=0), *spectral)
+        error = [before[p] + values[rows * p : rows * (p + 1)] for p in range(planes)]
+        error = swept(swept(swept(error)))
+        for p in range(planes):
+            g[0, p] = before[p] + error[p]
+        return
     sweep(a, g, 0, planes, None, seventh, planes)
     sweep(b, a, 0, planes, None, seventh, planes)
     for t in range(tiles):
@@ -491,20 +515,17 @@
             total = total + a[t, 2 * c + 1, pl.ds(1, half, stride=2), :]
             parts.append(total)
         values.append(jnp.concatenate(parts, axis=0))
-    if level == LEVELS - 2:
-        values = solve_last(values, *spectral)
-    else:
-        coarse = buffers[level + 1][0]
-        values = restrict_lanes(values, width, width // 2, coarse.shape[0])
-        for t, value in enumerate(values):
-            for c in range(planes // 2):
-                coarse[t, c] = value[half * c : half * (c + 1)] * 0.125
-        solve(level + 1, width // 2, buffers, spectral)
-        values = [
-            jnp.concatenate([coarse[t, c] for c in range(planes // 2)], axis=0)
-            for t in range(coarse.shape[0])
-        ]
-        values = prolong_lanes(values, width, tiles)
+    coarse = buffers[level + 1][0]
+    values = restrict_lanes(values, width, width // 2, coarse.shape[0])
+    for t, value in enumerate(values):
+        for c in range(planes // 2):
+            coarse[t, c] = value[half * c : half * (c + 1)] * 0.125
+    solve(level + 1, width // 2, buffers, spectral)
+    values = [
+        jnp.concatenate([coarse[t, c] for c in range(planes // 2)], axis=0)
+        for t in range(coarse.shape[0])
+    ]
+    values = prolong_lanes(values, width, tiles)
     for t, value in enumerate(values):
         for c in range(planes // 2):
             part = value[half * c : half * (c + 1)]
@@ -613,29 +634,45 @@
         up[k] = total[40:48]
 
 
-EDGE = 64
-BEYOND = 96
-
-
-def fine_edge_kernel(sources, above, below, own, out, base, first, second):
-    planes, rows = out.shape[0] - 1, base.shape[2]
+GROUPS = 3
+GROUP_LANES = 42
+LOW_END, HIGH_AT, OWN_AT = 5, 16, 22
+
+
+def fine_edge_kernel(sources, planes, above, below, own, out, base, first, second):
+    rows = base.shape[2]
+    size = out.shape[0]
     lane = iota((rows, LANES), 1)
     strips = 1 + max(index for index, offset in sources)
     start = above.shape[0] - rows * strips
-    for k in range(base.shape[1]):
+    turned = []
+    for index in range(strips):
+        begin = start + rows * index
+        turned.append((below[begin : begin + rows],
+                       pltpu.roll(above[begin : begin + rows], HIGH_AT, 1),
+                       pltpu.roll(own[begin : begin + rows], OWN_AT, 1)))
+    spread = SPILL + 1
+    for j in range(base.shape[1]):
         value = jnp.zeros((rows, LANES), F32)
-        for index, offset in sources:
-            i = k - SPILL - offset * planes
-            if not 0 <= i <= planes:
+        for q in range(GROUPS):
+            total = None
+            for index, offset in sources:
+                i = size * q + j - SPILL - offset * planes
+                if not 0 <= i <= planes:
+                    continue
+                low, high, last = turned[index]
+                place = (lane - 7 * i) & (LANES - 1)
+                term = jnp.where(place < OWN_AT, jnp.where(place < HIGH_AT, low, high), last)
+                shift = (GROUP_LANES * q - 7 * i) % LANES
+                term = pltpu.roll(term, shift, 1) if shift else term
+                total = term if total is None else total + term
+            if total is None:
                 continue
-            begin = start + rows * index
-            turned = pltpu.roll(below[begin : begin + rows], (LANES - SPILL - 7 * i) % LANES, 1)
-            value = value + jnp.where((lane >= LANES - SPILL) | (lane == 0), turned, 0.0)
-            turned = pltpu.roll(above[begin : begin + rows], (EDGE - 7 * i) % LANES, 1)
-            value = value + jnp.where((lane >= EDGE) & (lane <= EDGE + SPILL), turned, 0.0)
-            turned = pltpu.roll(own[begin : begin + rows], (BEYOND - SPILL - 7 * i) % LANES, 1)
-            value = value + jnp.where((lane >= BEYOND - SPILL) & (lane <= BEYOND), turned, 0.0)
-        base[0, k] = value
+            place = lane - GROUP_LANES * q
+            inside = (place >= 0) & (place < OWN_AT + spread)
+            inside = inside & ((place < spread) | (place >= HIGH_AT))
+            value = jnp.where(inside, total, value)
+        base[0, j] = value
     seventh = 1.0 / 7.0
     high = base.shape[1]
     sweep(first, base, 1, high - 1, base, seventh)
@@ -643,14 +680,21 @@
     sweep(first, second, 3, high - 3, base, seventh)
     sweep(second, first, 4, high - 4, base, seventh)
     kept = out.shape[1]
-    for i in range(planes + 1):
+    for i in range(size):
         p = SPILL + i
         value = (seven_sum(second, p, p - 1, p + 1)[0] * seventh + base[0, p]) * weight(0)
         out[i] = value[ROW0 : ROW0 + kept]
 
 
+def edge_sides(part, q):
+    lane = iota(part.shape, 1)
+    low = pltpu.roll(part, (-GROUP_LANES * q - LOW_END) % LANES, 1)
+    high = pltpu.roll(part, (LANES - SPILL - GROUP_LANES * q - LOW_END - 6) % LANES, 1)
+    return jnp.where(lane <= SPILL, low, jnp.where(lane >= LANES - SPILL, high, 0.0))
+
+
 def turned_to_last(value, lane):
-    return pltpu.roll(value, LANES - 1 - lane, 1)
+    return pltpu.roll(value, (LANES - 1 - lane) % LANES, 1)
 
 
 def fine_sum_kernel(f0, below_x, above_x, work, out, beyond):
@@ -663,20 +707,19 @@
             value = value + below_x[1 + i]
         if i >= planes - SPILL:
             value = value + above_x[i - (planes - SPILL)]
-        part = work[i, 0:rows]
-        turned = pltpu.roll(part, EDGE, 1)
-        value = value + jnp.where(lane <= SPILL, part, 0.0)
-        out[i, 0:rows] = value + jnp.where(lane >= LANES - SPILL, turned, 0.0)
+        q, m = i // work.shape[0], i % work.shape[0]
+        part = work[m, 0:rows]
+        out[i, 0:rows] = value + edge_sides(part, q)
         if i < planes:
-            beyond[i] = turned_to_last(part, EDGE) + turned_to_last(part, BEYOND)
+            first = GROUP_LANES * q
+            last = turned_to_last(part, first + HIGH_AT)
+            beyond[i] = last + turned_to_last(part, first + OWN_AT + SPILL)
             row = f0[6, i + SPILL : i + SPILL + 1]
             if i <= SPILL:
                 row = row + below_x[0, i + SPILL + planes : i + SPILL + planes + 1]
             if i >= planes - SPILL:
                 row = row + above_x[6, i + SPILL - planes : i + SPILL - planes + 1]
-            part = work[i, rows : rows + 1]
-            row = row + jnp.where(lane1 <= SPILL, part, 0.0)
-            row = row + jnp.where(lane1 >= LANES - SPILL, pltpu.roll(part, EDGE, 1), 0.0)
+            row = row + edge_sides(work[m, rows : rows + 1], q)
             out[i, rows : rows + 1] = row
 
 
@@ -796,6 +839,7 @@
         [(share0, rows0, LANES)],
         0.4,
         main, f_above, f_below,
+        after=(g2,),
     )
     if size_x == 2:
         other = from_offset(f0[0:13], "gx", 1)
@@ -803,10 +847,11 @@
     else:
         f_above = from_offset(f0[0:7], "gx", 1)
         f_below = from_offset(f0[6:13], "gx", -1)
-    edges = (1, nx + 11, rows0, LANES)
+    group = -(-(nx + 1) // GROUPS)
+    edges = (1, group + 2 * SPILL, rows0, LANES)
     edge = call(
-        functools.partial(fine_edge_kernel, tuple(sources[:3])),
-        shape(nx + 1, ny + 8, LANES),
+        functools.partial(fine_edge_kernel, tuple(sources[:3]), nx),
+        shape(group, ny + 8, LANES),
         [edges, edges, edges],
         1.9,
         above, below, up,

time: 35.5 us -> 34.7 us (0.977)
  Pallas kernels: 13.4 us -> 12.6 us
    pallas_call x13, Pallas kernels: 13.4 us -> 12.6 us  [call(): pl.pallas_call(kernel, out_shape=outs, scratch_shapes=[pltpu.VMEM(s, F32)...]
  transfers between devices with their start and end apart: 15 -> 15, of which waited for: 5 -> 5; matrix products, arithmetic and copies ran while one was open for 0% -> 0% of each run, Pallas kernels for 26% -> 24%
where the time goes in v6:
time: 34.7 us; the launch traced here: 34.6 us
  starting transfers between devices  15.6 us (45%)
  Pallas kernels  12.6 us (36%)
  waiting for transfers between devices  4.97 us (14%)
  local copies, waits for them, and re-layouts  1.2 us (3%)
    ppermute x15, starting transfers between devices, from_offset(): return lax.ppermute(value, axis, pairs)  15.6 us
    pallas_call x13, Pallas kernels, call(): pl.pallas_call(kernel, out_shape=outs, scratch_shapes=[pltpu.VMEM(s, F32)...  12.6 us
    ppermute x15, waiting for transfers between devices, from_offset(): return lax.ppermute(value, axis, pairs)  4.97 us
    unnamed x14, local copies, waits for them, and re-layouts  1.17 us
  transfers between devices with their start and end apart: 15, of which 5 were waited for; matrix products, arithmetic and copies ran while one was open for 0% of the time, Pallas kernels for 24%

profile of v6, /device:TPU:0, one launch (start us, length us, event | category | flops | bytes accessed | tf_op | source)
XLA Modules:
  0.0 34.6 jit_solution(1928953879712624119)
XLA Ops:
  0.0 1.1 %copy-done = f32[3,16,32,128]{3,2,1,0:T(8,128)S(1)} copy-done((f32[3,16,32,128]{3,2,1,0:T(8,128)S(1)}, f32[3,16,32,128]{3,2,1,0:T(8,128)}, u32[]{:S(2)}) %copy-start) | copy-done | bytes 786456
  1.1 2.6 %shard_map.64 = (f32[220,128]{1,0:T(8,128)S(1)}, f32[64,128]{1,0:T(8,128)S(1)}, f32[12,24,128]{2,1,0:T(8,128)S(1)}, f32[2,29,48,128]{3,2,1,0:T(8,128)S(1)}, f32[...) custom-call(f32[3,16,32,128]{3,2,1,0:T(8,128)S(1)} %copy-done), custom_call_target="tpu_custom_call" | custom-call | flops 3335000064 | tf_op jit(solution)/shard_map/pallas_call | solution.py:39
  3.8 3.0 %collective-permute-start = (f32[220,128]{1,0:T(8,128)S(1)}, f32[220,128]{1,0:T(8,128)S(1)}, u32[]{:S(2)}, u32[]{:S(2)}) collective-permute-start(f32[220,128]{1,0:T(8,128)S(1)} %get-tuple-element.28.refs_1_.refs_0_), channel_id=1, source_target_pairs={{0,16},{16,0},{1,17},{17,1},{2,18},{18,2},{3,19},{19,3},{4,20},{20... | collective-permute-start | bytes 337928 | tf_op jit(solution)/shard_map/ppermute | solution.py:750
  6.8 3.6 %collective-permute-start.1 = (f32[64,128]{1,0:T(8,128)S(1)}, f32[64,128]{1,0:T(8,128)S(1)}, u32[]{:S(2)}, u32[]{:S(2)}) collective-permute-start(f32[64,128]{1,0:T(8,128)S(1)} %get-tuple-element.30.refs_0_), channel_id=1, source_target_pairs={{0,3},{1,0},{2,1},{3,2},{4,7},{5,4},{6,5},{7,6},{8,11},{9,8},{10,9... | collective-permute-start | bytes 98312 | tf_op jit(solution)/shard_map/ppermute | solution.py:750
  10.4 1.0 %collective-permute-start.3 = (f32[64,128]{1,0:T(8,128)S(1)}, f32[64,128]{1,0:T(8,128)S(1)}, u32[]{:S(2)}, u32[]{:S(2)}) collective-permute-start(f32[64,128]{1,0:T(8,128)S(1)} %get-tuple-element.30.refs_0_), channel_id=1, source_target_pairs={{0,1},{1,2},{2,3},{3,0},{4,5},{5,6},{6,7},{7,4},{8,9},{9,10},{10,1... | collective-permute-start | bytes 98312 | tf_op jit(solution)/shard_map/ppermute | solution.py:750
  11.4 0.2 shard_map.66
  11.7 0.5 %collective-permute-start.6 = (f32[222,128]{1,0:T(8,128)S(1)}, f32[222,128]{1,0:T(8,128)S(1)}, u32[]{:S(2)}, u32[]{:S(2)}) collective-permute-start(f32[222,128]{1,0:T(8,128)S(1)} %get-tuple-element.35), channel_id=1, source_target_pairs={{0,4},{4,8},{8,12},{12,0},{1,5},{5,9},{9,13},{13,1},{2,6},{6,10},{... | collective-permute-start | bytes 341000 | tf_op jit(solution)/shard_map/ppermute | solution.py:750
  12.2 1.6 %shard_map.65 = (f32[27,48,128]{2,1,0:T(8,128)S(1)}, f32[27,8,128]{2,1,0:T(8,128)S(1)}, f32[27,8,128]{2,1,0:T(8,128)S(1)}, f32[3,16,32,128]{3,2,1,0:T(8,128)S(1)}) custom-call(f32[2,29,48,128]{3,2,1,0:T(8,128)S(1)} %get-tuple-element.24.refs_0_, f32[2,29,48,128]{3,2,1,0:T(8,128)S(1)} %get-tuple-element.25.refs_1_, ...), custom_call_target="tpu_custom_call" | custom-call | flops 3449999872 | tf_op jit(solution)/shard_map/pallas_call | solution.py:39
  13.8 1.4 %collective-permute-start.12 = (f32[27,8,128]{2,1,0:T(8,128)S(1)}, f32[27,8,128]{2,1,0:T(8,128)S(1)}, u32[]{:S(2)}, u32[]{:S(2)}) collective-permute-start(f32[27,8,128]{2,1,0:T(8,128)S(1)} %get-tuple-element.39), channel_id=1, source_target_pairs={{0,12},{4,0},{8,4},{12,8},{1,13},{5,1},{9,5},{13,9},{2,14},{6,2},{... | collective-permute-start | bytes 331784 | tf_op jit(solution)/shard_map/ppermute | solution.py:750
  15.2 0.9 %collective-permute-done.3.refs_3_ = f32[64,128]{1,0:T(8,128)S(1)} collective-permute-done((f32[64,128]{1,0:T(8,128)S(1)}, f32[64,128]{1,0:T(8,128)S(1)}, u32[]{:S(2)}, u32[]{:S(2)}) %collective-permute-start.3) | collective-permute-done | bytes 32800 | tf_op jit(solution)/shard_map/ppermute | solution.py:750
  16.3 0.6 %collective-permute-start.4 = (f32[1,10,16,128]{3,2,1,0:T(8,128)S(1)}, f32[1,10,16,128]{3,2,1,0:T(8,128)S(1)}, u32[]{:S(2)}, u32[]{:S(2)}) collective-permute-start(f32[1,10,16,128]{3,2,1,0:T(8,128)S(1)} %shard_map.67.refs_0_), channel_id=1, source_target_pairs={{0,16},{16,0},{1,17},{17,1},{2,18},{18,2},{3,19},{19,3},{4,20},{20... | collective-permute-start | bytes 245768 | tf_op jit(solution)/shard_map/ppermute | solution.py:750
  16.9 0.3 collective-permute-done.6.refs_3_
  17.2 0.3 shard_map.68
  17.5 2.9 %collective-permute-start.10 = (f32[160,128]{1,0:T(8,128)S(1)}, f32[160,128]{1,0:T(8,128)S(1)}, u32[]{:S(2)}, u32[]{:S(2)}) collective-permute-start(f32[160,128]{1,0:T(8,128)S(1)} %get-tuple-element.37), channel_id=1, source_target_pairs={{0,3},{1,0},{2,1},{3,2},{4,7},{5,4},{6,5},{7,6},{8,11},{9,8},{10,9... | collective-permute-start | bytes 245768 | tf_op jit(solution)/shard_map/ppermute | solution.py:750
  20.3 1.1 %collective-permute-done.4.refs_1_ = f32[1,10,16,128]{3,2,1,0:T(8,128)S(1)} collective-permute-done((f32[1,10,16,128]{3,2,1,0:T(8,128)S(1)}, f32[1,10,16,128]{3,2,1,0:T(8,128)S(1)}, u32[]{:S(2)}, u32[]{:S(2)}) %collective-permute-start.4) | collective-permute-done | bytes 81952 | tf_op jit(solution)/shard_map/ppermute | solution.py:750
  21.5 1.5 %collective-permute-start.8 = (f32[1,8,16,128]{3,2,1,0:T(8,128)S(1)}, f32[1,8,16,128]{3,2,1,0:T(8,128)S(1)}, u32[]{:S(2)}, u32[]{:S(2)}) collective-permute-start(f32[1,8,16,128]{3,2,1,0:T(8,128)S(1)} %shard_map.69.refs_0_.refs_3_), channel_id=1, source_target_pairs={{0,8},{4,12},{8,0},{12,4},{1,9},{5,13},{9,1},{13,5},{2,10},{6,14},... | collective-permute-start | bytes 196616 | tf_op jit(solution)/shard_map/ppermute | solution.py:750
  23.2 1.0 %collective-permute-start.14 = (f32[13,32,128]{2,1,0:T(8,128)S(1)}, f32[13,32,128]{2,1,0:T(8,128)S(1)}, u32[]{:S(2)}, u32[]{:S(2)}) collective-permute-start(f32[13,32,128]{2,1,0:T(8,128)S(1)} %slice.12), channel_id=1, source_target_pairs={{0,16},{16,0},{1,17},{17,1},{2,18},{18,2},{3,19},{19,3},{4,20},{20... | collective-permute-start | bytes 638984 | tf_op jit(solution)/shard_map/ppermute | solution.py:750
  24.2 2.6 %collective-permute-done.11.below = f32[160,128]{1,0:T(8,128)S(1)} collective-permute-done((f32[160,128]{1,0:T(8,128)S(1)}, f32[160,128]{1,0:T(8,128)S(1)}, u32[]{:S(2)}, u32[]{:S(2)}) %collective-permute-start.11) | collective-permute-done | bytes 81952 | tf_op jit(solution)/shard_map/ppermute | solution.py:750
  26.8 0.9 %shard_map.70.refs_9_.f1 = f32[12,32,128]{2,1,0:T(8,128)S(1)} custom-call(f32[22,32,128]{2,1,0:T(8,128)S(1)} %get-tuple-element.36.refs_2_.g1, f32[160,128]{1,0:T(8,128)S(1)} %collective-permute-done.10.above, f32[160,128]{1,0:T(8,128)S(1)} %collective-permute-done.11.below), custom_call_target="tpu_custom_call" | custom-call | flops 1035000000 | tf_op jit(solution)/shard_map/pallas_call | solution.py:39
  27.8 2.1 %shard_map.71.e2 = f32[10,16,128]{2,1,0:T(8,128)S(1)} custom-call(f32[1,8,16,128]{3,2,1,0:T(8,128)S(1)} %shard_map.69.refs_0_.refs_3_, f32[1,8,16,128]{3,2,1,0:T(8,128)S(1)} %collective-permute-done.7.refs_1_, f32[1,8,16,128]{3,2,1,0:T(8,128)S(1)} %collective-permute-done.8.refs_2_, f32[1,8,16,128]{3,2,1,0:T(8,128)S(1)} %collective-permute-done.9.refs_3_, ...), custom_call_target="tpu_custom_call" | custom-call | flops 2529999872 | tf_op jit(solution)/shard_map/pallas_call | solution.py:39
  29.9 2.1 %shard_map.72.u0_b = f32[2,24,40,128]{3,2,1,0:T(8,128)S(1)} custom-call(f32[10,16,128]{2,1,0:T(8,128)S(1)} %shard_map.71.e2, f32[12,32,128]{2,1,0:T(8,128)S(1)} %shard_map.70.refs_9_.f1), custom_call_target="tpu_custom_call" | custom-call | flops 2529999872 | tf_op jit(solution)/shard_map/pallas_call | solution.py:39
  32.0 1.1 %shard_map.74.work = f32[6,40,128]{2,1,0:T(8,128)S(1)} custom-call(f32[160,128]{1,0:T(8,128)S(1)} %collective-permute-done.10.above, f32[160,128]{1,0:T(8,128)S(1)} %collective-permute-done.11.below, f32[160,128]{1,0:T(8,128)S(1)} %get-tuple-element.38.own), custom_call_target="tpu_custom_call" | custom-call | flops 2184999936 | tf_op jit(solution)/shard_map/pallas_call | solution.py:39
  33.1 0.4 %shard_map.75 = (f32[17,40,128]{2,1,0:T(8,128)S(1)}, f32[16,32,128]{2,1,0:T(8,128)S(1)}) custom-call(f32[28,32,128]{2,1,0:T(8,128)S(1)} %shard_map.73.f0, f32[7,32,128]{2,1,0:T(8,128)S(1)} %get-tuple-element.44.below_x, f32[7,32,128]{2,1,0:T(8,128)S(1)} %get-tuple-element.43.above_x, f32[6,40,128]{2,1,0:T(8,128)S(1)} %shard_map.74.work), custom_call_target="tpu_custom_call" | custom-call | flops 345000000 | tf_op jit(solution)/shard_map/pallas_call | solution.py:39
  33.5 1.1 %shard_map.76 = f32[3,16,32,128]{3,2,1,0:T(8,128)} custom-call(f32[3,16,32,128]{3,2,1,0:T(8,128)S(1)} %get-tuple-element.29.field, f32[2,24,40,128]{3,2,1,0:T(8,128)S(1)} %shard_map.72.u0_b, f32[17,40,128]{2,1,0:T(8,128)S(1)} %get-tuple-element.41.f0, f32[16,32,128]{2,1,0:T(8,128)S(1)} %get-tuple-element.42.beyond), custom_call_target="tpu_custom_call" | custom-call | flops 1035000000 | tf_op jit(solution)/shard_map/pallas_call | solution.py:39
  (35 shorter events, 0.6 us)
Async XLA Ops:
  0.0 1.1 %copy-start = (f32[3,16,32,128]{3,2,1,0:T(8,128)S(1)}, f32[3,16,32,128]{3,2,1,0:T(8,128)}, u32[]{:S(2)}) copy-start(f32[3,16,32,128]{3,2,1,0:T(8,128)} %refs_4_.2) | copy-start | bytes 2359300
  1.1 11.0 %copy-start.1 = (f32[3,16,32,128]{3,2,1,0:T(8,128)S(1)}, f32[3,16,32,128]{3,2,1,0:T(8,128)}, u32[]{:S(2)}) copy-start(f32[3,16,32,128]{3,2,1,0:T(8,128)} %refs_4_.2) | copy-start | bytes 2359300
  3.8 7.7 %collective-permute-start = (f32[220,128]{1,0:T(8,128)S(1)}, f32[220,128]{1,0:T(8,128)S(1)}, u32[]{:S(2)}, u32[]{:S(2)}) collective-permute-start(f32[220,128]{1,0:T(8,128)S(1)} %get-tuple-element.28.refs_1_.refs_0_), channel_id=1, source_target_pairs={{0,16},{16,0},{1,17},{17,1},{2,18},{18,2},{3,19},{19,3},{4,20},{20... | collective-permute-start | bytes 337928 | tf_op jit(solution)/shard_map/ppermute | solution.py:750
  6.8 7.0 %collective-permute-start.1 = (f32[64,128]{1,0:T(8,128)S(1)}, f32[64,128]{1,0:T(8,128)S(1)}, u32[]{:S(2)}, u32[]{:S(2)}) collective-permute-start(f32[64,128]{1,0:T(8,128)S(1)} %get-tuple-element.30.refs_0_), channel_id=1, source_target_pairs={{0,3},{1,0},{2,1},{3,2},{4,7},{5,4},{6,5},{7,6},{8,11},{9,8},{10,9... | collective-permute-start | bytes 98312 | tf_op jit(solution)/shard_map/ppermute | solution.py:750
  10.4 4.8 %collective-permute-start.2 = (f32[64,128]{1,0:T(8,128)S(1)}, f32[64,128]{1,0:T(8,128)S(1)}, u32[]{:S(2)}, u32[]{:S(2)}) collective-permute-start(f32[64,128]{1,0:T(8,128)S(1)} %get-tuple-element.30.refs_0_), channel_id=1, source_target_pairs={{0,2},{1,3},{2,0},{3,1},{4,6},{5,7},{6,4},{7,5},{8,10},{9,11},{10,... | collective-permute-start | bytes 98312 | tf_op jit(solution)/shard_map/ppermute | solution.py:750
  10.4 5.7 %collective-permute-start.3 = (f32[64,128]{1,0:T(8,128)S(1)}, f32[64,128]{1,0:T(8,128)S(1)}, u32[]{:S(2)}, u32[]{:S(2)}) collective-permute-start(f32[64,128]{1,0:T(8,128)S(1)} %get-tuple-element.30.refs_0_), channel_id=1, source_target_pairs={{0,1},{1,2},{2,3},{3,0},{4,5},{5,6},{6,7},{7,4},{8,9},{9,10},{10,1... | collective-permute-start | bytes 98312 | tf_op jit(solution)/shard_map/ppermute | solution.py:750
  11.6 5.2 %collective-permute-start.5 = (f32[222,128]{1,0:T(8,128)S(1)}, f32[222,128]{1,0:T(8,128)S(1)}, u32[]{:S(2)}, u32[]{:S(2)}) collective-permute-start(f32[222,128]{1,0:T(8,128)S(1)} %get-tuple-element.34), channel_id=1, source_target_pairs={{0,12},{4,0},{8,4},{12,8},{1,13},{5,1},{9,5},{13,9},{2,14},{6,2},{... | collective-permute-start | bytes 341000 | tf_op jit(solution)/shard_map/ppermute | solution.py:750
  11.7 5.5 %collective-permute-start.6 = (f32[222,128]{1,0:T(8,128)S(1)}, f32[222,128]{1,0:T(8,128)S(1)}, u32[]{:S(2)}, u32[]{:S(2)}) collective-permute-start(f32[222,128]{1,0:T(8,128)S(1)} %get-tuple-element.35), channel_id=1, source_target_pairs={{0,4},{4,8},{8,12},{12,0},{1,5},{5,9},{9,13},{13,1},{2,6},{6,10},{... | collective-permute-start | bytes 341000 | tf_op jit(solution)/shard_map/ppermute | solution.py:750
  13.8 7.7 %collective-permute-start.12 = (f32[27,8,128]{2,1,0:T(8,128)S(1)}, f32[27,8,128]{2,1,0:T(8,128)S(1)}, u32[]{:S(2)}, u32[]{:S(2)}) collective-permute-start(f32[27,8,128]{2,1,0:T(8,128)S(1)} %get-tuple-element.39), channel_id=1, source_target_pairs={{0,12},{4,0},{8,4},{12,8},{1,13},{5,1},{9,5},{13,9},{2,14},{6,2},{... | collective-permute-start | bytes 331784 | tf_op jit(solution)/shard_map/ppermute | solution.py:750
  15.2 7.7 %collective-permute-start.13 = (f32[27,8,128]{2,1,0:T(8,128)S(1)}, f32[27,8,128]{2,1,0:T(8,128)S(1)}, u32[]{:S(2)}, u32[]{:S(2)}) collective-permute-start(f32[27,8,128]{2,1,0:T(8,128)S(1)} %get-tuple-element.40), channel_id=1, source_target_pairs={{0,4},{4,8},{8,12},{12,0},{1,5},{5,9},{9,13},{13,1},{2,6},{6,10},{... | collective-permute-start | bytes 331784 | tf_op jit(solution)/shard_map/ppermute | solution.py:750
  16.3 5.1 %collective-permute-start.4 = (f32[1,10,16,128]{3,2,1,0:T(8,128)S(1)}, f32[1,10,16,128]{3,2,1,0:T(8,128)S(1)}, u32[]{:S(2)}, u32[]{:S(2)}) collective-permute-start(f32[1,10,16,128]{3,2,1,0:T(8,128)S(1)} %shard_map.67.refs_0_), channel_id=1, source_target_pairs={{0,16},{16,0},{1,17},{17,1},{2,18},{18,2},{3,19},{19,3},{4,20},{20... | collective-permute-start | bytes 245768 | tf_op jit(solution)/shard_map/ppermute | solution.py:750
  17.5 5.7 %collective-permute-start.10 = (f32[160,128]{1,0:T(8,128)S(1)}, f32[160,128]{1,0:T(8,128)S(1)}, u32[]{:S(2)}, u32[]{:S(2)}) collective-permute-start(f32[160,128]{1,0:T(8,128)S(1)} %get-tuple-element.37), channel_id=1, source_target_pairs={{0,3},{1,0},{2,1},{3,2},{4,7},{5,4},{6,5},{7,6},{8,11},{9,8},{10,9... | collective-permute-start | bytes 245768 | tf_op jit(solution)/shard_map/ppermute | solution.py:750
  20.3 6.5 %collective-permute-start.11 = (f32[160,128]{1,0:T(8,128)S(1)}, f32[160,128]{1,0:T(8,128)S(1)}, u32[]{:S(2)}, u32[]{:S(2)}) collective-permute-start(f32[160,128]{1,0:T(8,128)S(1)} %get-tuple-element.38.own), channel_id=1, source_target_pairs={{0,1},{1,2},{2,3},{3,0},{4,5},{5,6},{6,7},{7,4},{8,9},{9,10},{10,1... | collective-permute-start | bytes 245768 | tf_op jit(solution)/shard_map/ppermute | solution.py:750
  21.4 6.3 %collective-permute-start.7 = (f32[1,8,16,128]{3,2,1,0:T(8,128)S(1)}, f32[1,8,16,128]{3,2,1,0:T(8,128)S(1)}, u32[]{:S(2)}, u32[]{:S(2)}) collective-permute-start(f32[1,8,16,128]{3,2,1,0:T(8,128)S(1)} %shard_map.69.refs_0_.refs_3_), channel_id=1, source_target_pairs={{0,12},{4,0},{8,4},{12,8},{1,13},{5,1},{9,5},{13,9},{2,14},{6,2},{... | collective-permute-start | bytes 196616 | tf_op jit(solution)/shard_map/ppermute | solution.py:750
  21.5 6.2 %collective-permute-start.8 = (f32[1,8,16,128]{3,2,1,0:T(8,128)S(1)}, f32[1,8,16,128]{3,2,1,0:T(8,128)S(1)}, u32[]{:S(2)}, u32[]{:S(2)}) collective-permute-start(f32[1,8,16,128]{3,2,1,0:T(8,128)S(1)} %shard_map.69.refs_0_.refs_3_), channel_id=1, source_target_pairs={{0,8},{4,12},{8,0},{12,4},{1,9},{5,13},{9,1},{13,5},{2,10},{6,14},... | collective-permute-start | bytes 196616 | tf_op jit(solution)/shard_map/ppermute | solution.py:750
  23.0 4.8 %collective-permute-start.9 = (f32[1,8,16,128]{3,2,1,0:T(8,128)S(1)}, f32[1,8,16,128]{3,2,1,0:T(8,128)S(1)}, u32[]{:S(2)}, u32[]{:S(2)}) collective-permute-start(f32[1,8,16,128]{3,2,1,0:T(8,128)S(1)} %shard_map.69.refs_0_.refs_3_), channel_id=1, source_target_pairs={{0,4},{4,8},{8,12},{12,0},{1,5},{5,9},{9,13},{13,1},{2,6},{6,10},{... | collective-permute-start | bytes 196616 | tf_op jit(solution)/shard_map/ppermute | solution.py:750
  23.1 4.7 %copy-start.2 = (f32[1,128,128]{2,1,0:T(8,128)S(1)}, f32[1,128,128]{2,1,0:T(8,128)}, u32[]{:S(2)}) copy-start(f32[1,128,128]{2,1,0:T(8,128)} %constant.12.clone.refs_6_) | copy-start | bytes 196612
  23.1 4.7 %copy-start.3 = (f32[1,128,128]{2,1,0:T(8,128)S(1)}, f32[1,128,128]{2,1,0:T(8,128)}, u32[]{:S(2)}) copy-start(f32[1,128,128]{2,1,0:T(8,128)} %constant.13.clone.refs_7_) | copy-start | bytes 196612
  23.1 4.7 %copy-start.4 = (f32[64,16]{1,0:T(8,128)S(1)}, f32[64,16]{1,0:T(8,128)}, u32[]{:S(2)}) copy-start(f32[64,16]{1,0:T(8,128)} %constant.11.clone.refs_5_) | copy-start | bytes 12292
  23.1 4.7 %copy-start.5 = (f32[16,64]{1,0:T(8,128)S(1)}, f32[16,64]{1,0:T(8,128)}, u32[]{:S(2)}) copy-start(f32[16,64]{1,0:T(8,128)} %constant.10.clone.refs_4_) | copy-start | bytes 12292
  23.1 4.6 %copy-start.6 = (f32[16,128]{1,0:T(8,128)S(1)}, f32[16,128]{1,0:T(8,128)}, u32[]{:S(2)}) copy-start(f32[16,128]{1,0:T(8,128)} %constant.14.clone.refs_8_) | copy-start | bytes 24580
  23.2 9.9 %collective-permute-start.14 = (f32[13,32,128]{2,1,0:T(8,128)S(1)}, f32[13,32,128]{2,1,0:T(8,128)S(1)}, u32[]{:S(2)}, u32[]{:S(2)}) collective-permute-start(f32[13,32,128]{2,1,0:T(8,128)S(1)} %slice.12), channel_id=1, source_target_pairs={{0,16},{16,0},{1,17},{17,1},{2,18},{18,2},{3,19},{19,3},{4,20},{20... | collective-permute-start | bytes 638984 | tf_op jit(solution)/shard_map/ppermute | solution.py:750

commit v7 on v6

--- a/solution.py
+++ b/solution.py
@@ -99,7 +99,20 @@
     return out
 
 
-def sweep(target, source, low, high, base=None, scale=None, period=None, span=None):
+def sweep(*args, **options):
+    for _ in sweep_steps(*args, **options):
+        pass
+
+
+def together(*runs):
+    waiting = list(runs)
+    while waiting:
+        for run in list(waiting):
+            if next(run, "end") == "end":
+                waiting.remove(run)
+
+
+def sweep_steps(target, source, low, high, base=None, scale=None, period=None, span=None):
     for plane in range(low, high):
         below, above = plane - 1, plane + 1
         if period is not None:
@@ -110,6 +123,7 @@
             if base is not None and (span is None or span[0] <= plane < span[1]):
                 value = value + base[t, plane]
             target[t, plane] = value
+        yield
 
 
 PLANE0 = 6
@@ -377,28 +391,63 @@
             out[t, x] = total
 
 
-def window_kernel(g1, above, below, out, base, first, second):
-    planes, rows = base.shape[1], base.shape[2]
+def fine_sweeps(base, first, second):
+    seventh = 1.0 / 7.0
+    planes = base.shape[1]
+    yield from sweep_steps(first, base, 1, planes - 1, base, seventh)
+    yield from sweep_steps(second, first, 2, planes - 2, base, seventh)
+    yield from sweep_steps(first, second, 3, planes - 3, base, seventh)
+    yield from sweep_steps(second, first, 4, planes - 4, base, seventh)
+
+
+def window_kernel(g1, out, base, first, second):
+    for p in range(base.shape[1]):
+        base[0, p] = g1[p]
+    together(fine_sweeps(base, first, second))
+    for c in range(out.shape[0]):
+        p = 5 + c
+        out[c] = (seven_sum(second, p, p - 1, p + 1)[0] * (1.0 / 7.0) + base[0, p]) * weight(1)
+
+
+WINDOW_LANES = 28
+
+
+def window_edge_steps(f1, above, below, out, base, first, second):
+    rows = base.shape[2]
+    share = out.shape[0]
+    size = share // 4
+    planes = share + 10
     lane = iota((rows, LANES), 1)
-    kept_lanes = ((lane >= 25) & (lane < 34)) | ((lane >= 94) & (lane < 103))
     turned = []
     for begin in range(0, rows * -(-planes // 14), rows):
-        turned.append((pltpu.roll(below[begin : begin + rows], 25, 1),
-                       pltpu.roll(above[begin : begin + rows], 94, 1)))
-    for p in range(planes):
-        lower, upper = turned[p // 14]
-        shift = 9 * (p % 14)
-        term = jnp.where(((lane - shift) & (LANES - 1)) < 64, lower, upper)
-        term = pltpu.roll(term, (LANES - shift) % LANES, 1) if shift else term
-        base[0, p] = g1[p] + jnp.where(kept_lanes, term, 0.0)
-    seventh = 1.0 / 7.0
-    sweep(first, base, 1, planes - 1, base, seventh)
-    sweep(second, first, 2, planes - 2, base, seventh)
-    sweep(first, second, 3, planes - 3, base, seventh)
-    sweep(second, first, 4, planes - 4, base, seventh)
-    for c in range(out.shape[0]):
-        p = 5 + c
-        out[c] = (seven_sum(second, p, p - 1, p + 1)[0] * seventh + base[0, p]) * weight(1)
+        turned.append((below[begin : begin + rows],
+                       pltpu.roll(above[begin : begin + rows], 19, 1)))
+    for j in range(base.shape[1]):
+        value = jnp.zeros((rows, LANES), F32)
+        for q in range(4):
+            p = size * q + j
+            lower, upper = turned[p // 14]
+            shift = 9 * (p % 14)
+            term = jnp.where(((lane - shift) & (LANES - 1)) < 14, lower, upper)
+            shift = (WINDOW_LANES * q - shift) % LANES
+            term = pltpu.roll(term, shift, 1) if shift else term
+            place = lane - WINDOW_LANES * q
+            inside = (place >= 0) & (place < WINDOW_LANES) & ((place < 9) | (place >= 19))
+            value = jnp.where(inside, term, value)
+        base[0, j] = value
+        yield
+    yield from fine_sweeps(base, first, second)
+    for m in range(size):
+        p = 5 + m
+        value = seven_sum(second, p, p - 1, p + 1)[0] * (1.0 / 7.0) + base[0, p]
+        value = value * weight(1)
+        for q in range(4):
+            c = size * q + m
+            low = pltpu.roll(value, (25 - WINDOW_LANES * q) % LANES, 1)
+            high = pltpu.roll(value, (75 - WINDOW_LANES * q) % LANES, 1)
+            part = jnp.where((lane >= 89) & (lane < 98), high, 0.0)
+            out[c] = f1[c] + jnp.where((lane >= 30) & (lane < 39), low, part)
+        yield
 
 
 def restrict_lanes(values, width, coarse_width, coarse_tiles):
@@ -477,8 +526,13 @@
 
 
 def solve_last(values, into, back, to_waves, from_waves, scale):
-    waves = dot(dot(into[...], values), to_waves[0])
-    return dot(dot(back[...], waves * scale[...]), from_waves[0])
+    values = dot(into[...], values)
+    yield
+    values = dot(values, to_waves[0]) * scale[...]
+    yield
+    values = dot(back[...], values)
+    yield
+    return dot(values, from_waves[0])
 
 
 def solve(level, width, buffers, spectral):
@@ -489,21 +543,27 @@
     if level == LEVELS - 2:
         source = [g[0, p] for p in range(planes)]
         first = swept(source)
+        yield
         second = swept(first)
+        yield
         third = swept(second)
+        yield
         before = [(x + y + z) * w for x, y, z in zip(source, first, second)]
-        values = solve_last(jnp.concatenate(third, axis=0), *spectral)
+        values = yield from solve_last(jnp.concatenate(third, axis=0), *spectral)
         error = [before[p] + values[rows * p : rows * (p + 1)] for p in range(planes)]
-        error = swept(swept(swept(error)))
+        yield
+        for _ in range(SWEEPS):
+            error = swept(error)
+            yield
         for p in range(planes):
             g[0, p] = before[p] + error[p]
         return
-    sweep(a, g, 0, planes, None, seventh, planes)
-    sweep(b, a, 0, planes, None, seventh, planes)
+    yield from sweep_steps(a, g, 0, planes, None, seventh, planes)
+    yield from sweep_steps(b, a, 0, planes, None, seventh, planes)
     for t in range(tiles):
         for p in range(planes):
             g[t, p] = (g[t, p] + a[t, p] + b[t, p]) * w
-    sweep(a, b, 0, planes, None, seventh, planes)
+    yield from sweep_steps(a, b, 0, planes, None, seventh, planes)
     half = rows // 2
     values = []
     for t in range(tiles):
@@ -520,7 +580,7 @@
     for t, value in enumerate(values):
         for c in range(planes // 2):
             coarse[t, c] = value[half * c : half * (c + 1)] * 0.125
-    solve(level + 1, width // 2, buffers, spectral)
+    yield from solve(level + 1, width // 2, buffers, spectral)
     values = [
         jnp.concatenate([coarse[t, c] for c in range(planes // 2)], axis=0)
         for t in range(coarse.shape[0])
@@ -534,15 +594,15 @@
                 b[t, p, pl.ds(1, half, stride=2), :] = part
         for p in range(planes):
             b[t, p] = b[t, p] + g[t, p]
-    sweep(a, b, 0, planes, None, seventh, planes)
-    sweep(b, a, 0, planes, None, seventh, planes)
-    sweep(a, b, 0, planes, None, seventh, planes)
+    yield from sweep_steps(a, b, 0, planes, None, seventh, planes)
+    yield from sweep_steps(b, a, 0, planes, None, seventh, planes)
+    yield from sweep_steps(a, b, 0, planes, None, seventh, planes)
     for t in range(tiles):
         for p in range(planes):
             g[t, p] = g[t, p] + a[t, p]
 
 
-def coarse_kernel(count, *refs):
+def coarse_steps(count, *refs):
     shares, spectral = refs[:count], refs[count : count + 5]
     out, scratch = refs[count + 5], refs[count + 6 :]
     buffers = {level: scratch[3 * (level - 2) : 3 * (level - 1)] for level in (2, 3)}
@@ -553,9 +613,24 @@
             for b in range(count):
                 value = shares[b][t, p, 0:8] + shares[(b - 1) % count][t, p, 8:16]
                 g[t, p, 8 * b : 8 * b + 8] = value
-    solve(2, LANES * tiles, buffers, spectral)
+    yield from solve(2, LANES * tiles, buffers, spectral)
     for c in range(out.shape[0]):
         out[c] = g[0, (c - 3) % planes, 0:16]
+
+
+def arrived_kernel(above, below, out):
+    out[...] = jnp.zeros(out.shape, F32)
+
+
+def late_kernel(count, sources, planes, *refs):
+    shares, rest = refs[: count + 5], refs[count + 5 :]
+    f1, above, below, own, e2_out, f1_out, edge_out = rest[:7]
+    scratch = rest[7:]
+    together(
+        coarse_steps(count, *shares, e2_out, *scratch[:6]),
+        window_edge_steps(f1, above, below, f1_out, *scratch[6:9]),
+        fine_edge_steps(sources, planes, above, below, own, edge_out, *scratch[9:12]),
+    )
 
 
 def correct_kernel(e2, f1, u0_b, u1_a, u1_b, u0_a):
@@ -639,7 +714,7 @@
 LOW_END, HIGH_AT, OWN_AT = 5, 16, 22
 
 
-def fine_edge_kernel(sources, planes, above, below, own, out, base, first, second):
+def fine_edge_steps(sources, planes, above, below, own, out, base, first, second):
     rows = base.shape[2]
     size = out.shape[0]
     lane = iota((rows, LANES), 1)
@@ -673,17 +748,15 @@
             inside = inside & ((place < spread) | (place >= HIGH_AT))
             value = jnp.where(inside, total, value)
         base[0, j] = value
+        yield
     seventh = 1.0 / 7.0
-    high = base.shape[1]
-    sweep(first, base, 1, high - 1, base, seventh)
-    sweep(second, first, 2, high - 2, base, seventh)
-    sweep(first, second, 3, high - 3, base, seventh)
-    sweep(second, first, 4, high - 4, base, seventh)
+    yield from fine_sweeps(base, first, second)
     kept = out.shape[1]
     for i in range(size):
         p = SPILL + i
         value = (seven_sum(second, p, p - 1, p + 1)[0] * seventh + base[0, p]) * weight(0)
         out[i] = value[ROW0 : ROW0 + kept]
+        yield
 
 
 def edge_sides(part, q):
@@ -797,9 +870,10 @@
         window_kernel,
         shape(share1, *window[2:]),
         [window, window, window],
-        0.9,
-        window_g1, above, below,
-    )
+        0.01,
+        window_g1,
+    )
+    packed = (1, share1 // 4 + 10, *window[2:])
     share0 = nx + 11
     main, f_down, f_up, kept = call(
         fine_own_kernel,
@@ -837,7 +911,7 @@
         fine_y_kernel,
         shape(share0 + 1, ny, LANES),
         [(share0, rows0, LANES)],
-        0.4,
+        0.01,
         main, f_above, f_below,
         after=(g2,),
     )
@@ -849,12 +923,19 @@
         f_below = from_offset(f0[6:13], "gx", -1)
     group = -(-(nx + 1) // GROUPS)
     edges = (1, group + 2 * SPILL, rows0, LANES)
-    edge = call(
-        functools.partial(fine_edge_kernel, tuple(sources[:3]), nx),
-        shape(group, ny + 8, LANES),
-        [edges, edges, edges],
-        1.9,
-        above, below, up,
+    scratch = []
+    for level in (2, 3):
+        cut = 2 ** (level - 2)
+        extent = (max(1, tiles // cut), 4 * size_x // cut, 8 * size_y // cut, LANES)
+        scratch.extend([extent] * 3)
+    arrived = call(arrived_kernel, shape(8, LANES), [], 2.0, above, below)
+    e2, f1, edge = call(
+        functools.partial(late_kernel, size_y, tuple(sources[:3]), nx),
+        [shape(n1 // 2 + 6, 16, LANES), shape(share1, *window[2:]), shape(group, ny + 8, LANES)],
+        scratch + [packed] * 3 + [edges] * 3,
+        3.0,
+        *shares, *last_level_matrices(size_x, 2 * size_y, 8 * size_z), f1, above, below, up,
+        after=(arrived,),
     )
     f0, beyond = call(
         fine_sum_kernel,
@@ -864,19 +945,6 @@
         f0, f_below, f_above, edge,
     )
 
-    scratch = []
-    for level in (2, 3):
-        cut = 2 ** (level - 2)
-        extent = (max(1, tiles // cut), 4 * size_x // cut, 8 * size_y // cut, LANES)
-        scratch.extend([extent] * 3)
-    e2 = call(
-        functools.partial(coarse_kernel, size_y),
-        shape(n1 // 2 + 6, 16, LANES),
-        scratch,
-        2.2,
-        *shares, *last_level_matrices(size_x, 2 * size_y, 8 * size_z),
-        after=(f1,),
-    )
     fine = (2, nx + 8, ny + 8, LANES)
     correction = call(
         correct_kernel,

time: 34.7 us -> 33.7 us (0.971)
  starting transfers between devices: 15.6 us -> 15 us
    ppermute x15, starting transfers between devices: 15.6 us -> 15 us  [from_offset(): return lax.ppermute(value, axis, pairs)]
  transfers between devices with their start and end apart: 15 -> 15, of which waited for: 5 -> 4; matrix products, arithmetic and copies ran while one was open for 0% -> 0% of each run, Pallas kernels for 24% -> 24%
where the time goes in v7:
time: 33.7 us; the launch traced here: 33.6 us
  starting transfers between devices  15 us (45%)
  Pallas kernels  12.4 us (37%)
  waiting for transfers between devices  4.71 us (14%)
  local copies, waits for them, and re-layouts  1.2 us (4%)
    ppermute x15, starting transfers between devices, from_offset(): return lax.ppermute(value, axis, pairs)  15 us
    pallas_call x13, Pallas kernels, call(): pl.pallas_call(kernel, out_shape=outs, scratch_shapes=[pltpu.VMEM(s, F32)...  12.4 us
    ppermute x15, waiting for transfers between devices, from_offset(): return lax.ppermute(value, axis, pairs)  4.71 us
    unnamed x14, local copies, waits for them, and re-layouts  1.17 us
  transfers between devices with their start and end apart: 15, of which 4 were waited for; matrix products, arithmetic and copies ran while one was open for 0% of the time, Pallas kernels for 24%

profile of v7, /device:TPU:0, one launch (start us, length us, event | category | flops | bytes accessed | tf_op | source)
XLA Modules:
  0.0 33.6 jit_solution(10240850106735575287)
XLA Ops:
  0.0 1.1 %copy-done = f32[3,16,32,128]{3,2,1,0:T(8,128)S(1)} copy-done((f32[3,16,32,128]{3,2,1,0:T(8,128)S(1)}, f32[3,16,32,128]{3,2,1,0:T(8,128)}, u32[]{:S(2)}) %copy-start) | copy-done | bytes 786456
  1.1 2.6 %shard_map.64 = (f32[220,128]{1,0:T(8,128)S(1)}, f32[64,128]{1,0:T(8,128)S(1)}, f32[12,24,128]{2,1,0:T(8,128)S(1)}, f32[2,29,48,128]{3,2,1,0:T(8,128)S(1)}, f32[...) custom-call(f32[3,16,32,128]{3,2,1,0:T(8,128)S(1)} %copy-done), custom_call_target="tpu_custom_call" | custom-call | flops 3335000064 | tf_op jit(solution)/shard_map/pallas_call | solution.py:39
  3.8 3.0 %collective-permute-start = (f32[220,128]{1,0:T(8,128)S(1)}, f32[220,128]{1,0:T(8,128)S(1)}, u32[]{:S(2)}, u32[]{:S(2)}) collective-permute-start(f32[220,128]{1,0:T(8,128)S(1)} %get-tuple-element.31.refs_1_.refs_0_), channel_id=1, source_target_pairs={{0,16},{16,0},{1,17},{17,1},{2,18},{18,2},{3,19},{19,3},{4,20},{20... | collective-permute-start | bytes 337928 | tf_op jit(solution)/shard_map/ppermute | solution.py:823
  6.8 3.6 %collective-permute-start.1 = (f32[64,128]{1,0:T(8,128)S(1)}, f32[64,128]{1,0:T(8,128)S(1)}, u32[]{:S(2)}, u32[]{:S(2)}) collective-permute-start(f32[64,128]{1,0:T(8,128)S(1)} %get-tuple-element.33.refs_0_), channel_id=1, source_target_pairs={{0,3},{1,0},{2,1},{3,2},{4,7},{5,4},{6,5},{7,6},{8,11},{9,8},{10,9... | collective-permute-start | bytes 98312 | tf_op jit(solution)/shard_map/ppermute | solution.py:823
  10.4 1.0 %collective-permute-start.3 = (f32[64,128]{1,0:T(8,128)S(1)}, f32[64,128]{1,0:T(8,128)S(1)}, u32[]{:S(2)}, u32[]{:S(2)}) collective-permute-start(f32[64,128]{1,0:T(8,128)S(1)} %get-tuple-element.33.refs_0_), channel_id=1, source_target_pairs={{0,1},{1,2},{2,3},{3,0},{4,5},{5,6},{6,7},{7,4},{8,9},{9,10},{10,1... | collective-permute-start | bytes 98312 | tf_op jit(solution)/shard_map/ppermute | solution.py:823
  11.4 0.2 shard_map.66
  11.7 0.5 %collective-permute-start.6 = (f32[222,128]{1,0:T(8,128)S(1)}, f32[222,128]{1,0:T(8,128)S(1)}, u32[]{:S(2)}, u32[]{:S(2)}) collective-permute-start(f32[222,128]{1,0:T(8,128)S(1)} %get-tuple-element.38), channel_id=1, source_target_pairs={{0,4},{4,8},{8,12},{12,0},{1,5},{5,9},{9,13},{13,1},{2,6},{6,10},{... | collective-permute-start | bytes 341000 | tf_op jit(solution)/shard_map/ppermute | solution.py:823
  12.2 1.6 %shard_map.65 = (f32[27,48,128]{2,1,0:T(8,128)S(1)}, f32[27,8,128]{2,1,0:T(8,128)S(1)}, f32[27,8,128]{2,1,0:T(8,128)S(1)}, f32[3,16,32,128]{3,2,1,0:T(8,128)S(1)}) custom-call(f32[2,29,48,128]{3,2,1,0:T(8,128)S(1)} %get-tuple-element.27.refs_0_, f32[2,29,48,128]{3,2,1,0:T(8,128)S(1)} %get-tuple-element.28.refs_1_, ...), custom_call_target="tpu_custom_call" | custom-call | flops 3449999872 | tf_op jit(solution)/shard_map/pallas_call | solution.py:39
  13.8 1.5 %collective-permute-done.2.refs_2_ = f32[64,128]{1,0:T(8,128)S(1)} collective-permute-done((f32[64,128]{1,0:T(8,128)S(1)}, f32[64,128]{1,0:T(8,128)S(1)}, u32[]{:S(2)}, u32[]{:S(2)}) %collective-permute-start.2) | collective-permute-done | bytes 32800 | tf_op jit(solution)/shard_map/ppermute | solution.py:823
  15.2 0.9 %collective-permute-done.3.refs_3_ = f32[64,128]{1,0:T(8,128)S(1)} collective-permute-done((f32[64,128]{1,0:T(8,128)S(1)}, f32[64,128]{1,0:T(8,128)S(1)}, u32[]{:S(2)}, u32[]{:S(2)}) %collective-permute-start.3) | collective-permute-done | bytes 32800 | tf_op jit(solution)/shard_map/ppermute | solution.py:823
  16.3 0.6 %collective-permute-start.4 = (f32[1,10,16,128]{3,2,1,0:T(8,128)S(1)}, f32[1,10,16,128]{3,2,1,0:T(8,128)S(1)}, u32[]{:S(2)}, u32[]{:S(2)}) collective-permute-start(f32[1,10,16,128]{3,2,1,0:T(8,128)S(1)} %shard_map.67.refs_0_), channel_id=1, source_target_pairs={{0,16},{16,0},{1,17},{17,1},{2,18},{18,2},{3,19},{19,3},{4,20},{20... | collective-permute-start | bytes 245768 | tf_op jit(solution)/shard_map/ppermute | solution.py:823
  16.9 0.5 %collective-permute-start.13 = (f32[27,8,128]{2,1,0:T(8,128)S(1)}, f32[27,8,128]{2,1,0:T(8,128)S(1)}, u32[]{:S(2)}, u32[]{:S(2)}) collective-permute-start(f32[27,8,128]{2,1,0:T(8,128)S(1)} %get-tuple-element.45), channel_id=1, source_target_pairs={{0,4},{4,8},{8,12},{12,0},{1,5},{5,9},{9,13},{13,1},{2,6},{6,10},{... | collective-permute-start | bytes 331784 | tf_op jit(solution)/shard_map/ppermute | solution.py:823
  17.4 0.3 shard_map.68
  17.7 2.7 %collective-permute-start.10 = (f32[160,128]{1,0:T(8,128)S(1)}, f32[160,128]{1,0:T(8,128)S(1)}, u32[]{:S(2)}, u32[]{:S(2)}) collective-permute-start(f32[160,128]{1,0:T(8,128)S(1)} %get-tuple-element.40), channel_id=1, source_target_pairs={{0,3},{1,0},{2,1},{3,2},{4,7},{5,4},{6,5},{7,6},{8,11},{9,8},{10,9... | collective-permute-start | bytes 245768 | tf_op jit(solution)/shard_map/ppermute | solution.py:823
  20.3 0.4 %collective-permute-done.4.refs_1_ = f32[1,10,16,128]{3,2,1,0:T(8,128)S(1)} collective-permute-done((f32[1,10,16,128]{3,2,1,0:T(8,128)S(1)}, f32[1,10,16,128]{3,2,1,0:T(8,128)S(1)}, u32[]{:S(2)}, u32[]{:S(2)}) %collective-permute-start.4) | collective-permute-done | bytes 81952 | tf_op jit(solution)/shard_map/ppermute | solution.py:823
  20.9 1.6 %collective-permute-start.8 = (f32[1,8,16,128]{3,2,1,0:T(8,128)S(1)}, f32[1,8,16,128]{3,2,1,0:T(8,128)S(1)}, u32[]{:S(2)}, u32[]{:S(2)}) collective-permute-start(f32[1,8,16,128]{3,2,1,0:T(8,128)S(1)} %shard_map.69.refs_0_.refs_3_), channel_id=1, source_target_pairs={{0,8},{4,12},{8,0},{12,4},{1,9},{5,13},{9,1},{13,5},{2,10},{6,14},... | collective-permute-start | bytes 196616 | tf_op jit(solution)/shard_map/ppermute | solution.py:823
  22.4 0.2 collective-permute-start.9
  22.7 0.7 %shard_map.70.refs_9_ = f32[12,32,128]{2,1,0:T(8,128)S(1)} custom-call(f32[22,32,128]{2,1,0:T(8,128)S(1)} %get-tuple-element.39.refs_2_.g1), custom_call_target="tpu_custom_call" | custom-call | flops 11500000 | tf_op jit(solution)/shard_map/pallas_call | solution.py:39
  23.5 1.3 %collective-permute-start.14 = (f32[13,32,128]{2,1,0:T(8,128)S(1)}, f32[13,32,128]{2,1,0:T(8,128)S(1)}, u32[]{:S(2)}, u32[]{:S(2)}) collective-permute-start(f32[13,32,128]{2,1,0:T(8,128)S(1)} %slice.12), channel_id=1, source_target_pairs={{0,16},{16,0},{1,17},{17,1},{2,18},{18,2},{3,19},{19,3},{4,20},{20... | collective-permute-start | bytes 638984 | tf_op jit(solution)/shard_map/ppermute | solution.py:823
  24.9 1.9 %collective-permute-done.11.below.refs_11_ = f32[160,128]{1,0:T(8,128)S(1)} collective-permute-done((f32[160,128]{1,0:T(8,128)S(1)}, f32[160,128]{1,0:T(8,128)S(1)}, u32[]{:S(2)}, u32[]{:S(2)}) %collective-permute-start.11) | collective-permute-done | bytes 81952 | tf_op jit(solution)/shard_map/ppermute | solution.py:823
  26.8 3.1 %shard_map.72 = (f32[10,16,128]{2,1,0:T(8,128)S(1)}, f32[12,32,128]{2,1,0:T(8,128)S(1)}, f32[6,40,128]{2,1,0:T(8,128)S(1)}) custom-call(f32[1,8,16,128]{3,2,1,0:T(8,128)S(1)} %shard_map.69.refs_0_.refs_3_, f32[1,8,16,128]{3,2,1,0:T(8,128)S(1)} %collective-permute-done.7.refs_1_, f32[1,8,16,128]{3,2,1,0:T(8,128)S(1)} %collective-permute-done.8.refs_2_, ...), custom_call_target="tpu_custom_call" | custom-call | flops 3449999872 | tf_op jit(solution)/shard_map/pallas_call | solution.py:39
  29.9 2.1 %shard_map.73.u0_b = f32[2,24,40,128]{3,2,1,0:T(8,128)S(1)} custom-call(f32[10,16,128]{2,1,0:T(8,128)S(1)} %get-tuple-element.42.e2, f32[12,32,128]{2,1,0:T(8,128)S(1)} %get-tuple-element.43.f1), custom_call_target="tpu_custom_call" | custom-call | flops 2529999872 | tf_op jit(solution)/shard_map/pallas_call | solution.py:39
  32.0 0.4 %shard_map.75 = (f32[17,40,128]{2,1,0:T(8,128)S(1)}, f32[16,32,128]{2,1,0:T(8,128)S(1)}) custom-call(f32[28,32,128]{2,1,0:T(8,128)S(1)} %shard_map.74.f0, f32[7,32,128]{2,1,0:T(8,128)S(1)} %get-tuple-element.50.below_x, f32[7,32,128]{2,1,0:T(8,128)S(1)} %get-tuple-element.49.above_x, f32[6,40,128]{2,1,0:T(8,128)S(1)} %get-tuple-element.46.work), custom_call_target="tpu_custom_call" | custom-call | flops 345000000 | tf_op jit(solution)/shard_map/pallas_call | solution.py:39
  32.4 1.1 %shard_map.76 = f32[3,16,32,128]{3,2,1,0:T(8,128)} custom-call(f32[3,16,32,128]{3,2,1,0:T(8,128)S(1)} %get-tuple-element.32.field, f32[2,24,40,128]{3,2,1,0:T(8,128)S(1)} %shard_map.73.u0_b, f32[17,40,128]{2,1,0:T(8,128)S(1)} %get-tuple-element.47.f0, f32[16,32,128]{2,1,0:T(8,128)S(1)} %get-tuple-element.48.beyond), custom_call_target="tpu_custom_call" | custom-call | flops 1035000000 | tf_op jit(solution)/shard_map/pallas_call | solution.py:39
  (35 shorter events, 0.5 us)
Async XLA Ops:
  0.0 1.1 %copy-start = (f32[3,16,32,128]{3,2,1,0:T(8,128)S(1)}, f32[3,16,32,128]{3,2,1,0:T(8,128)}, u32[]{:S(2)}) copy-start(f32[3,16,32,128]{3,2,1,0:T(8,128)} %refs_4_.2) | copy-start | bytes 2359300
  1.1 11.0 %copy-start.1 = (f32[3,16,32,128]{3,2,1,0:T(8,128)S(1)}, f32[3,16,32,128]{3,2,1,0:T(8,128)}, u32[]{:S(2)}) copy-start(f32[3,16,32,128]{3,2,1,0:T(8,128)} %refs_4_.2) | copy-start | bytes 2359300
  3.8 7.7 %collective-permute-start = (f32[220,128]{1,0:T(8,128)S(1)}, f32[220,128]{1,0:T(8,128)S(1)}, u32[]{:S(2)}, u32[]{:S(2)}) collective-permute-start(f32[220,128]{1,0:T(8,128)S(1)} %get-tuple-element.31.refs_1_.refs_0_), channel_id=1, source_target_pairs={{0,16},{16,0},{1,17},{17,1},{2,18},{18,2},{3,19},{19,3},{4,20},{20... | collective-permute-start | bytes 337928 | tf_op jit(solution)/shard_map/ppermute | solution.py:823
  6.8 7.0 %collective-permute-start.1 = (f32[64,128]{1,0:T(8,128)S(1)}, f32[64,128]{1,0:T(8,128)S(1)}, u32[]{:S(2)}, u32[]{:S(2)}) collective-permute-start(f32[64,128]{1,0:T(8,128)S(1)} %get-tuple-element.33.refs_0_), channel_id=1, source_target_pairs={{0,3},{1,0},{2,1},{3,2},{4,7},{5,4},{6,5},{7,6},{8,11},{9,8},{10,9... | collective-permute-start | bytes 98312 | tf_op jit(solution)/shard_map/ppermute | solution.py:823
  10.4 4.8 %collective-permute-start.2 = (f32[64,128]{1,0:T(8,128)S(1)}, f32[64,128]{1,0:T(8,128)S(1)}, u32[]{:S(2)}, u32[]{:S(2)}) collective-permute-start(f32[64,128]{1,0:T(8,128)S(1)} %get-tuple-element.33.refs_0_), channel_id=1, source_target_pairs={{0,2},{1,3},{2,0},{3,1},{4,6},{5,7},{6,4},{7,5},{8,10},{9,11},{10,... | collective-permute-start | bytes 98312 | tf_op jit(solution)/shard_map/ppermute | solution.py:823
  10.4 5.7 %collective-permute-start.3 = (f32[64,128]{1,0:T(8,128)S(1)}, f32[64,128]{1,0:T(8,128)S(1)}, u32[]{:S(2)}, u32[]{:S(2)}) collective-permute-start(f32[64,128]{1,0:T(8,128)S(1)} %get-tuple-element.33.refs_0_), channel_id=1, source_target_pairs={{0,1},{1,2},{2,3},{3,0},{4,5},{5,6},{6,7},{7,4},{8,9},{9,10},{10,1... | collective-permute-start | bytes 98312 | tf_op jit(solution)/shard_map/ppermute | solution.py:823
  11.6 5.8 %collective-permute-start.5 = (f32[222,128]{1,0:T(8,128)S(1)}, f32[222,128]{1,0:T(8,128)S(1)}, u32[]{:S(2)}, u32[]{:S(2)}) collective-permute-start(f32[222,128]{1,0:T(8,128)S(1)} %get-tuple-element.37), channel_id=1, source_target_pairs={{0,12},{4,0},{8,4},{12,8},{1,13},{5,1},{9,5},{13,9},{2,14},{6,2},{... | collective-permute-start | bytes 341000 | tf_op jit(solution)/shard_map/ppermute | solution.py:823
  11.7 5.7 %collective-permute-start.6 = (f32[222,128]{1,0:T(8,128)S(1)}, f32[222,128]{1,0:T(8,128)S(1)}, u32[]{:S(2)}, u32[]{:S(2)}) collective-permute-start(f32[222,128]{1,0:T(8,128)S(1)} %get-tuple-element.38), channel_id=1, source_target_pairs={{0,4},{4,8},{8,12},{12,0},{1,5},{5,9},{9,13},{13,1},{2,6},{6,10},{... | collective-permute-start | bytes 341000 | tf_op jit(solution)/shard_map/ppermute | solution.py:823
  16.3 4.5 %collective-permute-start.4 = (f32[1,10,16,128]{3,2,1,0:T(8,128)S(1)}, f32[1,10,16,128]{3,2,1,0:T(8,128)S(1)}, u32[]{:S(2)}, u32[]{:S(2)}) collective-permute-start(f32[1,10,16,128]{3,2,1,0:T(8,128)S(1)} %shard_map.67.refs_0_), channel_id=1, source_target_pairs={{0,16},{16,0},{1,17},{17,1},{2,18},{18,2},{3,19},{19,3},{4,20},{20... | collective-permute-start | bytes 245768 | tf_op jit(solution)/shard_map/ppermute | solution.py:823
  16.8 4.0 %collective-permute-start.12 = (f32[27,8,128]{2,1,0:T(8,128)S(1)}, f32[27,8,128]{2,1,0:T(8,128)S(1)}, u32[]{:S(2)}, u32[]{:S(2)}) collective-permute-start(f32[27,8,128]{2,1,0:T(8,128)S(1)} %get-tuple-element.44), channel_id=1, source_target_pairs={{0,12},{4,0},{8,4},{12,8},{1,13},{5,1},{9,5},{13,9},{2,14},{6,2},{... | collective-permute-start | bytes 331784 | tf_op jit(solution)/shard_map/ppermute | solution.py:823
  16.9 5.6 %collective-permute-start.13 = (f32[27,8,128]{2,1,0:T(8,128)S(1)}, f32[27,8,128]{2,1,0:T(8,128)S(1)}, u32[]{:S(2)}, u32[]{:S(2)}) collective-permute-start(f32[27,8,128]{2,1,0:T(8,128)S(1)} %get-tuple-element.45), channel_id=1, source_target_pairs={{0,4},{4,8},{8,12},{12,0},{1,5},{5,9},{9,13},{13,1},{2,6},{6,10},{... | collective-permute-start | bytes 331784 | tf_op jit(solution)/shard_map/ppermute | solution.py:823
  17.7 5.8 %collective-permute-start.10 = (f32[160,128]{1,0:T(8,128)S(1)}, f32[160,128]{1,0:T(8,128)S(1)}, u32[]{:S(2)}, u32[]{:S(2)}) collective-permute-start(f32[160,128]{1,0:T(8,128)S(1)} %get-tuple-element.40), channel_id=1, source_target_pairs={{0,3},{1,0},{2,1},{3,2},{4,7},{5,4},{6,5},{7,6},{8,11},{9,8},{10,9... | collective-permute-start | bytes 245768 | tf_op jit(solution)/shard_map/ppermute | solution.py:823
  20.3 6.4 %collective-permute-start.11 = (f32[160,128]{1,0:T(8,128)S(1)}, f32[160,128]{1,0:T(8,128)S(1)}, u32[]{:S(2)}, u32[]{:S(2)}) collective-permute-start(f32[160,128]{1,0:T(8,128)S(1)} %get-tuple-element.41.refs_12_), channel_id=1, source_target_pairs={{0,1},{1,2},{2,3},{3,0},{4,5},{5,6},{6,7},{7,4},{8,9},{9,10},{10,1... | collective-permute-start | bytes 245768 | tf_op jit(solution)/shard_map/ppermute | solution.py:823
  20.8 6.0 %collective-permute-start.7 = (f32[1,8,16,128]{3,2,1,0:T(8,128)S(1)}, f32[1,8,16,128]{3,2,1,0:T(8,128)S(1)}, u32[]{:S(2)}, u32[]{:S(2)}) collective-permute-start(f32[1,8,16,128]{3,2,1,0:T(8,128)S(1)} %shard_map.69.refs_0_.refs_3_), channel_id=1, source_target_pairs={{0,12},{4,0},{8,4},{12,8},{1,13},{5,1},{9,5},{13,9},{2,14},{6,2},{... | collective-permute-start | bytes 196616 | tf_op jit(solution)/shard_map/ppermute | solution.py:823
  20.9 5.9 %collective-permute-start.8 = (f32[1,8,16,128]{3,2,1,0:T(8,128)S(1)}, f32[1,8,16,128]{3,2,1,0:T(8,128)S(1)}, u32[]{:S(2)}, u32[]{:S(2)}) collective-permute-start(f32[1,8,16,128]{3,2,1,0:T(8,128)S(1)} %shard_map.69.refs_0_.refs_3_), channel_id=1, source_target_pairs={{0,8},{4,12},{8,0},{12,4},{1,9},{5,13},{9,1},{13,5},{2,10},{6,14},... | collective-permute-start | bytes 196616 | tf_op jit(solution)/shard_map/ppermute | solution.py:823
  22.4 4.3 %collective-permute-start.9 = (f32[1,8,16,128]{3,2,1,0:T(8,128)S(1)}, f32[1,8,16,128]{3,2,1,0:T(8,128)S(1)}, u32[]{:S(2)}, u32[]{:S(2)}) collective-permute-start(f32[1,8,16,128]{3,2,1,0:T(8,128)S(1)} %shard_map.69.refs_0_.refs_3_), channel_id=1, source_target_pairs={{0,4},{4,8},{8,12},{12,0},{1,5},{5,9},{9,13},{13,1},{2,6},{6,10},{... | collective-permute-start | bytes 196616 | tf_op jit(solution)/shard_map/ppermute | solution.py:823
  23.5 3.3 %copy-start.2 = (f32[1,128,128]{2,1,0:T(8,128)S(1)}, f32[1,128,128]{2,1,0:T(8,128)}, u32[]{:S(2)}) copy-start(f32[1,128,128]{2,1,0:T(8,128)} %constant.12.clone.refs_6_) | copy-start | bytes 196612
  23.5 3.3 %copy-start.3 = (f32[1,128,128]{2,1,0:T(8,128)S(1)}, f32[1,128,128]{2,1,0:T(8,128)}, u32[]{:S(2)}) copy-start(f32[1,128,128]{2,1,0:T(8,128)} %constant.13.clone.refs_7_) | copy-start | bytes 196612
  23.5 3.3 %copy-start.4 = (f32[64,16]{1,0:T(8,128)S(1)}, f32[64,16]{1,0:T(8,128)}, u32[]{:S(2)}) copy-start(f32[64,16]{1,0:T(8,128)} %constant.11.clone.refs_5_) | copy-start | bytes 12292
  23.5 3.3 %copy-start.5 = (f32[16,64]{1,0:T(8,128)S(1)}, f32[16,64]{1,0:T(8,128)}, u32[]{:S(2)}) copy-start(f32[16,64]{1,0:T(8,128)} %constant.10.clone.refs_4_) | copy-start | bytes 12292
  23.5 3.3 %copy-start.6 = (f32[16,128]{1,0:T(8,128)S(1)}, f32[16,128]{1,0:T(8,128)}, u32[]{:S(2)}) copy-start(f32[16,128]{1,0:T(8,128)} %constant.14.clone.refs_8_) | copy-start | bytes 24580
  23.5 8.5 %collective-permute-start.14 = (f32[13,32,128]{2,1,0:T(8,128)S(1)}, f32[13,32,128]{2,1,0:T(8,128)S(1)}, u32[]{:S(2)}, u32[]{:S(2)}) collective-permute-start(f32[13,32,128]{2,1,0:T(8,128)S(1)} %slice.12), channel_id=1, source_target_pairs={{0,16},{16,0},{1,17},{17,1},{2,18},{18,2},{3,19},{19,3},{4,20},{20... | collective-permute-start | bytes 638984 | tf_op jit(solution)/shard_map/ppermute | solution.py:823

commit v8 on v7

--- a/solution.py
+++ b/solution.py
@@ -27,7 +27,7 @@
     return jax.ShapeDtypeStruct(extent, F32)
 
 
-def call(kernel, outs, scratch, microseconds, *args, after=()):
+def call(kernel, outs, scratch, microseconds, *args, after=(), **specs):
     flops = int(microseconds * PEAK_FLOPS_PER_US)
     if after:
         inner, first, last = kernel, len(args), len(args) + len(after)
@@ -39,8 +39,9 @@
     return pl.pallas_call(
         kernel,
         out_shape=outs,
-        scratch_shapes=[pltpu.VMEM(s, F32) for s in scratch],
+        scratch_shapes=[pltpu.VMEM(s, F32) if isinstance(s, tuple) else s for s in scratch],
         compiler_params=pltpu.CompilerParams(vmem_limit_bytes=VMEM_LIMIT),
+        **specs,
         cost_estimate=pl.CostEstimate(flops=flops, bytes_accessed=0, transcendentals=0),
     )(*args)
 
@@ -667,22 +668,59 @@
     sweep(u0_b, u0_a, 3, count0 - 3)
 
 
-def finish_kernel(field, u0_b, f0, beyond, out, pot):
+def plane_copies(source, target, semaphores):
+    step = source.shape[1] // semaphores.shape[0]
+    copies = []
+    for k in range(semaphores.shape[0]):
+        planes = pl.ds(step * k, step)
+        copies.append(
+            pltpu.make_async_copy(source.at[:, planes], target.at[:, planes], semaphores.at[k])
+        )
+    return copies
+
+
+def finish_kernel(field, u0_b, f0, below_x, above_x, edge, result, out, finished):
     planes, rows = field.shape[1], field.shape[2]
     scale = 1.0 / 343.0
-    for i in range(planes + 1):
-        pot[i, 0:rows] = u0_b[0, 4 + i, 4 : 4 + rows] * scale + f0[i, 0:rows]
-        if i < planes:
-            edge = u0_b[0, 4 + i, 4 + rows : 5 + rows] * scale
-            pot[i, rows : rows + 1] = edge + f0[i, rows : rows + 1]
     lane = iota((rows, LANES), 1)
+    row = iota((rows, LANES), 0)
+    copies = plane_copies(out, result, finished)
+    step = planes // len(copies)
+
+    def potential(i):
+        q, m = i // edge.shape[0], i % edge.shape[0]
+        value = u0_b[0, 4 + i, 4 : 4 + rows] * scale + f0[fine_place(i + SPILL, planes + 11)]
+        if i <= SPILL:
+            value = value + below_x[1 + i]
+        if i >= planes - SPILL:
+            value = value + above_x[i - (planes - SPILL)]
+        return value + edge_sides(edge[m, 0:rows], q)
+
+    here = potential(0)
     for i in range(planes):
-        here = pot[i, 0:rows]
-        out[0, i] = field[0, i] - (pot[i + 1, 0:rows] - here)
-        out[1, i] = field[1, i] - (pot[i, 1 : rows + 1] - here)
-        last = pltpu.roll(u0_b[1, 4 + i, 4 : 4 + rows], LANES - 1, 1) * scale + beyond[i]
+        above = potential(i + 1)
+        out[0, i] = field[0, i] - (above - here)
+        q, m = i // edge.shape[0], i % edge.shape[0]
+        end = u0_b[0, 4 + i, 4 + rows : 5 + rows] * scale + f0[6, i + SPILL : i + SPILL + 1]
+        if i <= SPILL:
+            end = end + below_x[0, i + SPILL + planes : i + SPILL + planes + 1]
+        if i >= planes - SPILL:
+            end = end + above_x[6, i + SPILL - planes : i + SPILL - planes + 1]
+        end = end + edge_sides(edge[m, rows : rows + 1], q)
+        end = jnp.broadcast_to(end, (rows, LANES))
+        next_y = jnp.where(row == rows - 1, end, pltpu.roll(here, rows - 1, 0))
+        out[1, i] = field[1, i] - (next_y - here)
+        part = edge[m, 0:rows]
+        last = pltpu.roll(u0_b[1, 4 + i, 4 : 4 + rows], LANES - 1, 1) * scale
+        last = last + turned_to_last(part, GROUP_LANES * q + HIGH_AT)
+        last = last + turned_to_last(part, GROUP_LANES * q + OWN_AT + SPILL)
         next_z = jnp.where(lane == LANES - 1, last, pltpu.roll(here, LANES - 1, 1))
         out[2, i] = field[2, i] - (next_z - here)
+        if i % step == step - 1:
+            copies[i // step].start()
+        here = above
+    for copy in copies:
+        copy.wait()
 
 
 def fine_place(p, share):
@@ -770,32 +808,6 @@
     return pltpu.roll(value, (LANES - 1 - lane) % LANES, 1)
 
 
-def fine_sum_kernel(f0, below_x, above_x, work, out, beyond):
-    planes, rows = beyond.shape[0], beyond.shape[1]
-    lane = iota((rows, LANES), 1)
-    lane1 = iota((1, LANES), 1)
-    for i in range(planes + 1):
-        value = f0[fine_place(i + SPILL, planes + 11)]
-        if i <= SPILL:
-            value = value + below_x[1 + i]
-        if i >= planes - SPILL:
-            value = value + above_x[i - (planes - SPILL)]
-        q, m = i // work.shape[0], i % work.shape[0]
-        part = work[m, 0:rows]
-        out[i, 0:rows] = value + edge_sides(part, q)
-        if i < planes:
-            first = GROUP_LANES * q
-            last = turned_to_last(part, first + HIGH_AT)
-            beyond[i] = last + turned_to_last(part, first + OWN_AT + SPILL)
-            row = f0[6, i + SPILL : i + SPILL + 1]
-            if i <= SPILL:
-                row = row + below_x[0, i + SPILL + planes : i + SPILL + planes + 1]
-            if i >= planes - SPILL:
-                row = row + above_x[6, i + SPILL - planes : i + SPILL - planes + 1]
-            row = row + edge_sides(work[m, rows : rows + 1], q)
-            out[i, rows : rows + 1] = row
-
-
 def fine_y_kernel(main, above, below, out, work):
     share = main.shape[0]
     rows = out.shape[1]
@@ -937,14 +949,6 @@
         *shares, *last_level_matrices(size_x, 2 * size_y, 8 * size_z), f1, above, below, up,
         after=(arrived,),
     )
-    f0, beyond = call(
-        fine_sum_kernel,
-        [shape(nx + 1, ny + 8, LANES), shape(nx, ny, LANES)],
-        [],
-        0.3,
-        f0, f_below, f_above, edge,
-    )
-
     fine = (2, nx + 8, ny + 8, LANES)
     correction = call(
         correct_kernel,
@@ -956,9 +960,10 @@
     return call(
         finish_kernel,
         shape(*field.shape),
-        [(nx + 1, ny + 8, LANES)],
-        0.9,
-        kept, correction, f0, beyond,
+        [field.shape, pltpu.SemaphoreType.DMA((4,))],
+        1.2,
+        kept, correction, f0, f_below, f_above, edge,
+        out_specs=pl.BlockSpec(memory_space=pltpu.HBM),
     )
 
 

time: 33.7 us -> 33.6 us (level)
    pallas_call x13 -> x12, Pallas kernels: 12.4 us -> 12.2 us  [call(): pl.pallas_call(kernel, out_shape=outs, scratch_shapes=[pltpu.VMEM(s, F32)...]
  transfers between devices with their start and end apart: 15 -> 15, of which waited for: 4 -> 4; matrix products, arithmetic and copies ran while one was open for 0% -> 0% of each run, Pallas kernels for 24% -> 25%
where the time goes in v8:
time: 33.6 us; the launch traced here: 33.4 us
  starting transfers between devices  15 us (45%)
  Pallas kernels  12.2 us (36%)
  waiting for transfers between devices  4.71 us (14%)
  local copies, waits for them, and re-layouts  1.2 us (4%)
    ppermute x15, starting transfers between devices, from_offset(): return lax.ppermute(value, axis, pairs)  15 us
    pallas_call x12, Pallas kernels, call(): pl.pallas_call(kernel, out_shape=outs, scratch_shapes=[pltpu.VMEM(s, F32)...  12.2 us
    ppermute x15, waiting for transfers between devices, from_offset(): return lax.ppermute(value, axis, pairs)  4.71 us
    unnamed x14, local copies, waits for them, and re-layouts  1.17 us
  transfers between devices with their start and end apart: 15, of which 4 were waited for; matrix products, arithmetic and copies ran while one was open for 0% of the time, Pallas kernels for 25%

profile of v8, /device:TPU:0, one launch (start us, length us, event | category | flops | bytes accessed | tf_op | source)
XLA Modules:
  0.0 33.4 jit_solution(17484363215686875504)
XLA Ops:
  0.0 1.1 %copy-done = f32[3,16,32,128]{3,2,1,0:T(8,128)S(1)} copy-done((f32[3,16,32,128]{3,2,1,0:T(8,128)S(1)}, f32[3,16,32,128]{3,2,1,0:T(8,128)}, u32[]{:S(2)}) %copy-start) | copy-done | bytes 786456
  1.1 2.6 %shard_map.64 = (f32[220,128]{1,0:T(8,128)S(1)}, f32[64,128]{1,0:T(8,128)S(1)}, f32[12,24,128]{2,1,0:T(8,128)S(1)}, f32[2,29,48,128]{3,2,1,0:T(8,128)S(1)}, f32[...) custom-call(f32[3,16,32,128]{3,2,1,0:T(8,128)S(1)} %copy-done), custom_call_target="tpu_custom_call" | custom-call | flops 3335000064 | tf_op jit(solution)/shard_map/pallas_call | solution.py:39
  3.8 3.0 %collective-permute-start = (f32[220,128]{1,0:T(8,128)S(1)}, f32[220,128]{1,0:T(8,128)S(1)}, u32[]{:S(2)}, u32[]{:S(2)}) collective-permute-start(f32[220,128]{1,0:T(8,128)S(1)} %get-tuple-element.29.refs_1_.refs_0_), channel_id=1, source_target_pairs={{0,16},{16,0},{1,17},{17,1},{2,18},{18,2},{3,19},{19,3},{4,20},{20... | collective-permute-start | bytes 337928 | tf_op jit(solution)/shard_map/ppermute | solution.py:835
  6.8 3.6 %collective-permute-start.1 = (f32[64,128]{1,0:T(8,128)S(1)}, f32[64,128]{1,0:T(8,128)S(1)}, u32[]{:S(2)}, u32[]{:S(2)}) collective-permute-start(f32[64,128]{1,0:T(8,128)S(1)} %get-tuple-element.31.refs_0_), channel_id=1, source_target_pairs={{0,3},{1,0},{2,1},{3,2},{4,7},{5,4},{6,5},{7,6},{8,11},{9,8},{10,9... | collective-permute-start | bytes 98312 | tf_op jit(solution)/shard_map/ppermute | solution.py:835
  10.4 1.0 %collective-permute-start.3 = (f32[64,128]{1,0:T(8,128)S(1)}, f32[64,128]{1,0:T(8,128)S(1)}, u32[]{:S(2)}, u32[]{:S(2)}) collective-permute-start(f32[64,128]{1,0:T(8,128)S(1)} %get-tuple-element.31.refs_0_), channel_id=1, source_target_pairs={{0,1},{1,2},{2,3},{3,0},{4,5},{5,6},{6,7},{7,4},{8,9},{9,10},{10,1... | collective-permute-start | bytes 98312 | tf_op jit(solution)/shard_map/ppermute | solution.py:835
  11.4 0.2 shard_map.66
  11.7 0.5 %collective-permute-start.6 = (f32[222,128]{1,0:T(8,128)S(1)}, f32[222,128]{1,0:T(8,128)S(1)}, u32[]{:S(2)}, u32[]{:S(2)}) collective-permute-start(f32[222,128]{1,0:T(8,128)S(1)} %get-tuple-element.36), channel_id=1, source_target_pairs={{0,4},{4,8},{8,12},{12,0},{1,5},{5,9},{9,13},{13,1},{2,6},{6,10},{... | collective-permute-start | bytes 341000 | tf_op jit(solution)/shard_map/ppermute | solution.py:835
  12.2 1.6 %shard_map.65 = (f32[27,48,128]{2,1,0:T(8,128)S(1)}, f32[27,8,128]{2,1,0:T(8,128)S(1)}, f32[27,8,128]{2,1,0:T(8,128)S(1)}, f32[3,16,32,128]{3,2,1,0:T(8,128)S(1)}) custom-call(f32[2,29,48,128]{3,2,1,0:T(8,128)S(1)} %get-tuple-element.25.refs_0_, f32[2,29,48,128]{3,2,1,0:T(8,128)S(1)} %get-tuple-element.26.refs_1_, ...), custom_call_target="tpu_custom_call" | custom-call | flops 3449999872 | tf_op jit(solution)/shard_map/pallas_call | solution.py:39
  13.8 1.5 %collective-permute-done.2.refs_2_ = f32[64,128]{1,0:T(8,128)S(1)} collective-permute-done((f32[64,128]{1,0:T(8,128)S(1)}, f32[64,128]{1,0:T(8,128)S(1)}, u32[]{:S(2)}, u32[]{:S(2)}) %collective-permute-start.2) | collective-permute-done | bytes 32800 | tf_op jit(solution)/shard_map/ppermute | solution.py:835
  15.2 0.9 %collective-permute-done.3.refs_3_ = f32[64,128]{1,0:T(8,128)S(1)} collective-permute-done((f32[64,128]{1,0:T(8,128)S(1)}, f32[64,128]{1,0:T(8,128)S(1)}, u32[]{:S(2)}, u32[]{:S(2)}) %collective-permute-start.3) | collective-permute-done | bytes 32800 | tf_op jit(solution)/shard_map/ppermute | solution.py:835
  16.1 0.1 shard_map.67.refs_0_
  16.3 0.6 %collective-permute-start.4 = (f32[1,10,16,128]{3,2,1,0:T(8,128)S(1)}, f32[1,10,16,128]{3,2,1,0:T(8,128)S(1)}, u32[]{:S(2)}, u32[]{:S(2)}) collective-permute-start(f32[1,10,16,128]{3,2,1,0:T(8,128)S(1)} %shard_map.67.refs_0_), channel_id=1, source_target_pairs={{0,16},{16,0},{1,17},{17,1},{2,18},{18,2},{3,19},{19,3},{4,20},{20... | collective-permute-start | bytes 245768 | tf_op jit(solution)/shard_map/ppermute | solution.py:835
  16.9 0.5 %collective-permute-start.13 = (f32[27,8,128]{2,1,0:T(8,128)S(1)}, f32[27,8,128]{2,1,0:T(8,128)S(1)}, u32[]{:S(2)}, u32[]{:S(2)}) collective-permute-start(f32[27,8,128]{2,1,0:T(8,128)S(1)} %get-tuple-element.43), channel_id=1, source_target_pairs={{0,4},{4,8},{8,12},{12,0},{1,5},{5,9},{9,13},{13,1},{2,6},{6,10},{... | collective-permute-start | bytes 331784 | tf_op jit(solution)/shard_map/ppermute | solution.py:835
  17.4 0.3 shard_map.68
  17.7 2.7 %collective-permute-start.10 = (f32[160,128]{1,0:T(8,128)S(1)}, f32[160,128]{1,0:T(8,128)S(1)}, u32[]{:S(2)}, u32[]{:S(2)}) collective-permute-start(f32[160,128]{1,0:T(8,128)S(1)} %get-tuple-element.38), channel_id=1, source_target_pairs={{0,3},{1,0},{2,1},{3,2},{4,7},{5,4},{6,5},{7,6},{8,11},{9,8},{10,9... | collective-permute-start | bytes 245768 | tf_op jit(solution)/shard_map/ppermute | solution.py:835
  20.3 0.4 %collective-permute-done.4.refs_1_ = f32[1,10,16,128]{3,2,1,0:T(8,128)S(1)} collective-permute-done((f32[1,10,16,128]{3,2,1,0:T(8,128)S(1)}, f32[1,10,16,128]{3,2,1,0:T(8,128)S(1)}, u32[]{:S(2)}, u32[]{:S(2)}) %collective-permute-start.4) | collective-permute-done | bytes 81952 | tf_op jit(solution)/shard_map/ppermute | solution.py:835
  20.9 1.6 %collective-permute-start.8 = (f32[1,8,16,128]{3,2,1,0:T(8,128)S(1)}, f32[1,8,16,128]{3,2,1,0:T(8,128)S(1)}, u32[]{:S(2)}, u32[]{:S(2)}) collective-permute-start(f32[1,8,16,128]{3,2,1,0:T(8,128)S(1)} %shard_map.69.refs_0_.refs_3_), channel_id=1, source_target_pairs={{0,8},{4,12},{8,0},{12,4},{1,9},{5,13},{9,1},{13,5},{2,10},{6,14},... | collective-permute-start | bytes 196616 | tf_op jit(solution)/shard_map/ppermute | solution.py:835
  22.4 0.2 collective-permute-start.9
  22.7 0.7 %shard_map.70.refs_9_ = f32[12,32,128]{2,1,0:T(8,128)S(1)} custom-call(f32[22,32,128]{2,1,0:T(8,128)S(1)} %get-tuple-element.37.refs_2_.g1), custom_call_target="tpu_custom_call" | custom-call | flops 11500000 | tf_op jit(solution)/shard_map/pallas_call | solution.py:39
  23.5 1.3 %collective-permute-start.14 = (f32[13,32,128]{2,1,0:T(8,128)S(1)}, f32[13,32,128]{2,1,0:T(8,128)S(1)}, u32[]{:S(2)}, u32[]{:S(2)}) collective-permute-start(f32[13,32,128]{2,1,0:T(8,128)S(1)} %slice.12), channel_id=1, source_target_pairs={{0,16},{16,0},{1,17},{17,1},{2,18},{18,2},{3,19},{19,3},{4,20},{20... | collective-permute-start | bytes 638984 | tf_op jit(solution)/shard_map/ppermute | solution.py:835
  24.9 1.9 %collective-permute-done.11.below.refs_11_ = f32[160,128]{1,0:T(8,128)S(1)} collective-permute-done((f32[160,128]{1,0:T(8,128)S(1)}, f32[160,128]{1,0:T(8,128)S(1)}, u32[]{:S(2)}, u32[]{:S(2)}) %collective-permute-start.11) | collective-permute-done | bytes 81952 | tf_op jit(solution)/shard_map/ppermute | solution.py:835
  26.8 3.1 %shard_map.72 = (f32[10,16,128]{2,1,0:T(8,128)S(1)}, f32[12,32,128]{2,1,0:T(8,128)S(1)}, f32[6,40,128]{2,1,0:T(8,128)S(1)}) custom-call(f32[1,8,16,128]{3,2,1,0:T(8,128)S(1)} %shard_map.69.refs_0_.refs_3_, f32[1,8,16,128]{3,2,1,0:T(8,128)S(1)} %collective-permute-done.7.refs_1_, f32[1,8,16,128]{3,2,1,0:T(8,128)S(1)} %collective-permute-done.8.refs_2_, ...), custom_call_target="tpu_custom_call" | custom-call | flops 3449999872 | tf_op jit(solution)/shard_map/pallas_call | solution.py:39
  29.9 2.1 %shard_map.73.u0_b = f32[2,24,40,128]{3,2,1,0:T(8,128)S(1)} custom-call(f32[10,16,128]{2,1,0:T(8,128)S(1)} %get-tuple-element.40.e2, f32[12,32,128]{2,1,0:T(8,128)S(1)} %get-tuple-element.41.f1), custom_call_target="tpu_custom_call" | custom-call | flops 2529999872 | tf_op jit(solution)/shard_map/pallas_call | solution.py:39
  32.0 1.4 %shard_map.75 = f32[3,16,32,128]{3,2,1,0:T(8,128)} custom-call(f32[3,16,32,128]{3,2,1,0:T(8,128)S(1)} %get-tuple-element.30.field, f32[2,24,40,128]{3,2,1,0:T(8,128)S(1)} %shard_map.73.u0_b, f32[28,32,128]{2,1,0:T(8,128)S(1)} %shard_map.74.f0, f32[7,32,128]{2,1,0:T(8,128)S(1)} %get-tuple-element.46.below_x, f32[7,32,128]{2,1,0:T(8,128)S(1)} %get-tuple-element.45.above_x, ...), custom_call_target="tpu_custom_call" | custom-call | flops 1380000000 | tf_op jit(solution)/shard_map/pallas_call | solution.py:39
  (34 shorter events, 0.3 us)
Async XLA Ops:
  0.0 1.1 %copy-start = (f32[3,16,32,128]{3,2,1,0:T(8,128)S(1)}, f32[3,16,32,128]{3,2,1,0:T(8,128)}, u32[]{:S(2)}) copy-start(f32[3,16,32,128]{3,2,1,0:T(8,128)} %refs_4_.2) | copy-start | bytes 2359300
  1.1 11.0 %copy-start.1 = (f32[3,16,32,128]{3,2,1,0:T(8,128)S(1)}, f32[3,16,32,128]{3,2,1,0:T(8,128)}, u32[]{:S(2)}) copy-start(f32[3,16,32,128]{3,2,1,0:T(8,128)} %refs_4_.2) | copy-start | bytes 2359300
  3.8 7.7 %collective-permute-start = (f32[220,128]{1,0:T(8,128)S(1)}, f32[220,128]{1,0:T(8,128)S(1)}, u32[]{:S(2)}, u32[]{:S(2)}) collective-permute-start(f32[220,128]{1,0:T(8,128)S(1)} %get-tuple-element.29.refs_1_.refs_0_), channel_id=1, source_target_pairs={{0,16},{16,0},{1,17},{17,1},{2,18},{18,2},{3,19},{19,3},{4,20},{20... | collective-permute-start | bytes 337928 | tf_op jit(solution)/shard_map/ppermute | solution.py:835
  6.8 7.0 %collective-permute-start.1 = (f32[64,128]{1,0:T(8,128)S(1)}, f32[64,128]{1,0:T(8,128)S(1)}, u32[]{:S(2)}, u32[]{:S(2)}) collective-permute-start(f32[64,128]{1,0:T(8,128)S(1)} %get-tuple-element.31.refs_0_), channel_id=1, source_target_pairs={{0,3},{1,0},{2,1},{3,2},{4,7},{5,4},{6,5},{7,6},{8,11},{9,8},{10,9... | collective-permute-start | bytes 98312 | tf_op jit(solution)/shard_map/ppermute | solution.py:835
  10.4 4.8 %collective-permute-start.2 = (f32[64,128]{1,0:T(8,128)S(1)}, f32[64,128]{1,0:T(8,128)S(1)}, u32[]{:S(2)}, u32[]{:S(2)}) collective-permute-start(f32[64,128]{1,0:T(8,128)S(1)} %get-tuple-element.31.refs_0_), channel_id=1, source_target_pairs={{0,2},{1,3},{2,0},{3,1},{4,6},{5,7},{6,4},{7,5},{8,10},{9,11},{10,... | collective-permute-start | bytes 98312 | tf_op jit(solution)/shard_map/ppermute | solution.py:835
  10.4 5.7 %collective-permute-start.3 = (f32[64,128]{1,0:T(8,128)S(1)}, f32[64,128]{1,0:T(8,128)S(1)}, u32[]{:S(2)}, u32[]{:S(2)}) collective-permute-start(f32[64,128]{1,0:T(8,128)S(1)} %get-tuple-element.31.refs_0_), channel_id=1, source_target_pairs={{0,1},{1,2},{2,3},{3,0},{4,5},{5,6},{6,7},{7,4},{8,9},{9,10},{10,1... | collective-permute-start | bytes 98312 | tf_op jit(solution)/shard_map/ppermute | solution.py:835
  11.6 5.8 %collective-permute-start.5 = (f32[222,128]{1,0:T(8,128)S(1)}, f32[222,128]{1,0:T(8,128)S(1)}, u32[]{:S(2)}, u32[]{:S(2)}) collective-permute-start(f32[222,128]{1,0:T(8,128)S(1)} %get-tuple-element.35), channel_id=1, source_target_pairs={{0,12},{4,0},{8,4},{12,8},{1,13},{5,1},{9,5},{13,9},{2,14},{6,2},{... | collective-permute-start | bytes 341000 | tf_op jit(solution)/shard_map/ppermute | solution.py:835
  11.7 5.7 %collective-permute-start.6 = (f32[222,128]{1,0:T(8,128)S(1)}, f32[222,128]{1,0:T(8,128)S(1)}, u32[]{:S(2)}, u32[]{:S(2)}) collective-permute-start(f32[222,128]{1,0:T(8,128)S(1)} %get-tuple-element.36), channel_id=1, source_target_pairs={{0,4},{4,8},{8,12},{12,0},{1,5},{5,9},{9,13},{13,1},{2,6},{6,10},{... | collective-permute-start | bytes 341000 | tf_op jit(solution)/shard_map/ppermute | solution.py:835
  16.3 4.5 %collective-permute-start.4 = (f32[1,10,16,128]{3,2,1,0:T(8,128)S(1)}, f32[1,10,16,128]{3,2,1,0:T(8,128)S(1)}, u32[]{:S(2)}, u32[]{:S(2)}) collective-permute-start(f32[1,10,16,128]{3,2,1,0:T(8,128)S(1)} %shard_map.67.refs_0_), channel_id=1, source_target_pairs={{0,16},{16,0},{1,17},{17,1},{2,18},{18,2},{3,19},{19,3},{4,20},{20... | collective-permute-start | bytes 245768 | tf_op jit(solution)/shard_map/ppermute | solution.py:835
  16.8 4.0 %collective-permute-start.12 = (f32[27,8,128]{2,1,0:T(8,128)S(1)}, f32[27,8,128]{2,1,0:T(8,128)S(1)}, u32[]{:S(2)}, u32[]{:S(2)}) collective-permute-start(f32[27,8,128]{2,1,0:T(8,128)S(1)} %get-tuple-element.42), channel_id=1, source_target_pairs={{0,12},{4,0},{8,4},{12,8},{1,13},{5,1},{9,5},{13,9},{2,14},{6,2},{... | collective-permute-start | bytes 331784 | tf_op jit(solution)/shard_map/ppermute | solution.py:835
  16.9 5.6 %collective-permute-start.13 = (f32[27,8,128]{2,1,0:T(8,128)S(1)}, f32[27,8,128]{2,1,0:T(8,128)S(1)}, u32[]{:S(2)}, u32[]{:S(2)}) collective-permute-start(f32[27,8,128]{2,1,0:T(8,128)S(1)} %get-tuple-element.43), channel_id=1, source_target_pairs={{0,4},{4,8},{8,12},{12,0},{1,5},{5,9},{9,13},{13,1},{2,6},{6,10},{... | collective-permute-start | bytes 331784 | tf_op jit(solution)/shard_map/ppermute | solution.py:835
  17.7 5.8 %collective-permute-start.10 = (f32[160,128]{1,0:T(8,128)S(1)}, f32[160,128]{1,0:T(8,128)S(1)}, u32[]{:S(2)}, u32[]{:S(2)}) collective-permute-start(f32[160,128]{1,0:T(8,128)S(1)} %get-tuple-element.38), channel_id=1, source_target_pairs={{0,3},{1,0},{2,1},{3,2},{4,7},{5,4},{6,5},{7,6},{8,11},{9,8},{10,9... | collective-permute-start | bytes 245768 | tf_op jit(solution)/shard_map/ppermute | solution.py:835
  20.3 6.4 %collective-permute-start.11 = (f32[160,128]{1,0:T(8,128)S(1)}, f32[160,128]{1,0:T(8,128)S(1)}, u32[]{:S(2)}, u32[]{:S(2)}) collective-permute-start(f32[160,128]{1,0:T(8,128)S(1)} %get-tuple-element.39.refs_12_), channel_id=1, source_target_pairs={{0,1},{1,2},{2,3},{3,0},{4,5},{5,6},{6,7},{7,4},{8,9},{9,10},{10,1... | collective-permute-start | bytes 245768 | tf_op jit(solution)/shard_map/ppermute | solution.py:835
  20.8 6.0 %collective-permute-start.7 = (f32[1,8,16,128]{3,2,1,0:T(8,128)S(1)}, f32[1,8,16,128]{3,2,1,0:T(8,128)S(1)}, u32[]{:S(2)}, u32[]{:S(2)}) collective-permute-start(f32[1,8,16,128]{3,2,1,0:T(8,128)S(1)} %shard_map.69.refs_0_.refs_3_), channel_id=1, source_target_pairs={{0,12},{4,0},{8,4},{12,8},{1,13},{5,1},{9,5},{13,9},{2,14},{6,2},{... | collective-permute-start | bytes 196616 | tf_op jit(solution)/shard_map/ppermute | solution.py:835
  20.9 5.9 %collective-permute-start.8 = (f32[1,8,16,128]{3,2,1,0:T(8,128)S(1)}, f32[1,8,16,128]{3,2,1,0:T(8,128)S(1)}, u32[]{:S(2)}, u32[]{:S(2)}) collective-permute-start(f32[1,8,16,128]{3,2,1,0:T(8,128)S(1)} %shard_map.69.refs_0_.refs_3_), channel_id=1, source_target_pairs={{0,8},{4,12},{8,0},{12,4},{1,9},{5,13},{9,1},{13,5},{2,10},{6,14},... | collective-permute-start | bytes 196616 | tf_op jit(solution)/shard_map/ppermute | solution.py:835
  22.4 4.3 %collective-permute-start.9 = (f32[1,8,16,128]{3,2,1,0:T(8,128)S(1)}, f32[1,8,16,128]{3,2,1,0:T(8,128)S(1)}, u32[]{:S(2)}, u32[]{:S(2)}) collective-permute-start(f32[1,8,16,128]{3,2,1,0:T(8,128)S(1)} %shard_map.69.refs_0_.refs_3_), channel_id=1, source_target_pairs={{0,4},{4,8},{8,12},{12,0},{1,5},{5,9},{9,13},{13,1},{2,6},{6,10},{... | collective-permute-start | bytes 196616 | tf_op jit(solution)/shard_map/ppermute | solution.py:835
  23.5 3.3 %copy-start.2 = (f32[1,128,128]{2,1,0:T(8,128)S(1)}, f32[1,128,128]{2,1,0:T(8,128)}, u32[]{:S(2)}) copy-start(f32[1,128,128]{2,1,0:T(8,128)} %constant.12.clone.refs_6_) | copy-start | bytes 196612
  23.5 3.3 %copy-start.3 = (f32[1,128,128]{2,1,0:T(8,128)S(1)}, f32[1,128,128]{2,1,0:T(8,128)}, u32[]{:S(2)}) copy-start(f32[1,128,128]{2,1,0:T(8,128)} %constant.13.clone.refs_7_) | copy-start | bytes 196612
  23.5 3.3 %copy-start.4 = (f32[64,16]{1,0:T(8,128)S(1)}, f32[64,16]{1,0:T(8,128)}, u32[]{:S(2)}) copy-start(f32[64,16]{1,0:T(8,128)} %constant.11.clone.refs_5_) | copy-start | bytes 12292
  23.5 3.3 %copy-start.5 = (f32[16,64]{1,0:T(8,128)S(1)}, f32[16,64]{1,0:T(8,128)}, u32[]{:S(2)}) copy-start(f32[16,64]{1,0:T(8,128)} %constant.10.clone.refs_4_) | copy-start | bytes 12292
  23.5 3.3 %copy-start.6 = (f32[16,128]{1,0:T(8,128)S(1)}, f32[16,128]{1,0:T(8,128)}, u32[]{:S(2)}) copy-start(f32[16,128]{1,0:T(8,128)} %constant.14.clone.refs_8_) | copy-start | bytes 24580
  23.5 8.5 %collective-permute-start.14 = (f32[13,32,128]{2,1,0:T(8,128)S(1)}, f32[13,32,128]{2,1,0:T(8,128)S(1)}, u32[]{:S(2)}, u32[]{:S(2)}) collective-permute-start(f32[13,32,128]{2,1,0:T(8,128)S(1)} %slice.12), channel_id=1, source_target_pairs={{0,16},{16,0},{1,17},{17,1},{2,18},{18,2},{3,19},{19,3},{4,20},{20... | collective-permute-start | bytes 638984 | tf_op jit(solution)/shard_map/ppermute | solution.py:835

commit v9 on v8

--- a/solution.py
+++ b/solution.py
@@ -960,7 +960,7 @@
     return call(
         finish_kernel,
         shape(*field.shape),
-        [field.shape, pltpu.SemaphoreType.DMA((4,))],
+        [field.shape, pltpu.SemaphoreType.DMA((8,))],
         1.2,
         kept, correction, f0, f_below, f_above, edge,
         out_specs=pl.BlockSpec(memory_space=pltpu.HBM),

time: 33.6 us -> 33.6 us (level)
  no operation moved by 1% of the time
where the time goes in v9:
time: 33.6 us; the launch traced here: 33.4 us
  starting transfers between devices  15 us (45%)
  Pallas kernels  12.2 us (36%)
  waiting for transfers between devices  4.71 us (14%)
  local copies, waits for them, and re-layouts  1.2 us (4%)
    ppermute x15, starting transfers between devices, from_offset(): return lax.ppermute(value, axis, pairs)  15 us
    pallas_call x12, Pallas kernels, call(): pl.pallas_call(kernel, out_shape=outs, scratch_shapes=[pltpu.VMEM(s, F32)...  12.2 us
    ppermute x15, waiting for transfers between devices, from_offset(): return lax.ppermute(value, axis, pairs)  4.71 us
    unnamed x14, local copies, waits for them, and re-layouts  1.17 us
  transfers between devices with their start and end apart: 15, of which 4 were waited for; matrix products, arithmetic and copies ran while one was open for 0% of the time, Pallas kernels for 25%

profile of v9, /device:TPU:0, one launch (start us, length us, event | category | flops | bytes accessed | tf_op | source)
XLA Modules:
  0.0 33.4 jit_solution(18211966482986832157)
XLA Ops:
  0.0 1.1 %copy-done = f32[3,16,32,128]{3,2,1,0:T(8,128)S(1)} copy-done((f32[3,16,32,128]{3,2,1,0:T(8,128)S(1)}, f32[3,16,32,128]{3,2,1,0:T(8,128)}, u32[]{:S(2)}) %copy-start) | copy-done | bytes 786456
  1.1 2.6 %shard_map.64 = (f32[220,128]{1,0:T(8,128)S(1)}, f32[64,128]{1,0:T(8,128)S(1)}, f32[12,24,128]{2,1,0:T(8,128)S(1)}, f32[2,29,48,128]{3,2,1,0:T(8,128)S(1)}, f32[...) custom-call(f32[3,16,32,128]{3,2,1,0:T(8,128)S(1)} %copy-done), custom_call_target="tpu_custom_call" | custom-call | flops 3335000064 | tf_op jit(solution)/shard_map/pallas_call | solution.py:39
  3.8 3.0 %collective-permute-start = (f32[220,128]{1,0:T(8,128)S(1)}, f32[220,128]{1,0:T(8,128)S(1)}, u32[]{:S(2)}, u32[]{:S(2)}) collective-permute-start(f32[220,128]{1,0:T(8,128)S(1)} %get-tuple-element.29.refs_1_.refs_0_), channel_id=1, source_target_pairs={{0,16},{16,0},{1,17},{17,1},{2,18},{18,2},{3,19},{19,3},{4,20},{20... | collective-permute-start | bytes 337928 | tf_op jit(solution)/shard_map/ppermute | solution.py:835
  6.8 3.6 %collective-permute-start.1 = (f32[64,128]{1,0:T(8,128)S(1)}, f32[64,128]{1,0:T(8,128)S(1)}, u32[]{:S(2)}, u32[]{:S(2)}) collective-permute-start(f32[64,128]{1,0:T(8,128)S(1)} %get-tuple-element.31.refs_0_), channel_id=1, source_target_pairs={{0,3},{1,0},{2,1},{3,2},{4,7},{5,4},{6,5},{7,6},{8,11},{9,8},{10,9... | collective-permute-start | bytes 98312 | tf_op jit(solution)/shard_map/ppermute | solution.py:835
  10.4 1.0 %collective-permute-start.3 = (f32[64,128]{1,0:T(8,128)S(1)}, f32[64,128]{1,0:T(8,128)S(1)}, u32[]{:S(2)}, u32[]{:S(2)}) collective-permute-start(f32[64,128]{1,0:T(8,128)S(1)} %get-tuple-element.31.refs_0_), channel_id=1, source_target_pairs={{0,1},{1,2},{2,3},{3,0},{4,5},{5,6},{6,7},{7,4},{8,9},{9,10},{10,1... | collective-permute-start | bytes 98312 | tf_op jit(solution)/shard_map/ppermute | solution.py:835
  11.4 0.2 shard_map.66
  11.7 0.5 %collective-permute-start.6 = (f32[222,128]{1,0:T(8,128)S(1)}, f32[222,128]{1,0:T(8,128)S(1)}, u32[]{:S(2)}, u32[]{:S(2)}) collective-permute-start(f32[222,128]{1,0:T(8,128)S(1)} %get-tuple-element.36), channel_id=1, source_target_pairs={{0,4},{4,8},{8,12},{12,0},{1,5},{5,9},{9,13},{13,1},{2,6},{6,10},{... | collective-permute-start | bytes 341000 | tf_op jit(solution)/shard_map/ppermute | solution.py:835
  12.2 1.6 %shard_map.65 = (f32[27,48,128]{2,1,0:T(8,128)S(1)}, f32[27,8,128]{2,1,0:T(8,128)S(1)}, f32[27,8,128]{2,1,0:T(8,128)S(1)}, f32[3,16,32,128]{3,2,1,0:T(8,128)S(1)}) custom-call(f32[2,29,48,128]{3,2,1,0:T(8,128)S(1)} %get-tuple-element.25.refs_0_, f32[2,29,48,128]{3,2,1,0:T(8,128)S(1)} %get-tuple-element.26.refs_1_, ...), custom_call_target="tpu_custom_call" | custom-call | flops 3449999872 | tf_op jit(solution)/shard_map/pallas_call | solution.py:39
  13.8 1.5 %collective-permute-done.2.refs_2_ = f32[64,128]{1,0:T(8,128)S(1)} collective-permute-done((f32[64,128]{1,0:T(8,128)S(1)}, f32[64,128]{1,0:T(8,128)S(1)}, u32[]{:S(2)}, u32[]{:S(2)}) %collective-permute-start.2) | collective-permute-done | bytes 32800 | tf_op jit(solution)/shard_map/ppermute | solution.py:835
  15.2 0.9 %collective-permute-done.3.refs_3_ = f32[64,128]{1,0:T(8,128)S(1)} collective-permute-done((f32[64,128]{1,0:T(8,128)S(1)}, f32[64,128]{1,0:T(8,128)S(1)}, u32[]{:S(2)}, u32[]{:S(2)}) %collective-permute-start.3) | collective-permute-done | bytes 32800 | tf_op jit(solution)/shard_map/ppermute | solution.py:835
  16.1 0.1 shard_map.67.refs_0_
  16.3 0.6 %collective-permute-start.4 = (f32[1,10,16,128]{3,2,1,0:T(8,128)S(1)}, f32[1,10,16,128]{3,2,1,0:T(8,128)S(1)}, u32[]{:S(2)}, u32[]{:S(2)}) collective-permute-start(f32[1,10,16,128]{3,2,1,0:T(8,128)S(1)} %shard_map.67.refs_0_), channel_id=1, source_target_pairs={{0,16},{16,0},{1,17},{17,1},{2,18},{18,2},{3,19},{19,3},{4,20},{20... | collective-permute-start | bytes 245768 | tf_op jit(solution)/shard_map/ppermute | solution.py:835
  16.9 0.5 %collective-permute-start.13 = (f32[27,8,128]{2,1,0:T(8,128)S(1)}, f32[27,8,128]{2,1,0:T(8,128)S(1)}, u32[]{:S(2)}, u32[]{:S(2)}) collective-permute-start(f32[27,8,128]{2,1,0:T(8,128)S(1)} %get-tuple-element.43), channel_id=1, source_target_pairs={{0,4},{4,8},{8,12},{12,0},{1,5},{5,9},{9,13},{13,1},{2,6},{6,10},{... | collective-permute-start | bytes 331784 | tf_op jit(solution)/shard_map/ppermute | solution.py:835
  17.4 0.3 shard_map.68
  17.7 2.7 %collective-permute-start.10 = (f32[160,128]{1,0:T(8,128)S(1)}, f32[160,128]{1,0:T(8,128)S(1)}, u32[]{:S(2)}, u32[]{:S(2)}) collective-permute-start(f32[160,128]{1,0:T(8,128)S(1)} %get-tuple-element.38), channel_id=1, source_target_pairs={{0,3},{1,0},{2,1},{3,2},{4,7},{5,4},{6,5},{7,6},{8,11},{9,8},{10,9... | collective-permute-start | bytes 245768 | tf_op jit(solution)/shard_map/ppermute | solution.py:835
  20.3 0.4 %collective-permute-done.4.refs_1_ = f32[1,10,16,128]{3,2,1,0:T(8,128)S(1)} collective-permute-done((f32[1,10,16,128]{3,2,1,0:T(8,128)S(1)}, f32[1,10,16,128]{3,2,1,0:T(8,128)S(1)}, u32[]{:S(2)}, u32[]{:S(2)}) %collective-permute-start.4) | collective-permute-done | bytes 81952 | tf_op jit(solution)/shard_map/ppermute | solution.py:835
  20.9 1.6 %collective-permute-start.8 = (f32[1,8,16,128]{3,2,1,0:T(8,128)S(1)}, f32[1,8,16,128]{3,2,1,0:T(8,128)S(1)}, u32[]{:S(2)}, u32[]{:S(2)}) collective-permute-start(f32[1,8,16,128]{3,2,1,0:T(8,128)S(1)} %shard_map.69.refs_0_.refs_3_), channel_id=1, source_target_pairs={{0,8},{4,12},{8,0},{12,4},{1,9},{5,13},{9,1},{13,5},{2,10},{6,14},... | collective-permute-start | bytes 196616 | tf_op jit(solution)/shard_map/ppermute | solution.py:835
  22.4 0.2 collective-permute-start.9
  22.7 0.7 %shard_map.70.refs_9_ = f32[12,32,128]{2,1,0:T(8,128)S(1)} custom-call(f32[22,32,128]{2,1,0:T(8,128)S(1)} %get-tuple-element.37.refs_2_.g1), custom_call_target="tpu_custom_call" | custom-call | flops 11500000 | tf_op jit(solution)/shard_map/pallas_call | solution.py:39
  23.5 1.3 %collective-permute-start.14 = (f32[13,32,128]{2,1,0:T(8,128)S(1)}, f32[13,32,128]{2,1,0:T(8,128)S(1)}, u32[]{:S(2)}, u32[]{:S(2)}) collective-permute-start(f32[13,32,128]{2,1,0:T(8,128)S(1)} %slice.12), channel_id=1, source_target_pairs={{0,16},{16,0},{1,17},{17,1},{2,18},{18,2},{3,19},{19,3},{4,20},{20... | collective-permute-start | bytes 638984 | tf_op jit(solution)/shard_map/ppermute | solution.py:835
  24.9 1.9 %collective-permute-done.11.below.refs_11_ = f32[160,128]{1,0:T(8,128)S(1)} collective-permute-done((f32[160,128]{1,0:T(8,128)S(1)}, f32[160,128]{1,0:T(8,128)S(1)}, u32[]{:S(2)}, u32[]{:S(2)}) %collective-permute-start.11) | collective-permute-done | bytes 81952 | tf_op jit(solution)/shard_map/ppermute | solution.py:835
  26.8 3.1 %shard_map.72 = (f32[10,16,128]{2,1,0:T(8,128)S(1)}, f32[12,32,128]{2,1,0:T(8,128)S(1)}, f32[6,40,128]{2,1,0:T(8,128)S(1)}) custom-call(f32[1,8,16,128]{3,2,1,0:T(8,128)S(1)} %shard_map.69.refs_0_.refs_3_, f32[1,8,16,128]{3,2,1,0:T(8,128)S(1)} %collective-permute-done.7.refs_1_, f32[1,8,16,128]{3,2,1,0:T(8,128)S(1)} %collective-permute-done.8.refs_2_, ...), custom_call_target="tpu_custom_call" | custom-call | flops 3449999872 | tf_op jit(solution)/shard_map/pallas_call | solution.py:39
  29.9 2.1 %shard_map.73.u0_b = f32[2,24,40,128]{3,2,1,0:T(8,128)S(1)} custom-call(f32[10,16,128]{2,1,0:T(8,128)S(1)} %get-tuple-element.40.e2, f32[12,32,128]{2,1,0:T(8,128)S(1)} %get-tuple-element.41.f1), custom_call_target="tpu_custom_call" | custom-call | flops 2529999872 | tf_op jit(solution)/shard_map/pallas_call | solution.py:39
  32.0 1.4 %shard_map.75 = f32[3,16,32,128]{3,2,1,0:T(8,128)} custom-call(f32[3,16,32,128]{3,2,1,0:T(8,128)S(1)} %get-tuple-element.30.field, f32[2,24,40,128]{3,2,1,0:T(8,128)S(1)} %shard_map.73.u0_b, f32[28,32,128]{2,1,0:T(8,128)S(1)} %shard_map.74.f0, f32[7,32,128]{2,1,0:T(8,128)S(1)} %get-tuple-element.46.below_x, f32[7,32,128]{2,1,0:T(8,128)S(1)} %get-tuple-element.45.above_x, ...), custom_call_target="tpu_custom_call" | custom-call | flops 1380000000 | tf_op jit(solution)/shard_map/pallas_call | solution.py:39
  (34 shorter events, 0.3 us)
Async XLA Ops:
  0.0 1.1 %copy-start = (f32[3,16,32,128]{3,2,1,0:T(8,128)S(1)}, f32[3,16,32,128]{3,2,1,0:T(8,128)}, u32[]{:S(2)}) copy-start(f32[3,16,32,128]{3,2,1,0:T(8,128)} %refs_4_.2) | copy-start | bytes 2359300
  1.1 11.0 %copy-start.1 = (f32[3,16,32,128]{3,2,1,0:T(8,128)S(1)}, f32[3,16,32,128]{3,2,1,0:T(8,128)}, u32[]{:S(2)}) copy-start(f32[3,16,32,128]{3,2,1,0:T(8,128)} %refs_4_.2) | copy-start | bytes 2359300
  3.8 7.7 %collective-permute-start = (f32[220,128]{1,0:T(8,128)S(1)}, f32[220,128]{1,0:T(8,128)S(1)}, u32[]{:S(2)}, u32[]{:S(2)}) collective-permute-start(f32[220,128]{1,0:T(8,128)S(1)} %get-tuple-element.29.refs_1_.refs_0_), channel_id=1, source_target_pairs={{0,16},{16,0},{1,17},{17,1},{2,18},{18,2},{3,19},{19,3},{4,20},{20... | collective-permute-start | bytes 337928 | tf_op jit(solution)/shard_map/ppermute | solution.py:835
  6.8 7.0 %collective-permute-start.1 = (f32[64,128]{1,0:T(8,128)S(1)}, f32[64,128]{1,0:T(8,128)S(1)}, u32[]{:S(2)}, u32[]{:S(2)}) collective-permute-start(f32[64,128]{1,0:T(8,128)S(1)} %get-tuple-element.31.refs_0_), channel_id=1, source_target_pairs={{0,3},{1,0},{2,1},{3,2},{4,7},{5,4},{6,5},{7,6},{8,11},{9,8},{10,9... | collective-permute-start | bytes 98312 | tf_op jit(solution)/shard_map/ppermute | solution.py:835
  10.4 4.8 %collective-permute-start.2 = (f32[64,128]{1,0:T(8,128)S(1)}, f32[64,128]{1,0:T(8,128)S(1)}, u32[]{:S(2)}, u32[]{:S(2)}) collective-permute-start(f32[64,128]{1,0:T(8,128)S(1)} %get-tuple-element.31.refs_0_), channel_id=1, source_target_pairs={{0,2},{1,3},{2,0},{3,1},{4,6},{5,7},{6,4},{7,5},{8,10},{9,11},{10,... | collective-permute-start | bytes 98312 | tf_op jit(solution)/shard_map/ppermute | solution.py:835
  10.4 5.7 %collective-permute-start.3 = (f32[64,128]{1,0:T(8,128)S(1)}, f32[64,128]{1,0:T(8,128)S(1)}, u32[]{:S(2)}, u32[]{:S(2)}) collective-permute-start(f32[64,128]{1,0:T(8,128)S(1)} %get-tuple-element.31.refs_0_), channel_id=1, source_target_pairs={{0,1},{1,2},{2,3},{3,0},{4,5},{5,6},{6,7},{7,4},{8,9},{9,10},{10,1... | collective-permute-start | bytes 98312 | tf_op jit(solution)/shard_map/ppermute | solution.py:835
  11.6 5.8 %collective-permute-start.5 = (f32[222,128]{1,0:T(8,128)S(1)}, f32[222,128]{1,0:T(8,128)S(1)}, u32[]{:S(2)}, u32[]{:S(2)}) collective-permute-start(f32[222,128]{1,0:T(8,128)S(1)} %get-tuple-element.35), channel_id=1, source_target_pairs={{0,12},{4,0},{8,4},{12,8},{1,13},{5,1},{9,5},{13,9},{2,14},{6,2},{... | collective-permute-start | bytes 341000 | tf_op jit(solution)/shard_map/ppermute | solution.py:835
  11.7 5.7 %collective-permute-start.6 = (f32[222,128]{1,0:T(8,128)S(1)}, f32[222,128]{1,0:T(8,128)S(1)}, u32[]{:S(2)}, u32[]{:S(2)}) collective-permute-start(f32[222,128]{1,0:T(8,128)S(1)} %get-tuple-element.36), channel_id=1, source_target_pairs={{0,4},{4,8},{8,12},{12,0},{1,5},{5,9},{9,13},{13,1},{2,6},{6,10},{... | collective-permute-start | bytes 341000 | tf_op jit(solution)/shard_map/ppermute | solution.py:835
  16.3 4.5 %collective-permute-start.4 = (f32[1,10,16,128]{3,2,1,0:T(8,128)S(1)}, f32[1,10,16,128]{3,2,1,0:T(8,128)S(1)}, u32[]{:S(2)}, u32[]{:S(2)}) collective-permute-start(f32[1,10,16,128]{3,2,1,0:T(8,128)S(1)} %shard_map.67.refs_0_), channel_id=1, source_target_pairs={{0,16},{16,0},{1,17},{17,1},{2,18},{18,2},{3,19},{19,3},{4,20},{20... | collective-permute-start | bytes 245768 | tf_op jit(solution)/shard_map/ppermute | solution.py:835
  16.8 4.0 %collective-permute-start.12 = (f32[27,8,128]{2,1,0:T(8,128)S(1)}, f32[27,8,128]{2,1,0:T(8,128)S(1)}, u32[]{:S(2)}, u32[]{:S(2)}) collective-permute-start(f32[27,8,128]{2,1,0:T(8,128)S(1)} %get-tuple-element.42), channel_id=1, source_target_pairs={{0,12},{4,0},{8,4},{12,8},{1,13},{5,1},{9,5},{13,9},{2,14},{6,2},{... | collective-permute-start | bytes 331784 | tf_op jit(solution)/shard_map/ppermute | solution.py:835
  16.9 5.6 %collective-permute-start.13 = (f32[27,8,128]{2,1,0:T(8,128)S(1)}, f32[27,8,128]{2,1,0:T(8,128)S(1)}, u32[]{:S(2)}, u32[]{:S(2)}) collective-permute-start(f32[27,8,128]{2,1,0:T(8,128)S(1)} %get-tuple-element.43), channel_id=1, source_target_pairs={{0,4},{4,8},{8,12},{12,0},{1,5},{5,9},{9,13},{13,1},{2,6},{6,10},{... | collective-permute-start | bytes 331784 | tf_op jit(solution)/shard_map/ppermute | solution.py:835
  17.7 5.8 %collective-permute-start.10 = (f32[160,128]{1,0:T(8,128)S(1)}, f32[160,128]{1,0:T(8,128)S(1)}, u32[]{:S(2)}, u32[]{:S(2)}) collective-permute-start(f32[160,128]{1,0:T(8,128)S(1)} %get-tuple-element.38), channel_id=1, source_target_pairs={{0,3},{1,0},{2,1},{3,2},{4,7},{5,4},{6,5},{7,6},{8,11},{9,8},{10,9... | collective-permute-start | bytes 245768 | tf_op jit(solution)/shard_map/ppermute | solution.py:835
  20.3 6.4 %collective-permute-start.11 = (f32[160,128]{1,0:T(8,128)S(1)}, f32[160,128]{1,0:T(8,128)S(1)}, u32[]{:S(2)}, u32[]{:S(2)}) collective-permute-start(f32[160,128]{1,0:T(8,128)S(1)} %get-tuple-element.39.refs_12_), channel_id=1, source_target_pairs={{0,1},{1,2},{2,3},{3,0},{4,5},{5,6},{6,7},{7,4},{8,9},{9,10},{10,1... | collective-permute-start | bytes 245768 | tf_op jit(solution)/shard_map/ppermute | solution.py:835
  20.8 6.0 %collective-permute-start.7 = (f32[1,8,16,128]{3,2,1,0:T(8,128)S(1)}, f32[1,8,16,128]{3,2,1,0:T(8,128)S(1)}, u32[]{:S(2)}, u32[]{:S(2)}) collective-permute-start(f32[1,8,16,128]{3,2,1,0:T(8,128)S(1)} %shard_map.69.refs_0_.refs_3_), channel_id=1, source_target_pairs={{0,12},{4,0},{8,4},{12,8},{1,13},{5,1},{9,5},{13,9},{2,14},{6,2},{... | collective-permute-start | bytes 196616 | tf_op jit(solution)/shard_map/ppermute | solution.py:835
  20.9 5.9 %collective-permute-start.8 = (f32[1,8,16,128]{3,2,1,0:T(8,128)S(1)}, f32[1,8,16,128]{3,2,1,0:T(8,128)S(1)}, u32[]{:S(2)}, u32[]{:S(2)}) collective-permute-start(f32[1,8,16,128]{3,2,1,0:T(8,128)S(1)} %shard_map.69.refs_0_.refs_3_), channel_id=1, source_target_pairs={{0,8},{4,12},{8,0},{12,4},{1,9},{5,13},{9,1},{13,5},{2,10},{6,14},... | collective-permute-start | bytes 196616 | tf_op jit(solution)/shard_map/ppermute | solution.py:835
  22.4 4.3 %collective-permute-start.9 = (f32[1,8,16,128]{3,2,1,0:T(8,128)S(1)}, f32[1,8,16,128]{3,2,1,0:T(8,128)S(1)}, u32[]{:S(2)}, u32[]{:S(2)}) collective-permute-start(f32[1,8,16,128]{3,2,1,0:T(8,128)S(1)} %shard_map.69.refs_0_.refs_3_), channel_id=1, source_target_pairs={{0,4},{4,8},{8,12},{12,0},{1,5},{5,9},{9,13},{13,1},{2,6},{6,10},{... | collective-permute-start | bytes 196616 | tf_op jit(solution)/shard_map/ppermute | solution.py:835
  23.5 3.3 %copy-start.2 = (f32[1,128,128]{2,1,0:T(8,128)S(1)}, f32[1,128,128]{2,1,0:T(8,128)}, u32[]{:S(2)}) copy-start(f32[1,128,128]{2,1,0:T(8,128)} %constant.12.clone.refs_6_) | copy-start | bytes 196612
  23.5 3.3 %copy-start.3 = (f32[1,128,128]{2,1,0:T(8,128)S(1)}, f32[1,128,128]{2,1,0:T(8,128)}, u32[]{:S(2)}) copy-start(f32[1,128,128]{2,1,0:T(8,128)} %constant.13.clone.refs_7_) | copy-start | bytes 196612
  23.5 3.3 %copy-start.4 = (f32[64,16]{1,0:T(8,128)S(1)}, f32[64,16]{1,0:T(8,128)}, u32[]{:S(2)}) copy-start(f32[64,16]{1,0:T(8,128)} %constant.11.clone.refs_5_) | copy-start | bytes 12292
  23.5 3.3 %copy-start.5 = (f32[16,64]{1,0:T(8,128)S(1)}, f32[16,64]{1,0:T(8,128)}, u32[]{:S(2)}) copy-start(f32[16,64]{1,0:T(8,128)} %constant.10.clone.refs_4_) | copy-start | bytes 12292
  23.5 3.3 %copy-start.6 = (f32[16,128]{1,0:T(8,128)S(1)}, f32[16,128]{1,0:T(8,128)}, u32[]{:S(2)}) copy-start(f32[16,128]{1,0:T(8,128)} %constant.14.clone.refs_8_) | copy-start | bytes 24580
  23.5 8.5 %collective-permute-start.14 = (f32[13,32,128]{2,1,0:T(8,128)S(1)}, f32[13,32,128]{2,1,0:T(8,128)S(1)}, u32[]{:S(2)}, u32[]{:S(2)}) collective-permute-start(f32[13,32,128]{2,1,0:T(8,128)S(1)} %slice.12), channel_id=1, source_target_pairs={{0,16},{16,0},{1,17},{17,1},{2,18},{18,2},{3,19},{19,3},{4,20},{20... | collective-permute-start | bytes 638984 | tf_op jit(solution)/shard_map/ppermute | solution.py:835
